TPU v7x, 256 devices: a whole 4x4x8 slice. The times are simulated.
256 devices in a mesh: blk: 128 (over z, x, y), cols: 2 (over core).
Axes of the slice: x: 4, y: 4, z: 8, core: 2. Of those that a mesh axis runs over, the one named last changes fastest.
Arguments:
- rhs: bfloat16 [2048, 128, 512], P('blk', None, 'cols'), parts along dimension 2, may hold values from -6 to 6
- diag_inverse: bfloat16 [2048, 128, 128], P('blk')
- lower_blocks: bfloat16 [2048, 2, 128, 128], P('blk'), may hold values from -0.25 to 0.25
- local_cols: int32 [2048, 2], P('blk'), may hold values from 0 to 14, as said below
- sep_rhs: bfloat16 [128, 384, 512], P('blk', None, 'cols'), parts along dimension 2, may hold values from -6 to 6
- sep_blocks: bfloat16 [128, 8, 2, 384, 128], P('blk')
- sep_cols: int32 [128, 8, 2], P('blk'), may hold values from 0 to 15
- sep_inverse: bfloat16 [128, 384, 384], P('blk')
- sep_link: bfloat16 [128, 384, 384], P('blk'), may hold values from -0.21875 to 0.21875
Outputs:
- solution: bfloat16 [2048, 128, 512], P('blk', None, 'cols'), parts along dimension 2
- sep_solution: bfloat16 [128, 384, 512], P('blk', None, 'cols'), parts along dimension 2
There are 2 independent parts, one for each index of `cols`. A program takes and returns all parts, laid end to end along the dimension named above; an argument that names none is the same for every part. Nothing has to cross between parts.
Inputs may be any that keep to these rules, and one draw needn't show every extreme that they name: `local_cols`: subtree row r of a device names its block r - 1 first and a block below r - 1 second; both are 0 for r < 2.
All inputs are finite; a program needn't handle non-finite values.
Results may differ from a plain program's by a relative error of at most 0.015.
Values may be sent and summed in bfloat16 or wider, within the bound.
No kernel may reach another device: no remote copies, remote signals or barrier semaphores. Data moves between devices by JAX's collectives and lax.ppermute only.
A program may use at most 64 MiB of HBM per device.

v0:
```python
import jax
import jax.numpy as jnp
from jax import lax
from jax.sharding import PartitionSpec as P


def partner(value, axis, stride):
    return lax.ppermute(value, axis, [(i, i ^ 1 << stride) for i in range(lax.axis_size(axis))])


def transposed_dot(matrix, vector):
    return lax.dot_general(
        matrix, vector, (((0,), (0,)), ((), ())), preferred_element_type=jnp.float32
    )


def pick_row(array, index):
    return lax.dynamic_index_in_dim(array, index, 0, keepdims=False)


def per_device(
    rhs,
    diag_inverse,
    lower_blocks,
    local_cols,
    sep_rhs,
    sep_blocks,
    sep_cols,
    sep_inverse,
    sep_link,
):
    levels_low = lax.axis_size("blk").bit_length() - 1
    top_count = levels_low + 1
    device = lax.axis_index("blk")
    own_inverse = sep_inverse[0]
    own_link = sep_link[0]
    row_count = rhs.shape[0]
    link_count = lower_blocks.shape[1]
    coupling_count = sep_blocks.shape[2]
    sep_shape = sep_rhs.shape[1:]

    def forward_row(row, solved):
        lower_row = pick_row(lower_blocks, row)
        column_row = pick_row(local_cols, row)
        update = jnp.zeros(rhs.shape[1:], jnp.float32)
        for slot in range(link_count):
            source = pick_row(solved, column_row[slot])
            update = update + jnp.dot(lower_row[slot], source, preferred_element_type=jnp.float32)
        target = (pick_row(rhs, row).astype(jnp.float32) - update).astype(jnp.bfloat16)
        value = jnp.dot(
            pick_row(diag_inverse, row), target, preferred_element_type=jnp.float32
        ).astype(jnp.bfloat16)
        return lax.dynamic_update_index_in_dim(solved, value, row, 0)

    local_solved = lax.fori_loop(0, row_count, forward_row, jnp.zeros_like(rhs))
    pattern = (device ^ device + 1) + 1
    partials = []
    for level_idx in range(top_count):
        total_part = jnp.zeros(sep_shape, jnp.float32)
        for slot in range(coupling_count):
            source = pick_row(local_solved, sep_cols[0, level_idx, slot])
            total_part = total_part + jnp.dot(
                sep_blocks[0, level_idx, slot], source, preferred_element_type=jnp.float32
            )
        owned = pattern == 2 ** (level_idx + 1)
        total_part = total_part - jnp.where(owned, sep_rhs[0].astype(jnp.float32), 0.0)
        partials.append(total_part)

    def owner_of(level):
        return (device >> level << level) + (2 ** (level - 1) - 1)

    node_value = jnp.zeros(sep_shape, jnp.bfloat16)
    for level in range(1, top_count + 1):
        running = partials[level - 1]
        if level >= 2:
            running = running + jnp.where(
                pattern == 2 ** (level - 1),
                jnp.dot(own_link, node_value, preferred_element_type=jnp.float32),
                0.0,
            )
        for bit_index in range(min(level, levels_low)):
            running = running + partner(running, "blk", bit_index)
        node_value = jnp.where(
            pattern == 2**level,
            jnp.dot(
                own_inverse, (-running).astype(jnp.bfloat16), preferred_element_type=jnp.float32
            ).astype(jnp.bfloat16),
            node_value,
        )

    def spread(value, level):
        owner = owner_of(level)
        width_bits = min(level, levels_low)
        low_mask = (1 << width_bits) - 1
        for bit_index in range(width_bits):
            arriving = partner(value, "blk", bit_index)
            done_mask = (1 << bit_index) - 1
            holding = (device ^ owner) & (low_mask & ~done_mask) == 0
            value = jnp.where(holding, value, arriving)
        return value

    ancestors = [None] * top_count
    top_value = transposed_dot(own_inverse, node_value).astype(jnp.bfloat16)
    own_solution = jnp.where(pattern == 2**top_count, top_value, jnp.zeros(sep_shape, jnp.bfloat16))
    ancestors[top_count - 1] = spread(top_value, top_count)
    for level in range(top_count - 1, 0, -1):
        target = (
            node_value.astype(jnp.float32) - transposed_dot(own_link, ancestors[level])
        ).astype(jnp.bfloat16)
        value = transposed_dot(own_inverse, target).astype(jnp.bfloat16)
        own_solution = jnp.where(pattern == 2**level, value, own_solution)
        ancestors[level - 1] = spread(value, level)
    pending = jnp.zeros(rhs.shape, jnp.float32)
    for level_idx in range(top_count):
        for slot in range(coupling_count):
            contrib = transposed_dot(sep_blocks[0, level_idx, slot], ancestors[level_idx])
            pending = pending.at[sep_cols[0, level_idx, slot]].add(contrib)

    def backward_row(step_no, carry):
        solution, pending = carry
        row = row_count - 1 - step_no
        target = (pick_row(local_solved, row).astype(jnp.float32) - pick_row(pending, row)).astype(
            jnp.bfloat16
        )
        value = transposed_dot(pick_row(diag_inverse, row), target).astype(jnp.bfloat16)
        solution = lax.dynamic_update_index_in_dim(solution, value, row, 0)
        lower_row = pick_row(lower_blocks, row)
        column_row = pick_row(local_cols, row)
        for slot in range(link_count):
            pending = pending.at[column_row[slot]].add(transposed_dot(lower_row[slot], value))
        return (solution, pending)

    solution, pending = lax.fori_loop(0, row_count, backward_row, (jnp.zeros_like(rhs), pending))
    return (solution, own_solution[None])


def solution(mesh):
    return jax.shard_map(
        per_device,
        mesh=mesh,
        in_specs=(
            P("blk", None, "cols"),
            P("blk", None, None),
            P("blk", None, None, None),
            P("blk", None),
            P("blk", None, "cols"),
            P("blk", None, None, None, None),
            P("blk", None, None),
            P("blk", None, None),
            P("blk", None, None),
        ),
        out_specs=(P("blk", None, "cols"), P("blk", None, "cols")),
        check_vma=False,
    )
```

profile of v0, /device:TPU:8, one launch (start us, length us, event | category | flops | bytes accessed | tf_op | source)
XLA Modules:
  0.0 955.5 jit_solution(17992533013732084582)
XLA Ops:
  5.4 112.7 %while.48 = (s32[]{:T(128)}, bf16[16,128,256]{2,1,0:T(8,128)(2,1)S(1)}, bf16[16,128,128]{2,1,0:T(8,128)(2,1)}, bf16[16,128,256]{2,1,0:T(8,128)(2,1)}, bf16[16,2,...) while((s32[]{:T(128)}, ...), condition=%wide.region_2.3_spmd, body=%wide.region_1.2_spmd.sunk | while | flops 25329672 | bytes 756453 | solution.py:55
  188.9 8.6 collective-permute-done.6
  232.6 8.4 collective-permute-done.10
  251.2 9.0 collective-permute-done.12
  281.0 7.8 collective-permute-done.15
  289.3 8.9 collective-permute-done.16
  329.5 9.5 collective-permute-done.20
  339.7 7.8 collective-permute-done.21
  347.9 9.0 collective-permute-done.22
  375.3 13.5 %collective-permute-done.25 = f32[384,256]{0,1:T(8,128)S(1)} collective-permute-done((f32[384,256]{0,1:T(8,128)S(1)}, f32[384,256]{0,1:T(8,128)S(1)}, u32[]{:S(2)}, u32[]{:S(2)}) %collective-permute-start.25) | collective-permute-done | bytes 393248 | tf_op jit(solution)/shard_map/ppermute | solution.py:8
  406.4 12.0 %collective-permute-done.27 = f32[384,256]{0,1:T(8,128)S(1)} collective-permute-done((f32[384,256]{0,1:T(8,128)S(1)}, f32[384,256]{0,1:T(8,128)S(1)}, u32[]{:S(2)}, u32[]{:S(2)}) %collective-permute-start.27) | collective-permute-done | bytes 393248 | tf_op jit(solution)/shard_map/ppermute | solution.py:8
  427.3 9.0 collective-permute-done.29
  436.3 10.1 %collective-permute-start.30 = (f32[384,256]{0,1:T(8,128)S(1)}, f32[384,256]{0,1:T(8,128)S(1)}, u32[]{:S(2)}, u32[]{:S(2)}) collective-permute-start(f32[384,256]{0,1:T(8,128)S(1)} %add.590), channel_id=1, source_target_pairs={{0,8},{2,10},{4,12},{6,14},{8,0},{10,2},{12,4},{14,6},{16,24},{18,... | collective-permute-start | bytes 1179656 | tf_op jit(solution)/shard_map/ppermute | solution.py:8
  462.6 7.8 collective-permute-done.32
  470.8 11.9 %collective-permute-done.33 = f32[384,256]{0,1:T(8,128)S(1)} collective-permute-done((f32[384,256]{0,1:T(8,128)S(1)}, f32[384,256]{0,1:T(8,128)S(1)}, u32[]{:S(2)}, u32[]{:S(2)}) %collective-permute-start.33) | collective-permute-done | bytes 393248 | tf_op jit(solution)/shard_map/ppermute | solution.py:8
  486.3 12.0 %collective-permute-done.34 = f32[384,256]{0,1:T(8,128)S(1)} collective-permute-done((f32[384,256]{0,1:T(8,128)S(1)}, f32[384,256]{0,1:T(8,128)S(1)}, u32[]{:S(2)}, u32[]{:S(2)}) %collective-permute-start.34) | collective-permute-done | bytes 393248 | tf_op jit(solution)/shard_map/ppermute | solution.py:8
  544.7 7.7 collective-permute-done.41
  558.9 9.1 collective-permute-done.43
  582.2 9.9 %collective-permute-start.46 = (bf16[384,256]{0,1:T(8,128)(2,1)S(1)}, bf16[384,256]{0,1:T(8,128)(2,1)S(1)}, u32[]{:S(2)}, u32[]{:S(2)}) collective-permute-start(bf16[384,256]{0,1:T(8,128)(2,1)S(1)} %broadcast_select_fusion.10), channel_id=1, source_target_pairs={{0,32},{2,34},{4,36},{6,38},{8,40},{10,42},{12,44},{14,46},{16,48}... | collective-permute-start | bytes 589832 | tf_op jit(solution)/shard_map/ppermute | solution.py:8
  625.1 8.5 collective-permute-done.50
  639.6 9.1 collective-permute-done.52
  654.6 8.1 collective-permute-done.54
  669.1 8.0 collective-permute-done.56
  781.5 172.6 %while.49 = (s32[]{:T(128)}, bf16[16,128,256]{2,1,0:T(8,128)(2,1)S(1)}, f32[16,128,256]{2,1,0:T(8,128)}, bf16[16,128,128]{2,1,0:T(8,128)(2,1)}, bf16[16,128,256]...) while((s32[]{:T(128)}, ...), condition=%wide.region_21.22_spmd, body=%wide.region_18.21_spmd.sunk | while | flops 25428012 | bytes 1085269 | solution.py:133
  (496 shorter events, 600.3 us)
Async XLA Ops:
  121.8 11.2 %collective-permute-start = (f32[384,256]{0,1:T(8,128)}, f32[384,256]{0,1:T(8,128)}, u32[]{:S(2)}, u32[]{:S(2)}) collective-permute-start(f32[384,256]{0,1:T(8,128)} %fusion.46), channel_id=1, source_target_pairs={{0,2},{2,0},{4,6},{6,4},{8,10},{10,8},{12,14},{14,12},{16,18},{18,... | collective-permute-start | bytes 1179656 | tf_op jit(solution)/shard_map/ppermute | solution.py:8
  136.1 10.1 %collective-permute-start.1 = (f32[384,256]{0,1:T(8,128)}, f32[384,256]{0,1:T(8,128)}, u32[]{:S(2)}, u32[]{:S(2)}) collective-permute-start(f32[384,256]{0,1:T(8,128)} %fusion.54), channel_id=1, source_target_pairs={{0,2},{2,0},{4,6},{6,4},{8,10},{10,8},{12,14},{14,12},{16,18},{18,... | collective-permute-start | bytes 1179656 | tf_op jit(solution)/shard_map/ppermute | solution.py:8
  147.4 10.5 %collective-permute-start.2 = (f32[384,256]{0,1:T(8,128)S(1)}, f32[384,256]{0,1:T(8,128)S(1)}, u32[]{:S(2)}, u32[]{:S(2)}) collective-permute-start(f32[384,256]{0,1:T(8,128)S(1)} %add.556), channel_id=1, source_target_pairs={{0,4},{2,6},{4,0},{6,2},{8,12},{10,14},{12,8},{14,10},{16,20},{18,... | collective-permute-start | bytes 1179656 | tf_op jit(solution)/shard_map/ppermute | solution.py:8
  168.0 9.6 %collective-permute-start.4 = (f32[384,256]{0,1:T(8,128)}, f32[384,256]{0,1:T(8,128)}, u32[]{:S(2)}, u32[]{:S(2)}) collective-permute-start(f32[384,256]{0,1:T(8,128)} %add.559), channel_id=1, source_target_pairs={{0,4},{2,6},{4,0},{6,2},{8,12},{10,14},{12,8},{14,10},{16,20},{18,... | collective-permute-start | bytes 1179656 | tf_op jit(solution)/shard_map/ppermute | solution.py:8
  187.3 10.2 %collective-permute-start.6 = (f32[384,256]{0,1:T(8,128)S(1)}, f32[384,256]{0,1:T(8,128)S(1)}, u32[]{:S(2)}, u32[]{:S(2)}) collective-permute-start(f32[384,256]{0,1:T(8,128)S(1)} %fusion.56), channel_id=1, source_target_pairs={{0,2},{2,0},{4,6},{6,4},{8,10},{10,8},{12,14},{14,12},{16,18},{18,... | collective-permute-start | bytes 1179656 | tf_op jit(solution)/shard_map/ppermute | solution.py:8
  197.6 11.0 %collective-permute-start.7 = (f32[384,256]{0,1:T(8,128)S(1)}, f32[384,256]{0,1:T(8,128)S(1)}, u32[]{:S(2)}, u32[]{:S(2)}) collective-permute-start(f32[384,256]{0,1:T(8,128)S(1)} %add.563), channel_id=1, source_target_pairs={{0,4},{2,6},{4,0},{6,2},{8,12},{10,14},{12,8},{14,10},{16,20},{18,... | collective-permute-start | bytes 1179656 | tf_op jit(solution)/shard_map/ppermute | solution.py:8
  209.4 11.0 %collective-permute-start.8 = (f32[384,256]{0,1:T(8,128)}, f32[384,256]{0,1:T(8,128)}, u32[]{:S(2)}, u32[]{:S(2)}) collective-permute-start(f32[384,256]{0,1:T(8,128)} %add.564), channel_id=1, source_target_pairs={{0,8},{2,10},{4,12},{6,14},{8,0},{10,2},{12,4},{14,6},{16,24},{18,... | collective-permute-start | bytes 1179656 | tf_op jit(solution)/shard_map/ppermute | solution.py:8
  221.5 10.3 %collective-permute-start.9 = (f32[384,256]{0,1:T(8,128)S(1)}, f32[384,256]{0,1:T(8,128)S(1)}, u32[]{:S(2)}, u32[]{:S(2)}) collective-permute-start(f32[384,256]{0,1:T(8,128)S(1)} %add.565), channel_id=1, source_target_pairs={{0,16},{2,18},{4,20},{6,22},{8,24},{10,26},{12,28},{14,30},{16,0},... | collective-permute-start | bytes 1179656 | tf_op jit(solution)/shard_map/ppermute | solution.py:8
  241.1 9.4 collective-permute-start.11
  250.5 9.8 %collective-permute-start.12 = (f32[384,256]{0,1:T(8,128)S(1)}, f32[384,256]{0,1:T(8,128)S(1)}, u32[]{:S(2)}, u32[]{:S(2)}) collective-permute-start(f32[384,256]{0,1:T(8,128)S(1)} %add.569), channel_id=1, source_target_pairs={{0,8},{2,10},{4,12},{6,14},{8,0},{10,2},{12,4},{14,6},{16,24},{18,... | collective-permute-start | bytes 1179656 | tf_op jit(solution)/shard_map/ppermute | solution.py:8
  261.1 9.8 %collective-permute-start.13 = (f32[384,256]{0,1:T(8,128)}, f32[384,256]{0,1:T(8,128)}, u32[]{:S(2)}, u32[]{:S(2)}) collective-permute-start(f32[384,256]{0,1:T(8,128)} %add.570), channel_id=1, source_target_pairs={{0,16},{2,18},{4,20},{6,22},{8,24},{10,26},{12,28},{14,30},{16,0},... | collective-permute-start | bytes 1179656 | tf_op jit(solution)/shard_map/ppermute | solution.py:8
  288.8 9.4 collective-permute-start.16
  306.2 9.4 collective-permute-start.18
  325.6 13.4 %collective-permute-start.20 = (f32[384,256]{0,1:T(8,128)S(1)}, f32[384,256]{0,1:T(8,128)S(1)}, u32[]{:S(2)}, u32[]{:S(2)}) collective-permute-start(f32[384,256]{0,1:T(8,128)S(1)} %add.578), channel_id=1, source_target_pairs={{0,64},{2,66},{4,68},{6,70},{8,72},{10,74},{12,76},{14,78},{16,80}... | collective-permute-start | bytes 1179656 | tf_op jit(solution)/shard_map/ppermute | solution.py:8
  374.3 14.6 %collective-permute-start.25 = (f32[384,256]{0,1:T(8,128)S(1)}, f32[384,256]{0,1:T(8,128)S(1)}, u32[]{:S(2)}, u32[]{:S(2)}) collective-permute-start(f32[384,256]{0,1:T(8,128)S(1)} %add.584), channel_id=1, source_target_pairs={{0,32},{2,34},{4,36},{6,38},{8,40},{10,42},{12,44},{14,46},{16,48}... | collective-permute-start | bytes 1179656 | tf_op jit(solution)/shard_map/ppermute | solution.py:8
  389.7 12.7 %collective-permute-start.26 = (f32[384,256]{0,1:T(8,128)}, f32[384,256]{0,1:T(8,128)}, u32[]{:S(2)}, u32[]{:S(2)}) collective-permute-start(f32[384,256]{0,1:T(8,128)} %add.585), channel_id=1, source_target_pairs={{0,64},{2,66},{4,68},{6,70},{8,72},{10,74},{12,76},{14,78},{16,80}... | collective-permute-start | bytes 1179656 | tf_op jit(solution)/shard_map/ppermute | solution.py:8
  403.6 14.8 %collective-permute-start.27 = (f32[384,256]{0,1:T(8,128)S(1)}, f32[384,256]{0,1:T(8,128)S(1)}, u32[]{:S(2)}, u32[]{:S(2)}) collective-permute-start(f32[384,256]{0,1:T(8,128)S(1)} %add.586), channel_id=1, source_target_pairs={{0,128},{2,130},{4,132},{6,134},{8,136},{10,138},{12,140},{14,142}... | collective-permute-start | bytes 1179656 | tf_op jit(solution)/shard_map/ppermute | solution.py:8
  436.3 16.7 %collective-permute-start.30 = (f32[384,256]{0,1:T(8,128)S(1)}, f32[384,256]{0,1:T(8,128)S(1)}, u32[]{:S(2)}, u32[]{:S(2)}) collective-permute-start(f32[384,256]{0,1:T(8,128)S(1)} %add.590), channel_id=1, source_target_pairs={{0,8},{2,10},{4,12},{6,14},{8,0},{10,2},{12,4},{14,6},{16,24},{18,... | collective-permute-start | bytes 1179656 | tf_op jit(solution)/shard_map/ppermute | solution.py:8
  470.4 12.4 %collective-permute-start.33 = (f32[384,256]{0,1:T(8,128)S(1)}, f32[384,256]{0,1:T(8,128)S(1)}, u32[]{:S(2)}, u32[]{:S(2)}) collective-permute-start(f32[384,256]{0,1:T(8,128)S(1)} %add.593), channel_id=1, source_target_pairs={{0,64},{2,66},{4,68},{6,70},{8,72},{10,74},{12,76},{14,78},{16,80}... | collective-permute-start | bytes 1179656 | tf_op jit(solution)/shard_map/ppermute | solution.py:8
  482.8 15.5 %collective-permute-start.34 = (f32[384,256]{0,1:T(8,128)S(1)}, f32[384,256]{0,1:T(8,128)S(1)}, u32[]{:S(2)}, u32[]{:S(2)}) collective-permute-start(f32[384,256]{0,1:T(8,128)S(1)} %add.594), channel_id=1, source_target_pairs={{0,128},{2,130},{4,132},{6,134},{8,136},{10,138},{12,140},{14,142}... | collective-permute-start | bytes 1179656 | tf_op jit(solution)/shard_map/ppermute | solution.py:8
  530.9 10.2 %collective-permute-start.40 = (bf16[384,256]{0,1:T(8,128)(2,1)S(1)}, bf16[384,256]{0,1:T(8,128)(2,1)S(1)}, u32[]{:S(2)}, u32[]{:S(2)}) collective-permute-start(bf16[384,256]{0,1:T(8,128)(2,1)S(1)} %broadcast_select_fusion.4), channel_id=1, source_target_pairs={{0,64},{2,66},{4,68},{6,70},{8,72},{10,74},{12,76},{14,78},{16,80}... | collective-permute-start | bytes 589832 | tf_op jit(solution)/shard_map/ppermute | solution.py:8
  541.1 11.2 %collective-permute-start.41 = (bf16[384,256]{0,1:T(8,128)(2,1)S(1)}, bf16[384,256]{0,1:T(8,128)(2,1)S(1)}, u32[]{:S(2)}, u32[]{:S(2)}) collective-permute-start(bf16[384,256]{0,1:T(8,128)(2,1)S(1)} %broadcast_select_fusion.5), channel_id=1, source_target_pairs={{0,128},{2,130},{4,132},{6,134},{8,136},{10,138},{12,140},{14,142}... | collective-permute-start | bytes 589832 | tf_op jit(solution)/shard_map/ppermute | solution.py:8
  582.2 15.6 %collective-permute-start.46 = (bf16[384,256]{0,1:T(8,128)(2,1)S(1)}, bf16[384,256]{0,1:T(8,128)(2,1)S(1)}, u32[]{:S(2)}, u32[]{:S(2)}) collective-permute-start(bf16[384,256]{0,1:T(8,128)(2,1)S(1)} %broadcast_select_fusion.10), channel_id=1, source_target_pairs={{0,32},{2,34},{4,36},{6,38},{8,40},{10,42},{12,44},{14,46},{16,48}... | collective-permute-start | bytes 589832 | tf_op jit(solution)/shard_map/ppermute | solution.py:8
  606.7 11.8 %collective-permute-start.48 = (bf16[384,256]{0,1:T(8,128)(2,1)S(1)}, bf16[384,256]{0,1:T(8,128)(2,1)S(1)}, u32[]{:S(2)}, u32[]{:S(2)}) collective-permute-start(bf16[384,256]{0,1:T(8,128)(2,1)S(1)} %broadcast_select_fusion.12), channel_id=1, source_target_pairs={{0,128},{2,130},{4,132},{6,134},{8,136},{10,138},{12,140},{14,142}... | collective-permute-start | bytes 589832 | tf_op jit(solution)/shard_map/ppermute | solution.py:8
  (83 other events, 1041.9 us)
where the time goes:
time: 971 us; the launch traced here: 955 us
  waiting for transfers between devices  461 us (47%)
  matrix products  156 us (16%)
  starting transfers between devices  120 us (12%)
  loops' own time  117 us (12%)
  local copies, waits for them, and re-layouts  39.8 us (4%)
  between operations  32.9 us (3%)
  other arithmetic  28.1 us (3%)
    ppermute x70, waiting for transfers between devices, partner(): lax.ppermute(value, axis, [(i, i ^ 1 << stride) for i in range(lax.axis_s...  461 us
    ppermute x70, starting transfers between devices, partner(): lax.ppermute(value, axis, [(i, i ^ 1 << stride) for i in range(lax.axis_s...  120 us
    dot_general x72, matrix products, transposed_dot(): lax.dot_general(matrix, vector, (((0,), (0,)), ((), ())), preferred_eleme...  112 us
    another operation x1, loops' own time, per_device(): lax.fori_loop(0, row_count, backward_row, (jnp.zeros_like(rhs), pending))  58.7 us
    another operation x1, loops' own time, per_device(): local_solved = lax.fori_loop(0, row_count, forward_row, jnp.zeros_like(rhs))  58.1 us
  transfers between devices with their start and end apart: 70, of which 70 were waited for; matrix products, arithmetic and copies ran while one was open for 1% of the time, Pallas kernels for 0%

commit v1 on v0

v1 whole, which is shorter than its diff:
```python
import jax
import jax.numpy as jnp
from jax import lax
from jax.experimental import pallas as pl
from jax.experimental.pallas import tpu as pltpu
from jax.sharding import PartitionSpec as P

F32 = jnp.float32
BF16 = jnp.bfloat16
PLANE_BITS = 4
LOW = 3


def dot(left, right):
    return jnp.dot(left, right, preferred_element_type=F32)


def dot_t(left, right):
    return lax.dot_general(left, right, (((0,), (0,)), ((), ())), preferred_element_type=F32)


def dot_nt(left, right):
    return lax.dot_general(left, right, (((1,), (1,)), ((), ())), preferred_element_type=F32)


def in_vmem(kernel, outs, scalars, arrays, scratch=(), flops=10**9):
    vmem = pl.BlockSpec(memory_space=pltpu.VMEM)
    smem = pl.BlockSpec(memory_space=pltpu.SMEM)
    moved = sum(a.size * a.dtype.itemsize for a in arrays)
    moved += sum(o.size * o.dtype.itemsize for o in outs)
    return pl.pallas_call(
        kernel,
        out_shape=tuple(outs),
        in_specs=[smem] * len(scalars) + [vmem] * len(arrays),
        out_specs=tuple(vmem for _ in outs),
        scratch_shapes=list(scratch),
        compiler_params=pltpu.CompilerParams(vmem_limit_bytes=48 * 2**20),
        cost_estimate=pl.CostEstimate(flops=flops, bytes_accessed=moved, transcendentals=0),
    )(*scalars, *arrays)


def shaped(shape, dtype):
    return jax.ShapeDtypeStruct(shape, dtype)


def whole(halves, index):
    return jnp.concatenate([halves[core, index] for core in range(halves.shape[0])], axis=0)


def gain_kernel(core, inverse, link, gains, full):
    own = inverse[...]
    full[0] = dot(link[...], own).astype(BF16)
    full[1] = dot_t(own, own).astype(BF16)
    rows = gains.shape[1]
    first = pl.multiple_of(core[0] * rows, rows)
    gains[0] = full[0, pl.ds(first, rows)]
    gains[1] = full[1, pl.ds(first, rows)]


def forward_kernel(cols, sep_cols, rhs, inverse, lower, sep_blocks, solved, partial, folded):
    rows, width, _ = rhs.shape
    for row in range(1, rows):
        pair = jnp.concatenate([lower[row, 0], lower[row, 1]], axis=1)
        folded[row] = dot(inverse[row], pair).astype(BF16)
    value = dot(inverse[0], rhs[0]).astype(BF16)
    solved[0] = value
    earlier = value
    for row in range(1, rows):
        base = dot(inverse[row], rhs[row]) - dot(folded[row, :, width:], earlier)
        if row + 1 < rows:
            earlier = solved[cols[row + 1, 1]]
        value = (base - dot(folded[row, :, :width], value)).astype(BF16)
        solved[row] = value
    for level in range(partial.shape[0]):
        pair = jnp.concatenate([sep_blocks[level, 0], sep_blocks[level, 1]], axis=1)
        sources = jnp.concatenate(
            [solved[sep_cols[level, 0]], solved[sep_cols[level, 1]]], axis=0
        )
        partial[level] = dot(pair, sources)


def path_kernel(own_level, partial, sep_rhs, gains, low, high):
    count = partial.shape[0]
    slices, _, slice_rows, _ = high.shape
    for level in range(count):
        total = partial[level]
        total = total - jnp.where(own_level[0] == level, sep_rhs[...].astype(F32), 0.0)
        if 1 <= level <= PLANE_BITS:
            total = total - dot(whole(gains, level - 1), value)
        value = total.astype(BF16)
        turned = value.T
        if level < LOW:
            low[level] = turned
        else:
            for piece in range(slices):
                rows = slice(piece * slice_rows, (piece + 1) * slice_rows)
                high[piece, level - LOW] = turned[rows]


def plane_kernel(arrived, gains, sums):
    for index in range(sums.shape[0]):
        total = arrived[0, index].astype(F32)
        for source in range(1, arrived.shape[0]):
            total = total + arrived[source, index].astype(F32)
        if index >= 2:
            total = total - dot_nt(value, whole(gains, index - 2))
        value = total.astype(BF16)
        sums[index] = total


def top_kernel(sums, finish, spread):
    for index in range(sums.shape[0]):
        value = -dot(sums[index].astype(BF16), whole(finish, index))
        value = value.astype(BF16)
        for piece in range(spread.shape[0]):
            spread[piece, index] = value


def prepare_kernel(cols, sep_cols, solved, inverse, lower, sep_blocks, start, chain, couple):
    rows = solved.shape[0]
    for row in range(rows):
        start[row] = dot_t(inverse[row], solved[row])
    for row in range(1, rows):
        for slot in range(2):
            column = cols[row, slot] if slot else row - 1
            chain[row, slot] = dot(lower[row, slot], inverse[column]).astype(BF16).T
    for level in range(sep_blocks.shape[0]):
        for slot in range(2):
            product = dot(sep_blocks[level, slot], inverse[sep_cols[level, slot]])
            couple[level, slot] = product.astype(BF16).T


def backward_kernel(
    cols,
    sep_cols,
    own_level,
    start,
    chain,
    couple,
    high,
    low1,
    low2,
    low3,
    finish,
    gains_low,
    gains_high,
    solution,
    own,
    pending,
    nodes,
):
    rows = start.shape[0]
    count = nodes.shape[0]
    lows = (low1, low2, low3)
    pending[...] = start[...]
    for level in range(count - 1, -1, -1):
        if level < LOW:
            node = -dot(lows[level][...], whole(finish, level))
        else:
            node = jnp.concatenate(
                [high[piece, level - LOW] for piece in range(high.shape[0])], axis=0
            ).astype(F32)
        if level + 1 < count:
            split = gains_low.shape[1]
            gain = whole(gains_low, level) if level < split else whole(gains_high, level - split)
            node = node - dot(vector, gain)
        vector = node.astype(BF16)
        nodes[level] = vector
        for slot in range(2):
            column = sep_cols[level, slot]
            pending[column] = pending[column] - dot_nt(couple[level, slot], vector)
    own[...] = nodes[own_level[0]].T
    following = pending[rows - 1]
    for row in range(rows - 1, -1, -1):
        value = following.astype(BF16)
        solution[row] = value
        if row:
            following = pending[row - 1] - dot(chain[row, 0], value)
            if row > 1:
                column = cols[row, 1]
                pending[column] = pending[column] - dot(chain[row, 1], value)
            else:
                following = following - dot(chain[row, 1], value)


def swap(value, mask):
    size = lax.axis_size("blk")
    return lax.ppermute(value, "blk", [(i, i ^ mask) for i in range(size)])


def per_device(
    rhs,
    diag_inverse,
    lower_blocks,
    local_cols,
    sep_rhs,
    sep_blocks,
    sep_cols,
    sep_inverse,
    sep_link,
):
    size = lax.axis_size("blk")
    device = lax.axis_index("blk")
    cores = lax.axis_size("cols")
    bits = size.bit_length() - 1
    count = bits + 1
    rows, width, columns = rhs.shape
    sep_width = sep_rhs.shape[1]
    plane = 1 << PLANE_BITS
    slice_rows = columns // plane
    sep_cols = sep_cols[0]
    sep_blocks = sep_blocks[0]
    own_level = sum(
        (((device + 1) & (2**k - 1)) == 0).astype(jnp.int32) for k in range(1, count)
    )[None]

    def step_mask(bit):
        base = 0 if bit < 2 else 2 if bit < 4 else 4
        return (2 << bit) - (1 << base)

    (gains,) = in_vmem(
        gain_kernel,
        [shaped((2, sep_width // cores, sep_width), BF16)],
        [lax.axis_index("cols")[None]],
        [sep_inverse[0], sep_link[0]],
        [pltpu.VMEM((2, sep_width, sep_width), BF16)],
    )

    def ancestors(top):
        found = []
        for bit in range(bits):
            arrived = swap(top, step_mask(bit))
            upper = (device >> bit & 1) == 1
            found.append(jnp.where(upper, arrived, top))
            top = jnp.where(upper, top, arrived)
        return found + [top]

    gain_list = ancestors(gains[0])
    finish_list = ancestors(gains[1])
    gains_low = lax.all_gather(jnp.stack(gain_list[:PLANE_BITS]), "cols")

    solved, partial = in_vmem(
        forward_kernel,
        [shaped(rhs.shape, BF16), shaped((count, sep_width, columns), F32)],
        [local_cols, sep_cols],
        [rhs, diag_inverse, lower_blocks, sep_blocks],
        [pltpu.VMEM((rows, width, 2 * width), BF16)],
    )
    start, chain, couple = in_vmem(
        prepare_kernel,
        [
            shaped(rhs.shape, F32),
            shaped((rows, 2, width, width), BF16),
            shaped((count, 2, width, sep_width), BF16),
        ],
        [local_cols, sep_cols],
        [solved, diag_inverse, lower_blocks, sep_blocks],
    )
    low, high = in_vmem(
        path_kernel,
        [
            shaped((LOW, columns, sep_width), BF16),
            shaped((plane, count - LOW, slice_rows, sep_width), BF16),
        ],
        [own_level],
        [partial, sep_rhs[0], gains_low],
    )

    def added(mine, arrived):
        return (mine.astype(F32) + arrived.astype(F32)).astype(BF16)

    lows = []
    rest = low
    for bit in range(LOW):
        rest = added(rest, swap(rest, step_mask(bit)))
        lows.append(rest[0])
        rest = rest[1:]

    groups = [[g * plane + i for i in range(plane)] for g in range(size // plane)]
    arrived = lax.all_to_all(high, "blk", 0, 0, axis_index_groups=groups, tiled=True)
    gains_high = lax.all_gather(jnp.stack(gain_list[PLANE_BITS:bits]), "cols")
    (sums,) = in_vmem(
        plane_kernel,
        [shaped((count - LOW, slice_rows, sep_width), F32)],
        [],
        [arrived, gains_high],
    )
    for bit in range(PLANE_BITS, bits):
        first = bit - LOW
        part = sums[first:]
        part = part + swap(part.astype(BF16), step_mask(bit)).astype(F32)
        sums = jnp.concatenate([sums[:first], part])
    finish = lax.all_gather(jnp.stack(finish_list), "cols")
    (spread,) = in_vmem(
        top_kernel,
        [shaped(high.shape, BF16)],
        [],
        [sums, finish[:, LOW:]],
    )
    values = lax.all_to_all(spread, "blk", 0, 0, axis_index_groups=groups, tiled=True)
    solution, own = in_vmem(
        backward_kernel,
        [shaped(rhs.shape, BF16), shaped((sep_width, columns), BF16)],
        [local_cols, sep_cols, own_level],
        [start, chain, couple, values, *lows, finish[:, :LOW], gains_low, gains_high],
        [pltpu.VMEM(rhs.shape, F32), pltpu.VMEM((count, columns, sep_width), BF16)],
    )
    return solution, own[None]


def solution(mesh):
    return jax.shard_map(
        per_device,
        mesh=mesh,
        in_specs=(
            P("blk", None, "cols"),
            P("blk", None, None),
            P("blk", None, None, None),
            P("blk", None),
            P("blk", None, "cols"),
            P("blk", None, None, None, None),
            P("blk", None, None),
            P("blk", None, None),
            P("blk", None, None),
        ),
        out_specs=(P("blk", None, "cols"), P("blk", None, "cols")),
        check_vma=False,
    )
```

time: 971 us -> 167 us (0.17); the launches traced: 955 us -> 166 us
  waiting for transfers between devices: 461 us -> 39.3 us
  matrix products: 156 us -> 0 us
  loops' own time: 117 us -> 0 us
  starting transfers between devices: 120 us -> 60.2 us
  local copies, waits for them, and re-layouts: 39.8 us -> 13.4 us
  Pallas kernels: 0 us -> 23.8 us
  between operations: 32.9 us -> 14.4 us
  other arithmetic: 28.1 us -> 12.6 us
    ppermute x70 -> x20, waiting for transfers between devices: 461 us -> 39.3 us  [swap(): return lax.ppermute(value, 'blk', [(i, i ^ mask) for i in range(size)])]
    dot_general x135 -> x0, matrix products: 156 us -> none  [the longest x72 112 us: transposed_dot(): lax.dot_general(matrix, vector, (((0,), (0,)), ((), ())), preferred_eleme...]
    another operation x2 -> x0, loops' own time: 117 us -> none  [the longest x1 58.7 us: per_device(): lax.fori_loop(0, row_count, backward_row, (jnp.zeros_like(rhs), pending))]
    ppermute x70 -> x20, starting transfers between devices: 120 us -> 45.2 us  [swap(): return lax.ppermute(value, 'blk', [(i, i ^ mask) for i in range(size)])]
    pallas_call x0 -> x7, Pallas kernels: none -> 23.8 us  [in_vmem(): pl.pallas_call(kernel, out_shape=tuple(outs), in_specs=[smem] * len(scala...]
    slice x33 -> x8, local copies, waits for them, and re-layouts: 19 us -> 2.89 us  [the longest x1 1.53 us: per_device(): finish[:, LOW:]]
    all_to_all x0 -> x2, starting transfers between devices: none -> 14.9 us  [the longest x1 8.19 us: per_device(): lax.all_to_all(spread, 'blk', 0, 0, axis_index_groups=groups, tiled=True)]
    dynamic_slice x48 -> x0, local copies, waits for them, and re-layouts: 13.5 us -> none  [pick_row(): return lax.dynamic_index_in_dim(array, index, 0, keepdims=False)]
  transfers between devices with their start and end apart: 70 -> 24, of which waited for: 70 -> 12; matrix products, arithmetic and copies ran while one was open for 1% -> 8% of each run, Pallas kernels for 0% -> 9%
where the time goes in v1:
time: 167 us; the launch traced here: 166 us
  starting transfers between devices  60.2 us (36%)
  waiting for transfers between devices  39.3 us (24%)
  Pallas kernels  23.8 us (14%)
  between operations  14.4 us (9%)
  local copies, waits for them, and re-layouts  13.4 us (8%)
  other arithmetic  12.6 us (8%)
  blocking collectives  2.43 us (1%)
    ppermute x20, starting transfers between devices, swap(): return lax.ppermute(value, 'blk', [(i, i ^ mask) for i in range(size)])  45.2 us
    ppermute x20, waiting for transfers between devices, swap(): return lax.ppermute(value, 'blk', [(i, i ^ mask) for i in range(size)])  39.3 us
    pallas_call x7, Pallas kernels, in_vmem(): pl.pallas_call(kernel, out_shape=tuple(outs), in_specs=[smem] * len(scala...  23.8 us
    unnamed x45, local copies, waits for them, and re-layouts  9.75 us
    all_to_all x1, starting transfers between devices, per_device(): lax.all_to_all(spread, 'blk', 0, 0, axis_index_groups=groups, tiled=True)  8.19 us
    all_to_all x1, starting transfers between devices, per_device(): lax.all_to_all(high, 'blk', 0, 0, axis_index_groups=groups, tiled=True)  6.68 us
    unnamed x7, other arithmetic  5.78 us
  transfers between devices with their start and end apart: 24, of which 12 were waited for; matrix products, arithmetic and copies ran while one was open for 8% of the time, Pallas kernels for 9%

profile of v1, /device:TPU:8, one launch (start us, length us, event | category | flops | bytes accessed | tf_op | source)
XLA Modules:
  0.0 166.1 jit_solution(3813372331552257358)
XLA Ops:
  10.4 2.2 %collective-permute-start.10 = (bf16[192,384]{1,0:T(8,128)(2,1)}, bf16[192,384]{1,0:T(8,128)(2,1)}, u32[]{:S(2)}, u32[]{:S(2)}) collective-permute-start(bf16[192,384]{1,0:T(8,128)(2,1)} %slice_bitcast_fusion.2), channel_id=1, source_target_pairs={{0,2},{2,0},{4,6},{6,4},{8,10},{10,8},{12,14},{14,12},{16,18},{18,... | collective-permute-start | bytes 442376 | tf_op jit(solution)/shard_map/ppermute | solution.py:188
  12.6 3.7 %collective-permute-done.10 = bf16[192,384]{1,0:T(8,128)(2,1)} collective-permute-done((bf16[192,384]{1,0:T(8,128)(2,1)}, bf16[192,384]{1,0:T(8,128)(2,1)}, u32[]{:S(2)}, u32[]{:S(2)}) %collective-permute-start.10) | collective-permute-done | bytes 147488 | tf_op jit(solution)/shard_map/ppermute | solution.py:188
  18.8 4.3 %collective-permute-done = bf16[192,384]{1,0:T(8,128)(2,1)S(1)} collective-permute-done((bf16[192,384]{1,0:T(8,128)(2,1)S(1)}, bf16[192,384]{1,0:T(8,128)(2,1)S(1)}, u32[]{:S(2)}, u32[]{:S(2)}) %collective-permute-start) | collective-permute-done | bytes 147488 | tf_op jit(solution)/shard_map/ppermute | solution.py:188
  27.0 5.7 %shard_map.104 = (bf16[16,128,256]{2,1,0:T(8,128)(2,1)S(1)}, f32[8,384,256]{2,1,0:T(8,128)}) custom-call(s32[16,2]{1,0:T(8,128)S(1)} %copy.21.cols, s32[8,2]{1,0:T(8,128)S(1)} %copy.22.sep_cols, bf16[16,128,256]{2,1,0:T(8,128)(2,1)S(1)} %copy-done.9, bf16[16,128,128]{2,1,0:T(8,128)(2,1)S(1)} %copy-done.7, bf16[16,2,128,128]{3,2,1,0:T(8,128)(2,1)S(1)} %copy-done.3, ...), custom_call_target="tpu_custom_call" | custom-call | flops 1000000000 | bytes 8388608 | tf_op jit(solution)/shard_map/pallas_call | solution.py:31
  35.6 2.3 %collective-permute-done.11 = bf16[192,384]{1,0:T(8,128)(2,1)S(1)} collective-permute-done((bf16[192,384]{1,0:T(8,128)(2,1)S(1)}, bf16[192,384]{1,0:T(8,128)(2,1)S(1)}, u32[]{:S(2)}, u32[]{:S(2)}) %collective-permute-start.11) | collective-permute-done | bytes 147488 | tf_op jit(solution)/shard_map/ppermute | solution.py:188
  40.4 2.9 %collective-permute-start.3 = (bf16[192,384]{1,0:T(8,128)(2,1)S(1)}, bf16[192,384]{1,0:T(8,128)(2,1)S(1)}, u32[]{:S(2)}, u32[]{:S(2)}) collective-permute-start(bf16[192,384]{1,0:T(8,128)(2,1)S(1)} %get-tuple-element.36), channel_id=1, source_target_pairs={{0,24},{2,26},{4,28},{6,30},{8,16},{10,18},{12,20},{14,22},{16,8},... | collective-permute-start | bytes 442376 | tf_op jit(solution)/shard_map/ppermute | solution.py:188
  43.3 2.7 %collective-permute-start.13 = (bf16[192,384]{1,0:T(8,128)(2,1)S(1)}, bf16[192,384]{1,0:T(8,128)(2,1)S(1)}, u32[]{:S(2)}, u32[]{:S(2)}) collective-permute-start(bf16[192,384]{1,0:T(8,128)(2,1)S(1)} %broadcast_select_fusion.6), channel_id=1, source_target_pairs={{0,24},{2,26},{4,28},{6,30},{8,16},{10,18},{12,20},{14,22},{16,8},... | collective-permute-start | bytes 442376 | tf_op jit(solution)/shard_map/ppermute | solution.py:188
  53.6 4.8 %collective-permute-start.5 = (bf16[192,384]{1,0:T(8,128)(2,1)S(1)}, bf16[192,384]{1,0:T(8,128)(2,1)}, u32[]{:S(2)}, u32[]{:S(2)}) collective-permute-start(bf16[192,384]{1,0:T(8,128)(2,1)S(1)} %get-tuple-element.28), channel_id=1, source_target_pairs={{0,96},{2,98},{4,100},{6,102},{8,104},{10,106},{12,108},{14,110},{... | collective-permute-start | bytes 442376 | tf_op jit(solution)/shard_map/ppermute | solution.py:188
  58.4 4.6 %collective-permute-start.15 = (bf16[192,384]{1,0:T(8,128)(2,1)S(1)}, bf16[192,384]{1,0:T(8,128)(2,1)S(1)}, u32[]{:S(2)}, u32[]{:S(2)}) collective-permute-start(bf16[192,384]{1,0:T(8,128)(2,1)S(1)} %broadcast_select_fusion.2), channel_id=1, source_target_pairs={{0,96},{2,98},{4,100},{6,102},{8,104},{10,106},{12,108},{14,110},{... | collective-permute-start | bytes 442376 | tf_op jit(solution)/shard_map/ppermute | solution.py:188
  63.7 3.5 %collective-permute-done.15 = bf16[192,384]{1,0:T(8,128)(2,1)S(1)} collective-permute-done((bf16[192,384]{1,0:T(8,128)(2,1)S(1)}, bf16[192,384]{1,0:T(8,128)(2,1)S(1)}, u32[]{:S(2)}, u32[]{:S(2)}) %collective-permute-start.15) | collective-permute-done | bytes 147488 | tf_op jit(solution)/shard_map/ppermute | solution.py:188
  67.3 4.2 %collective-permute-start.16 = (bf16[192,384]{1,0:T(8,128)(2,1)S(1)}, bf16[192,384]{1,0:T(8,128)(2,1)S(1)}, u32[]{:S(2)}, u32[]{:S(2)}) collective-permute-start(bf16[192,384]{1,0:T(8,128)(2,1)S(1)} %broadcast_select_fusion), channel_id=1, source_target_pairs={{0,224},{2,226},{4,228},{6,230},{8,232},{10,234},{12,236},{14,238}... | collective-permute-start | bytes 442376 | tf_op jit(solution)/shard_map/ppermute | solution.py:188
  72.2 4.0 %collective-permute-done.16 = bf16[192,384]{1,0:T(8,128)(2,1)S(1)} collective-permute-done((bf16[192,384]{1,0:T(8,128)(2,1)S(1)}, bf16[192,384]{1,0:T(8,128)(2,1)S(1)}, u32[]{:S(2)}, u32[]{:S(2)}) %collective-permute-start.16) | collective-permute-done | bytes 147488 | tf_op jit(solution)/shard_map/ppermute | solution.py:188
  80.8 2.3 %shard_map.107 = (bf16[3,256,384]{2,1,0:T(8,128)(2,1)S(1)}, bf16[16,5,16,384]{3,2,1,0:T(8,128)(2,1)}) custom-call(s32[1]{0:T(128)} %bitcast.1.own_level, f32[8,384,256]{2,1,0:T(8,128)S(1)} %copy-done.6, bf16[384,256]{1,0:T(8,128)(2,1)S(1)} %bitcast.65, bf16[2,4,192,384]{3,2,1,0:T(8,128)(2,1)S(1)} %bitcast.61), custom_call_target="tpu_custom_call" | custom-call | flops 1000000000 | bytes 6094848 | tf_op jit(solution)/shard_map/pallas_call | solution.py:31
  83.1 6.7 %all-to-all-start = ((bf16[16,5,16,384]{3,2,1,0:T(8,128)(2,1)}), bf16[16,5,16,384]{3,2,1,0:T(8,128)(2,1)}, u32[]{:S(2)}, u32[]{:S(2)}) async-start(bf16[16,5,16,384]{3,2,1,0:T(8,128)(2,1)} %get-tuple-element.16), calls=%async_computation | async-start | bytes 1966080 | tf_op jit(solution)/shard_map/all_to_all | solution.py:280
  90.8 3.6 %collective-permute-start.6 = (bf16[192,384]{1,0:T(8,128)(2,1)S(1)}, bf16[192,384]{1,0:T(8,128)(2,1)S(1)}, u32[]{:S(2)}, u32[]{:S(2)}) collective-permute-start(bf16[192,384]{1,0:T(8,128)(2,1)S(1)} %get-tuple-element.30), channel_id=1, source_target_pairs={{0,224},{2,226},{4,228},{6,230},{8,232},{10,234},{12,236},{14,238}... | collective-permute-start | bytes 442376 | tf_op jit(solution)/shard_map/ppermute | solution.py:188
  94.4 4.7 %collective-permute-done.6 = bf16[192,384]{1,0:T(8,128)(2,1)S(1)} collective-permute-done((bf16[192,384]{1,0:T(8,128)(2,1)S(1)}, bf16[192,384]{1,0:T(8,128)(2,1)S(1)}, u32[]{:S(2)}, u32[]{:S(2)}) %collective-permute-start.6) | collective-permute-done | bytes 147488 | tf_op jit(solution)/shard_map/ppermute | solution.py:188
  99.4 2.4 %all-gather.1 = bf16[6,192,384]{2,1,0:T(8,128)(2,1)S(1)} all-gather(bf16[3,192,384]{2,1,0:T(8,128)(2,1)S(1)} %pad_maximum_fusion.1), channel_id=3, replica_groups=mesh['blk'=128,'cols'=2] {'cols'}, dimensions={0}, use_global_device_ids=true | all-gather | bytes 1327104 | tf_op jit(solution)/shard_map/all_gather | solution.py:281
  104.5 3.3 %shard_map.105 = (f32[16,128,256]{2,1,0:T(8,128)}, bf16[16,2,128,128]{3,2,1,0:T(8,128)(2,1)S(1)}, bf16[8,2,128,384]{3,2,1,0:T(8,128)(2,1)S(1)}) custom-call(s32[16,2]{1,0:T(8,128)S(1)} %copy.21.cols, s32[8,2]{1,0:T(8,128)S(1)} %copy.22.sep_cols, bf16[16,128,256]{2,1,0:T(8,128)(2,1)S(1)} %copy-done.11, bf16[16,128,128]{2,1,0:T(8,128)(2,1)S(1)} %copy-done.7, ...), custom_call_target="tpu_custom_call" | custom-call | flops 1000000000 | bytes 8912896 | tf_op jit(solution)/shard_map/pallas_call | solution.py:31
  108.1 2.3 %collective-permute-start.8 = (bf16[3,16,384]{2,1,0:T(8,128)(2,1)S(1)}, bf16[3,16,384]{2,1,0:T(8,128)(2,1)S(1)}, u32[]{:S(2)}, u32[]{:S(2)}) collective-permute-start(bf16[3,16,384]{2,1,0:T(8,128)(2,1)S(1)} %slice.89), channel_id=1, source_target_pairs={{0,96},{2,98},{4,100},{6,102},{8,104},{10,106},{12,108},{14,110},{... | collective-permute-start | bytes 110600 | tf_op jit(solution)/shard_map/ppermute | solution.py:188
  111.8 2.5 %collective-permute-start.18 = (bf16[2,256,384]{2,1,0:T(8,128)(2,1)S(1)}, bf16[2,256,384]{2,1,0:T(8,128)(2,1)S(1)}, u32[]{:S(2)}, u32[]{:S(2)}) collective-permute-start(bf16[2,256,384]{2,1,0:T(8,128)(2,1)S(1)} %slice.64), channel_id=1, source_target_pairs={{0,6},{2,4},{4,2},{6,0},{8,14},{10,12},{12,10},{14,8},{16,22},{18,... | collective-permute-start | bytes 1179656 | tf_op jit(solution)/shard_map/ppermute | solution.py:188
  114.3 3.7 %collective-permute-start.9 = (bf16[2,16,384]{2,1,0:T(8,128)(2,1)S(1)}, bf16[2,16,384]{2,1,0:T(8,128)(2,1)S(1)}, u32[]{:S(2)}, u32[]{:S(2)}) collective-permute-start(bf16[2,16,384]{2,1,0:T(8,128)(2,1)S(1)} %slice.90), channel_id=1, source_target_pairs={{0,224},{2,226},{4,228},{6,230},{8,232},{10,234},{12,236},{14,238}... | collective-permute-start | bytes 73736 | tf_op jit(solution)/shard_map/ppermute | solution.py:188
  122.7 8.2 %all-to-all-start.1 = ((bf16[16,5,16,384]{3,2,1,0:T(8,128)(2,1)}), bf16[16,5,16,384]{3,2,1,0:T(8,128)(2,1)S(1)}, u32[]{:S(2)}, u32[]{:S(2)}) async-start(bf16[16,5,16,384]{3,2,1,0:T(8,128)(2,1)} %shard_map.109), calls=%async_computation.1 | async-start | bytes 1966080 | tf_op jit(solution)/shard_map/all_to_all | solution.py:300
  132.6 12.9 %collective-permute-done.19 = bf16[1,256,384]{2,1,0:T(8,128)(2,1)S(1)} collective-permute-done((bf16[1,256,384]{2,1,0:T(8,128)(2,1)S(1)}, bf16[1,256,384]{2,1,0:T(8,128)(2,1)S(1)}, u32[]{:S(2)}, u32[]{:S(2)}) %collective-permute-start.19) | collective-permute-done | bytes 196640 | tf_op jit(solution)/shard_map/ppermute | solution.py:188
  150.8 8.5 %shard_map.110 = (bf16[16,128,256]{2,1,0:T(8,128)(2,1)}, bf16[384,256]{1,0:T(8,128)(2,1)}) custom-call(s32[16,2]{1,0:T(8,128)S(1)} %copy.21.cols, s32[8,2]{1,0:T(8,128)S(1)} %copy.22.sep_cols, s32[1]{0:T(128)} %bitcast.1.own_level, f32[16,128,256]{2,1,0:T(8,128)} %get-tuple-element.12.start, bf16[16,2,128,128]{3,2,1,0:T(8,128)(2,1)S(1)} %copy-done.13, ...), custom_call_target="tpu_custom_call" | custom-call | flops 1000000000 | bytes 10485760 | tf_op jit(solution)/shard_map/pallas_call | solution.py:31
  (120 shorter events, 45.9 us)
Async XLA Ops:
  7.2 70.5 %all-gather.6.cloned.1.call-start = ((), (), s32[]{:S(2)}) async-start(), calls=%async_computation.2 | async-start | bytes 1769472 | tf_op jit(solution)/shard_map/all_gather | solution.py:240
  10.4 5.9 %collective-permute-start.10 = (bf16[192,384]{1,0:T(8,128)(2,1)}, bf16[192,384]{1,0:T(8,128)(2,1)}, u32[]{:S(2)}, u32[]{:S(2)}) collective-permute-start(bf16[192,384]{1,0:T(8,128)(2,1)} %slice_bitcast_fusion.2), channel_id=1, source_target_pairs={{0,2},{2,0},{4,6},{6,4},{8,10},{10,8},{12,14},{14,12},{16,18},{18,... | collective-permute-start | bytes 442376 | tf_op jit(solution)/shard_map/ppermute | solution.py:188
  17.9 5.1 %collective-permute-start = (bf16[192,384]{1,0:T(8,128)(2,1)S(1)}, bf16[192,384]{1,0:T(8,128)(2,1)S(1)}, u32[]{:S(2)}, u32[]{:S(2)}) collective-permute-start(bf16[192,384]{1,0:T(8,128)(2,1)S(1)} %get-tuple-element.26), channel_id=1, source_target_pairs={{0,2},{2,0},{4,6},{6,4},{8,10},{10,8},{12,14},{14,12},{16,18},{18,... | collective-permute-start | bytes 442376 | tf_op jit(solution)/shard_map/ppermute | solution.py:188
  23.9 9.1 %collective-permute-start.1 = (bf16[192,384]{1,0:T(8,128)(2,1)}, bf16[192,384]{1,0:T(8,128)(2,1)S(1)}, u32[]{:S(2)}, u32[]{:S(2)}) collective-permute-start(bf16[192,384]{1,0:T(8,128)(2,1)} %get-tuple-element.21), channel_id=1, source_target_pairs={{0,6},{2,4},{4,2},{6,0},{8,14},{10,12},{12,10},{14,8},{16,22},{18,... | collective-permute-start | bytes 442376 | tf_op jit(solution)/shard_map/ppermute | solution.py:188
  32.7 5.1 %collective-permute-start.11 = (bf16[192,384]{1,0:T(8,128)(2,1)S(1)}, bf16[192,384]{1,0:T(8,128)(2,1)S(1)}, u32[]{:S(2)}, u32[]{:S(2)}) collective-permute-start(bf16[192,384]{1,0:T(8,128)(2,1)S(1)} %copy-done.18), channel_id=1, source_target_pairs={{0,6},{2,4},{4,2},{6,0},{8,14},{10,12},{12,10},{14,8},{16,22},{18,... | collective-permute-start | bytes 442376 | tf_op jit(solution)/shard_map/ppermute | solution.py:188
  34.0 6.4 %collective-permute-start.2 = (bf16[192,384]{1,0:T(8,128)(2,1)S(1)}, bf16[192,384]{1,0:T(8,128)(2,1)S(1)}, u32[]{:S(2)}, u32[]{:S(2)}) collective-permute-start(bf16[192,384]{1,0:T(8,128)(2,1)S(1)} %get-tuple-element.34), channel_id=1, source_target_pairs={{0,8},{2,10},{4,12},{6,14},{8,0},{10,2},{12,4},{14,6},{16,24},{18,... | collective-permute-start | bytes 442376 | tf_op jit(solution)/shard_map/ppermute | solution.py:188
  37.9 5.4 %collective-permute-start.12 = (bf16[192,384]{1,0:T(8,128)(2,1)S(1)}, bf16[192,384]{1,0:T(8,128)(2,1)S(1)}, u32[]{:S(2)}, u32[]{:S(2)}) collective-permute-start(bf16[192,384]{1,0:T(8,128)(2,1)S(1)} %broadcast_select_fusion.8), channel_id=1, source_target_pairs={{0,8},{2,10},{4,12},{6,14},{8,0},{10,2},{12,4},{14,6},{16,24},{18,... | collective-permute-start | bytes 442376 | tf_op jit(solution)/shard_map/ppermute | solution.py:188
  40.4 6.8 %collective-permute-start.3 = (bf16[192,384]{1,0:T(8,128)(2,1)S(1)}, bf16[192,384]{1,0:T(8,128)(2,1)S(1)}, u32[]{:S(2)}, u32[]{:S(2)}) collective-permute-start(bf16[192,384]{1,0:T(8,128)(2,1)S(1)} %get-tuple-element.36), channel_id=1, source_target_pairs={{0,24},{2,26},{4,28},{6,30},{8,16},{10,18},{12,20},{14,22},{16,8},... | collective-permute-start | bytes 442376 | tf_op jit(solution)/shard_map/ppermute | solution.py:188
  43.3 7.0 %collective-permute-start.13 = (bf16[192,384]{1,0:T(8,128)(2,1)S(1)}, bf16[192,384]{1,0:T(8,128)(2,1)S(1)}, u32[]{:S(2)}, u32[]{:S(2)}) collective-permute-start(bf16[192,384]{1,0:T(8,128)(2,1)S(1)} %broadcast_select_fusion.6), channel_id=1, source_target_pairs={{0,24},{2,26},{4,28},{6,30},{8,16},{10,18},{12,20},{14,22},{16,8},... | collective-permute-start | bytes 442376 | tf_op jit(solution)/shard_map/ppermute | solution.py:188
  48.3 71.5 %all-gather.8.cloned.1.call-start = ((), (), s32[]{:S(2)}) async-start(), calls=%async_computation.3 | async-start | bytes 3538944 | tf_op jit(solution)/shard_map/all_gather | solution.py:293
  48.3 5.2 %collective-permute-start.4 = (bf16[192,384]{1,0:T(8,128)(2,1)S(1)}, bf16[192,384]{1,0:T(8,128)(2,1)S(1)}, u32[]{:S(2)}, u32[]{:S(2)}) collective-permute-start(bf16[192,384]{1,0:T(8,128)(2,1)S(1)} %get-tuple-element.31), channel_id=1, source_target_pairs={{0,32},{2,34},{4,36},{6,38},{8,40},{10,42},{12,44},{14,46},{16,48}... | collective-permute-start | bytes 442376 | tf_op jit(solution)/shard_map/ppermute | solution.py:188
  50.4 8.0 %collective-permute-start.14 = (bf16[192,384]{1,0:T(8,128)(2,1)S(1)}, bf16[192,384]{1,0:T(8,128)(2,1)S(1)}, u32[]{:S(2)}, u32[]{:S(2)}) collective-permute-start(bf16[192,384]{1,0:T(8,128)(2,1)S(1)} %broadcast_select_fusion.4), channel_id=1, source_target_pairs={{0,32},{2,34},{4,36},{6,38},{8,40},{10,42},{12,44},{14,46},{16,48}... | collective-permute-start | bytes 442376 | tf_op jit(solution)/shard_map/ppermute | solution.py:188
  53.6 36.2 %collective-permute-start.5 = (bf16[192,384]{1,0:T(8,128)(2,1)S(1)}, bf16[192,384]{1,0:T(8,128)(2,1)}, u32[]{:S(2)}, u32[]{:S(2)}) collective-permute-start(bf16[192,384]{1,0:T(8,128)(2,1)S(1)} %get-tuple-element.28), channel_id=1, source_target_pairs={{0,96},{2,98},{4,100},{6,102},{8,104},{10,106},{12,108},{14,110},{... | collective-permute-start | bytes 442376 | tf_op jit(solution)/shard_map/ppermute | solution.py:188
  58.4 8.8 %collective-permute-start.15 = (bf16[192,384]{1,0:T(8,128)(2,1)S(1)}, bf16[192,384]{1,0:T(8,128)(2,1)S(1)}, u32[]{:S(2)}, u32[]{:S(2)}) collective-permute-start(bf16[192,384]{1,0:T(8,128)(2,1)S(1)} %broadcast_select_fusion.2), channel_id=1, source_target_pairs={{0,96},{2,98},{4,100},{6,102},{8,104},{10,106},{12,108},{14,110},{... | collective-permute-start | bytes 442376 | tf_op jit(solution)/shard_map/ppermute | solution.py:188
  67.3 8.9 %collective-permute-start.16 = (bf16[192,384]{1,0:T(8,128)(2,1)S(1)}, bf16[192,384]{1,0:T(8,128)(2,1)S(1)}, u32[]{:S(2)}, u32[]{:S(2)}) collective-permute-start(bf16[192,384]{1,0:T(8,128)(2,1)S(1)} %broadcast_select_fusion), channel_id=1, source_target_pairs={{0,224},{2,226},{4,228},{6,230},{8,232},{10,234},{12,236},{14,238}... | collective-permute-start | bytes 442376 | tf_op jit(solution)/shard_map/ppermute | solution.py:188
  83.1 18.7 %all-to-all-start = ((bf16[16,5,16,384]{3,2,1,0:T(8,128)(2,1)}), bf16[16,5,16,384]{3,2,1,0:T(8,128)(2,1)}, u32[]{:S(2)}, u32[]{:S(2)}) async-start(bf16[16,5,16,384]{3,2,1,0:T(8,128)(2,1)} %get-tuple-element.16), calls=%async_computation | async-start | bytes 1966080 | tf_op jit(solution)/shard_map/all_to_all | solution.py:280
  90.8 8.3 %collective-permute-start.6 = (bf16[192,384]{1,0:T(8,128)(2,1)S(1)}, bf16[192,384]{1,0:T(8,128)(2,1)S(1)}, u32[]{:S(2)}, u32[]{:S(2)}) collective-permute-start(bf16[192,384]{1,0:T(8,128)(2,1)S(1)} %get-tuple-element.30), channel_id=1, source_target_pairs={{0,224},{2,226},{4,228},{6,230},{8,232},{10,234},{12,236},{14,238}... | collective-permute-start | bytes 442376 | tf_op jit(solution)/shard_map/ppermute | solution.py:188
  99.2 11.3 %collective-permute-start.17 = (bf16[3,256,384]{2,1,0:T(8,128)(2,1)S(1)}, bf16[3,256,384]{2,1,0:T(8,128)(2,1)}, u32[]{:S(2)}, u32[]{:S(2)}) collective-permute-start(bf16[3,256,384]{2,1,0:T(8,128)(2,1)S(1)} %get-tuple-element.17), channel_id=1, source_target_pairs={{0,2},{2,0},{4,6},{6,4},{8,10},{10,8},{12,14},{14,12},{16,18},{18,... | collective-permute-start | bytes 1769480 | tf_op jit(solution)/shard_map/ppermute | solution.py:188
  103.9 4.2 %collective-permute-start.7 = (bf16[4,16,384]{2,1,0:T(8,128)(2,1)S(1)}, bf16[4,16,384]{2,1,0:T(8,128)(2,1)S(1)}, u32[]{:S(2)}, u32[]{:S(2)}) collective-permute-start(bf16[4,16,384]{2,1,0:T(8,128)(2,1)S(1)} %slice.88), channel_id=1, source_target_pairs={{0,32},{2,34},{4,36},{6,38},{8,40},{10,42},{12,44},{14,46},{16,48}... | collective-permute-start | bytes 147464 | tf_op jit(solution)/shard_map/ppermute | solution.py:188
  108.1 6.1 %collective-permute-start.8 = (bf16[3,16,384]{2,1,0:T(8,128)(2,1)S(1)}, bf16[3,16,384]{2,1,0:T(8,128)(2,1)S(1)}, u32[]{:S(2)}, u32[]{:S(2)}) collective-permute-start(bf16[3,16,384]{2,1,0:T(8,128)(2,1)S(1)} %slice.89), channel_id=1, source_target_pairs={{0,96},{2,98},{4,100},{6,102},{8,104},{10,106},{12,108},{14,110},{... | collective-permute-start | bytes 110600 | tf_op jit(solution)/shard_map/ppermute | solution.py:188
  111.8 19.1 %collective-permute-start.18 = (bf16[2,256,384]{2,1,0:T(8,128)(2,1)S(1)}, bf16[2,256,384]{2,1,0:T(8,128)(2,1)S(1)}, u32[]{:S(2)}, u32[]{:S(2)}) collective-permute-start(bf16[2,256,384]{2,1,0:T(8,128)(2,1)S(1)} %slice.64), channel_id=1, source_target_pairs={{0,6},{2,4},{4,2},{6,0},{8,14},{10,12},{12,10},{14,8},{16,22},{18,... | collective-permute-start | bytes 1179656 | tf_op jit(solution)/shard_map/ppermute | solution.py:188
  114.3 5.5 %collective-permute-start.9 = (bf16[2,16,384]{2,1,0:T(8,128)(2,1)S(1)}, bf16[2,16,384]{2,1,0:T(8,128)(2,1)S(1)}, u32[]{:S(2)}, u32[]{:S(2)}) collective-permute-start(bf16[2,16,384]{2,1,0:T(8,128)(2,1)S(1)} %slice.90), channel_id=1, source_target_pairs={{0,224},{2,226},{4,228},{6,230},{8,232},{10,234},{12,236},{14,238}... | collective-permute-start | bytes 73736 | tf_op jit(solution)/shard_map/ppermute | solution.py:188
  122.7 24.8 %all-to-all-start.1 = ((bf16[16,5,16,384]{3,2,1,0:T(8,128)(2,1)}), bf16[16,5,16,384]{3,2,1,0:T(8,128)(2,1)S(1)}, u32[]{:S(2)}, u32[]{:S(2)}) async-start(bf16[16,5,16,384]{3,2,1,0:T(8,128)(2,1)} %shard_map.109), calls=%async_computation.1 | async-start | bytes 1966080 | tf_op jit(solution)/shard_map/all_to_all | solution.py:300
  131.0 14.5 %collective-permute-start.19 = (bf16[1,256,384]{2,1,0:T(8,128)(2,1)S(1)}, bf16[1,256,384]{2,1,0:T(8,128)(2,1)S(1)}, u32[]{:S(2)}, u32[]{:S(2)}) collective-permute-start(bf16[1,256,384]{2,1,0:T(8,128)(2,1)S(1)} %get-tuple-element.22), channel_id=1, source_target_pairs={{0,8},{2,10},{4,12},{6,14},{8,0},{10,2},{12,4},{14,6},{16,24},{18,... | collective-permute-start | bytes 589832 | tf_op jit(solution)/shard_map/ppermute | solution.py:188
  (22 other events, 152.3 us)
Sparse Core Ops, SparseCore 0:
  48.4 16.8 all-gather.5
  77.8 16.4 all-gather.7

commit v2 on v1

v2 whole, which is shorter than its diff:
```python
import jax
import jax.numpy as jnp
from jax import lax
from jax.experimental import pallas as pl
from jax.experimental.pallas import tpu as pltpu
from jax.sharding import PartitionSpec as P

F32 = jnp.float32
BF16 = jnp.bfloat16
PLANE_BITS = 4
LOW = 3


def dot(left, right):
    return jnp.dot(left, right, preferred_element_type=F32)


def dot_t(left, right):
    return lax.dot_general(left, right, (((0,), (0,)), ((), ())), preferred_element_type=F32)


def dot_nt(left, right):
    return lax.dot_general(left, right, (((1,), (1,)), ((), ())), preferred_element_type=F32)


def start_all(far, near, sems):
    copies = [pltpu.make_async_copy(far[i], near[i], sems.at[i]) for i in range(len(far))]
    for copy in copies:
        copy.start()
    return copies


def in_vmem(kernel, outs, scalars, arrays, scratch=()):
    counts = len(scalars), len(arrays), len(outs), len(arrays)

    def loaded(*refs):
        parts, first = [], 0
        for amount in counts:
            parts.append(refs[first : first + amount])
            first += amount
        small, far, results, near = parts
        for copy in start_all(far, near, refs[-1]):
            copy.wait()
        kernel(*small, *near, *results, *refs[first:-1])

    return placed(
        loaded,
        outs,
        scalars,
        arrays,
        [pltpu.VMEM(array.shape, array.dtype) for array in arrays]
        + list(scratch)
        + [pltpu.SemaphoreType.DMA((len(arrays),))],
    )


def placed(kernel, outs, scalars, arrays, scratch):
    vmem, smem = pl.BlockSpec(memory_space=pltpu.VMEM), pl.BlockSpec(memory_space=pltpu.SMEM)
    moved = sum(a.size * a.dtype.itemsize for a in arrays)
    moved += sum(o.size * o.dtype.itemsize for o in outs)
    return pl.pallas_call(
        kernel,
        out_shape=tuple(outs),
        in_specs=[smem] * len(scalars) + [pl.BlockSpec(memory_space=pl.ANY)] * len(arrays),
        out_specs=tuple(vmem for _ in outs),
        scratch_shapes=scratch,
        compiler_params=pltpu.CompilerParams(vmem_limit_bytes=56 * 2**20),
        cost_estimate=pl.CostEstimate(flops=10**9, bytes_accessed=moved, transcendentals=0),
    )(*scalars, *arrays)


def shaped(shape, dtype):
    return jax.ShapeDtypeStruct(shape, dtype)


def whole(core, mine, other, index):
    if mine.shape[1] == mine.shape[2]:
        return mine[index]
    first = core[0] == 0
    upper = jnp.where(first, mine[index], other[index])
    lower = jnp.where(first, other[index], mine[index])
    return jnp.concatenate([upper, lower], axis=0)


def gain_kernel(core, inverse, link, gain, finish, full):
    own = inverse[...]
    full[0] = dot(link[...], own).astype(BF16)
    full[1] = dot_t(own, own).astype(BF16)
    rows = gain.shape[0]
    first = pl.multiple_of(core[0] * rows, rows)
    gain[...] = full[0, pl.ds(first, rows)]
    finish[...] = full[1, pl.ds(first, rows)]


def spread_out(pieces, index, value):
    turned = value.T
    rows = pieces.shape[2]
    for piece in range(pieces.shape[0]):
        pieces[piece, index] = turned[piece * rows : (piece + 1) * rows]


def forward_kernel(
    cols,
    sep_cols,
    own_level,
    *refs,
):
    far, (solved, partial), near, (folded, sems) = refs[:5], refs[5:7], refs[7:12], refs[12:]
    inverse, lower, rhs, sep_blocks, sep_rhs = near
    copies = start_all(far, near, sems)
    copies[0].wait()
    copies[1].wait()
    rows, width, _ = rhs.shape
    for row in range(1, rows):
        pair = jnp.concatenate([lower[row, 0], lower[row, 1]], axis=1)
        folded[row] = dot(inverse[row], pair).astype(BF16)
    copies[2].wait()
    value = dot(inverse[0], rhs[0]).astype(BF16)
    solved[0] = value
    earlier = value
    for row in range(1, rows):
        base = dot(inverse[row], rhs[row]) - dot(folded[row, :, width:], earlier)
        if row + 1 < rows:
            earlier = solved[cols[row + 1, 1]]
        value = (base - dot(folded[row, :, :width], value)).astype(BF16)
        solved[row] = value
    copies[3].wait()
    copies[4].wait()
    for level in range(sep_blocks.shape[0]):
        pair = jnp.concatenate([sep_blocks[level, 0], sep_blocks[level, 1]], axis=1)
        sources = jnp.concatenate(
            [solved[sep_cols[level, 0]], solved[sep_cols[level, 1]]], axis=0
        )
        total = dot(pair, sources)
        partial[level] = total - jnp.where(own_level[0] == level, sep_rhs[...].astype(F32), 0.0)


def path_kernel(core, partial, mine, other, low, high):
    for level in range(partial.shape[0]):
        total = partial[level]
        if 1 <= level <= LOW:
            total = total - dot(whole(core, mine, other, level - 1), value)
        value = total.astype(BF16)
        if level < LOW:
            low[level] = value.T
        else:
            spread_out(high, level - LOW, value)


def plane_kernel(core, arrived, mine, other, fourth, above):
    sources = arrived.shape[0]
    value = sum(arrived[source, 0].astype(F32) for source in range(sources)).astype(BF16)
    fourth[...] = value
    for index in range(above.shape[1]):
        total = sum(arrived[source, index + 1].astype(F32) for source in range(sources))
        value = (total - dot_nt(value, whole(core, mine, other, index))).astype(BF16)
        for piece in range(above.shape[0]):
            above[piece, index] = value


def top_kernel(core, place, arrived, fourth, mine, other, spread):
    planes = arrived.shape[0]
    for level in range(spread.shape[1]):
        if level == 0:
            total = fourth[...]
        else:
            index = level - 1
            total = jnp.zeros(fourth.shape, F32)
            for source in range(planes):
                share = arrived[source, index].astype(F32)
                if 2 << index < planes:
                    near = (place[0] >> (index + 1)) == (source >> (index + 1))
                    share = jnp.where(near, share, 0.0)
                total = total + share
            total = total.astype(BF16)
        value = -dot(total, whole(core, mine, other, level))
        value = value.astype(BF16)
        for piece in range(spread.shape[0]):
            spread[piece, level] = value


def prepare_kernel(cols, sep_cols, solved, inverse, lower, sep_blocks, start, chain, couple):
    rows = solved.shape[0]
    for row in range(rows):
        start[row] = dot_t(inverse[row], solved[row])
    for row in range(1, rows):
        for slot in range(2):
            column = cols[row, slot] if slot else row - 1
            chain[row, slot] = dot(lower[row, slot], inverse[column]).astype(BF16).T
    for level in range(sep_blocks.shape[0]):
        for slot in range(2):
            product = dot(sep_blocks[level, slot], inverse[sep_cols[level, slot]])
            couple[level, slot] = product.astype(BF16).T


def backward_kernel(cols, sep_cols, core, own_level, *refs):
    far, (solution, own), near, (pending, nodes, sems) = (
        refs[:13],
        refs[13:15],
        refs[15:-3],
        refs[-3:],
    )
    far = far[:7] + tuple(stack.at[0] for stack in far[7:10]) + far[10:]
    copies = start_all(far, near, sems)
    high, gains_high, gains_high_other, gains_low, gains_low_other = near[:5]
    finish, finish_other = near[5:7]
    low = near[7:10]
    couple, start, chain = near[10:]
    rows = start.shape[0]
    count = nodes.shape[0]
    split = gains_low.shape[0]
    for copy in copies[:10]:
        copy.wait()
    for level in range(count - 1, -1, -1):
        if level < LOW:
            node = -dot(low[level][...], whole(core, finish, finish_other, level))
        else:
            pieces = [high[piece, level - LOW] for piece in range(high.shape[0])]
            node = jnp.concatenate(pieces, axis=0).astype(F32)
        if level + 1 < count:
            if level < split:
                gain = whole(core, gains_low, gains_low_other, level)
            else:
                gain = whole(core, gains_high, gains_high_other, level - split)
            node = node - dot(vector, gain)
        vector = node.astype(BF16)
        nodes[level] = vector
    own[...] = nodes[own_level[0]].T
    for copy in copies[10:]:
        copy.wait()
    pending[...] = start[...]
    for level in range(count - 1, -1, -1):
        for slot in range(2):
            column = sep_cols[level, slot]
            pending[column] = pending[column] - dot_nt(couple[level, slot], nodes[level])
    following = pending[rows - 1]
    for row in range(rows - 1, -1, -1):
        value = following.astype(BF16)
        solution[row] = value
        if row:
            following = pending[row - 1] - dot(chain[row, 0], value)
            if row > 1:
                column = cols[row, 1]
                pending[column] = pending[column] - dot(chain[row, 1], value)
            else:
                following = following - dot(chain[row, 1], value)


def other_core(mine):
    cores = lax.axis_size("cols")
    return lax.ppermute(mine, "cols", [(i, cores - 1 - i) for i in range(cores)])


def with_other_core(flags, pairs):
    mine = jnp.stack([jnp.where(flags[i] == 1, *pair[::-1]) for i, pair in enumerate(pairs)])
    return mine, other_core(mine)


def after(value, earlier):
    return lax.optimization_barrier((value, earlier))[0]


def per_device(
    rhs,
    diag_inverse,
    lower_blocks,
    local_cols,
    sep_rhs,
    sep_blocks,
    sep_cols,
    sep_inverse,
    sep_link,
):
    size = lax.axis_size("blk")
    device = lax.axis_index("blk")
    cores = lax.axis_size("cols")
    bits = size.bit_length() - 1
    count = bits + 1
    rows, width, columns = rhs.shape
    sep_width = sep_rhs.shape[1]
    plane = 1 << PLANE_BITS
    slice_rows = columns // plane
    sep_cols = sep_cols[0]
    sep_blocks = sep_blocks[0]
    own_level = sum(
        (((device + 1) & (2**k - 1)) == 0).astype(jnp.int32) for k in range(1, count)
    )[None]

    def step_mask(bit):
        base = 0 if bit < 2 else 2 if bit < 4 else 4
        return (2 << bit) - (1 << base)

    core = lax.axis_index("cols")[None]
    half = shaped((sep_width // cores, sep_width), BF16)
    gain, finish = in_vmem(
        gain_kernel,
        [half, half],
        [core],
        [sep_inverse[0], sep_link[0]],
        [pltpu.VMEM((2, sep_width, sep_width), BF16)],
    )

    flags = (device >> jnp.arange(count, dtype=jnp.int32)) & 1

    def climb(top, bit):
        mask = step_mask(bit)
        arrived = lax.ppermute(top, "blk", [(i, i ^ mask) for i in range(size)])
        return (top, arrived), jnp.where(flags[bit] == 1, top, arrived)

    piece = (slice_rows, sep_width)
    groups = [[g * plane + i for i in range(plane)] for g in range(size // plane)]
    towers = [[g + i * plane for i in range(size // plane)] for g in range(plane)]

    def within(value, members):
        return lax.all_to_all(value, "blk", 0, 0, axis_index_groups=members, tiled=True)

    arrays = [diag_inverse, lower_blocks, after(rhs, gain), sep_blocks, sep_rhs[0]]
    solved, partial = placed(
        forward_kernel,
        [shaped(rhs.shape, BF16), shaped((count, sep_width, columns), F32)],
        [local_cols, sep_cols, own_level],
        arrays,
        [pltpu.VMEM(array.shape, array.dtype) for array in arrays]
        + [pltpu.VMEM((rows, width, 2 * width), BF16), pltpu.SemaphoreType.DMA((len(arrays),))],
    )
    gain_list, finish_list = [], []

    def climb_gain(bit):
        nonlocal gain
        pair, gain = climb(gain, bit)
        gain_list.append(pair)

    def climb_finish(bit):
        nonlocal finish
        pair, finish = climb(finish, bit)
        finish_list.append(pair)

    def both(bit, event=None):
        nonlocal gain, finish
        finish = after(finish, gain)
        if event is not None:
            gain, finish = after(gain, event), after(finish, event)
        climb_gain(bit)
        climb_finish(bit - 1)

    climb_gain(0)
    both(1, solved)
    for bit in range(2, LOW):
        both(bit)
    gains_low = with_other_core(flags[:LOW], gain_list)
    both(LOW)
    both(LOW + 1)
    low, shares = in_vmem(
        path_kernel,
        [shaped((LOW, columns, sep_width), BF16), shaped((plane, count - LOW, *piece), BF16)],
        [core],
        [partial, *gains_low],
    )
    both(LOW + 2, shares)
    arrived = within(shares, groups)

    def added(mine, other):
        return (mine.astype(F32) + other.astype(F32)).astype(BF16)

    def swapped(value, bit):
        mask = step_mask(bit)
        return added(value, lax.ppermute(value, "blk", [(i, i ^ mask) for i in range(size)]))

    low1 = swapped(after(low, arrived), 0)
    both(LOW + 3, arrived)
    gains_high = with_other_core(flags[LOW:bits], gain_list[LOW:])
    climb_finish(bits - 1)
    finish_list.append((finish, finish))
    fourth, above = in_vmem(
        plane_kernel,
        [shaped(piece, BF16), shaped((size // plane, bits - LOW, *piece), BF16)],
        [core],
        [arrived, *gains_high],
    )
    finish_high = with_other_core(flags[LOW:], finish_list[LOW:])
    low2 = swapped(after(low1[1:], above), 1)
    arrived = after(within(above, towers), low2)
    (spread,) = in_vmem(
        top_kernel,
        [shaped((plane, count - LOW, *piece), BF16)],
        [core, (device >> PLANE_BITS)[None]],
        [arrived, fourth, *finish_high],
    )
    low3 = swapped(after(low2[1:], spread), 2)
    finish_low = with_other_core(flags[:LOW], finish_list[:LOW])
    start, chain, couple = in_vmem(
        prepare_kernel,
        [
            shaped(rhs.shape, F32),
            shaped((rows, 2, width, width), BF16),
            shaped((count, 2, width, sep_width), BF16),
        ],
        [local_cols, sep_cols],
        [after(solved, spread), diag_inverse, lower_blocks, sep_blocks],
    )
    high = within(spread, groups)
    far = [high, *gains_high, *gains_low, *finish_low, low1, low2, low3, couple, start, chain]
    shapes = [array.shape[1:] if 7 <= i < 10 else array.shape for i, array in enumerate(far)]
    solution, own = placed(
        backward_kernel,
        [shaped(rhs.shape, BF16), shaped((sep_width, columns), BF16)],
        [local_cols, sep_cols, core, own_level],
        far,
        [pltpu.VMEM(shape, array.dtype) for shape, array in zip(shapes, far)]
        + [
            pltpu.VMEM(rhs.shape, F32),
            pltpu.VMEM((count, columns, sep_width), BF16),
            pltpu.SemaphoreType.DMA((len(far),)),
        ],
    )
    return solution, own[None]


def solution(mesh):
    return jax.shard_map(
        per_device,
        mesh=mesh,
        in_specs=(
            P("blk", None, "cols"),
            P("blk", None, None),
            P("blk", None, None, None),
            P("blk", None),
            P("blk", None, "cols"),
            P("blk", None, None, None, None),
            P("blk", None, None),
            P("blk", None, None),
            P("blk", None, None),
        ),
        out_specs=(P("blk", None, "cols"), P("blk", None, "cols")),
        check_vma=False,
    )
```

time: 167 us -> 152 us (0.910)
  Pallas kernels: 23.8 us -> 35.4 us
  between operations: 14.4 us -> 5.49 us
  local copies, waits for them, and re-layouts: 13.4 us -> 5.66 us
  other arithmetic: 12.6 us -> 5.13 us
  starting transfers between devices: 60.2 us -> 54.4 us
  waiting for transfers between devices: 39.3 us -> 44.8 us
  blocking collectives: 2.43 us -> 0 us
    pallas_call x7, Pallas kernels: 23.8 us -> 35.4 us  [placed(): pl.pallas_call(kernel, out_shape=tuple(outs), in_specs=[smem] * len(scala...]
    ppermute x20 -> x21, starting transfers between devices: 45.2 us -> 34.5 us  [the longest x14 30.7 us: climb(): arrived = lax.ppermute(top, 'blk', [(i, i ^ mask) for i in range(size)])]
    unnamed x45 -> x33, local copies, waits for them, and re-layouts: 9.75 us -> 4.26 us
    all_to_all x2 -> x3, waiting for transfers between devices: 0.01 us -> 5.07 us  [within(): lax.all_to_all(value, 'blk', 0, 0, axis_index_groups=members, tiled=True)]
    all_to_all x2 -> x3, starting transfers between devices: 14.9 us -> 19.9 us  [within(): lax.all_to_all(value, 'blk', 0, 0, axis_index_groups=members, tiled=True)]
    another operation x9 -> x13, other arithmetic: 4.64 us -> 1.2 us  [with_other_core(): jnp.stack([jnp.where(flags[i] == 1, *pair[::-1]) for i, pair in enumerate...]
    unnamed x7 -> x4, other arithmetic: 5.78 us -> 2.84 us
    all_gather x1 -> x0, blocking collectives: 2.43 us -> none  [per_device(): gains_high = lax.all_gather(jnp.stack(gain_list[PLANE_BITS:bits]), 'cols')]
  transfers between devices with their start and end apart: 24 -> 24, of which waited for: 12 -> 13; matrix products, arithmetic and copies ran while one was open for 8% -> 5% of each run, Pallas kernels for 9% -> 14%
where the time goes in v2:
time: 152 us; the launch traced here: 151 us
  starting transfers between devices  54.4 us (36%)
  waiting for transfers between devices  44.8 us (29%)
  Pallas kernels  35.4 us (23%)
  local copies, waits for them, and re-layouts  5.66 us (4%)
  between operations  5.49 us (4%)
  other arithmetic  5.13 us (3%)
    pallas_call x7, Pallas kernels, placed(): pl.pallas_call(kernel, out_shape=tuple(outs), in_specs=[smem] * len(scala...  35.4 us
    ppermute x14, starting transfers between devices, climb(): arrived = lax.ppermute(top, 'blk', [(i, i ^ mask) for i in range(size)])  30.7 us
    ppermute x14, waiting for transfers between devices, climb(): arrived = lax.ppermute(top, 'blk', [(i, i ^ mask) for i in range(size)])  19.9 us
    all_to_all x3, starting transfers between devices, within(): lax.all_to_all(value, 'blk', 0, 0, axis_index_groups=members, tiled=True)  19.9 us
    ppermute x3, waiting for transfers between devices, swapped(): lax.ppermute(value, 'blk', [(i, i ^ mask) for i in range(size)])  19.8 us
    all_to_all x3, waiting for transfers between devices, within(): lax.all_to_all(value, 'blk', 0, 0, axis_index_groups=members, tiled=True)  5.07 us
    unnamed x33, local copies, waits for them, and re-layouts  4.26 us
    ppermute x3, starting transfers between devices, swapped(): lax.ppermute(value, 'blk', [(i, i ^ mask) for i in range(size)])  3.51 us
  transfers between devices with their start and end apart: 24, of which 13 were waited for; matrix products, arithmetic and copies ran while one was open for 5% of the time, Pallas kernels for 14%

profile of v2, /device:TPU:8, one launch (start us, length us, event | category | flops | bytes accessed | tf_op | source)
XLA Modules:
  0.0 150.9 jit_solution(285958507159287101)
XLA Ops:
  0.7 2.3 %shard_map.104 = (bf16[192,384]{1,0:T(8,128)(2,1)}, bf16[192,384]{1,0:T(8,128)(2,1)}) custom-call(s32[1]{0:T(128)} %bitcast.1.refs_0_.core, bf16[384,384]{1,0:T(8,128)(2,1)} %bitcast.50, bf16[384,384]{1,0:T(8,128)(2,1)} %bitcast.51), custom_call_target="tpu_custom_call" | custom-call | flops 1000000000 | bytes 884736 | tf_op jit(solution)/shard_map/pallas_call | solution.py:61
  3.0 2.3 %collective-permute-start = (bf16[192,384]{1,0:T(8,128)(2,1)}, bf16[192,384]{1,0:T(8,128)(2,1)S(1)}, u32[]{:S(2)}, u32[]{:S(2)}) collective-permute-start(bf16[192,384]{1,0:T(8,128)(2,1)} %get-tuple-element.33), channel_id=1, source_target_pairs={{0,2},{2,0},{4,6},{6,4},{8,10},{10,8},{12,14},{14,12},{16,18},{18,... | collective-permute-start | bytes 442376 | tf_op jit(solution)/shard_map/ppermute | solution.py:307
  8.0 7.5 %shard_map.105 = (bf16[16,128,256]{2,1,0:T(8,128)(2,1)}, f32[8,384,256]{2,1,0:T(8,128)}) custom-call(s32[16,2]{1,0:T(8,128)} %copy.15.cols.refs_0_, s32[8,2]{1,0:T(8,128)} %copy.16.sep_cols.refs_1_, s32[1]{0:T(128)} %bitcast.2.own_level, bf16[16,128,128]{2,1,0:T(8,128)(2,1)} %refs_3_.1, bf16[16,2,128,128]{3,2,1,0:T(8,128)(2,1)} %refs_4_.1, ...), custom_call_target="tpu_custom_call" | custom-call | flops 1000000000 | bytes 8585216 | tf_op jit(solution)/shard_map/pallas_call | solution.py:61
  17.8 3.0 %collective-permute-done.11 = bf16[192,384]{1,0:T(8,128)(2,1)S(1)} collective-permute-done((bf16[192,384]{1,0:T(8,128)(2,1)S(1)}, bf16[192,384]{1,0:T(8,128)(2,1)S(1)}, u32[]{:S(2)}, u32[]{:S(2)}) %collective-permute-start.11) | collective-permute-done | bytes 147488 | tf_op jit(solution)/shard_map/ppermute | solution.py:307
  31.1 2.2 %collective-permute-start.4 = (bf16[192,384]{1,0:T(8,128)(2,1)S(1)}, bf16[192,384]{1,0:T(8,128)(2,1)S(1)}, u32[]{:S(2)}, u32[]{:S(2)}) collective-permute-start(bf16[192,384]{1,0:T(8,128)(2,1)S(1)} %get-tuple-element.76), channel_id=1, source_target_pairs={{0,24},{2,26},{4,28},{6,30},{8,16},{10,18},{12,20},{14,22},{16,8},... | collective-permute-start | bytes 442376 | tf_op jit(solution)/shard_map/ppermute | solution.py:307
  34.2 3.4 %collective-permute-done.4 = bf16[192,384]{1,0:T(8,128)(2,1)S(1)} collective-permute-done((bf16[192,384]{1,0:T(8,128)(2,1)S(1)}, bf16[192,384]{1,0:T(8,128)(2,1)S(1)}, u32[]{:S(2)}, u32[]{:S(2)}) %collective-permute-start.4) | collective-permute-done | bytes 147488 | tf_op jit(solution)/shard_map/ppermute | solution.py:307
  37.6 2.3 %collective-permute-start.14 = (bf16[192,384]{1,0:T(8,128)(2,1)S(1)}, bf16[192,384]{1,0:T(8,128)(2,1)S(1)}, u32[]{:S(2)}, u32[]{:S(2)}) collective-permute-start(bf16[192,384]{1,0:T(8,128)(2,1)S(1)} %get-tuple-element.52), channel_id=1, source_target_pairs={{0,24},{2,26},{4,28},{6,30},{8,16},{10,18},{12,20},{14,22},{16,8},... | collective-permute-start | bytes 442376 | tf_op jit(solution)/shard_map/ppermute | solution.py:307
  44.9 4.1 %shard_map.106 = (bf16[3,256,384]{2,1,0:T(8,128)(2,1)}, bf16[16,5,16,384]{3,2,1,0:T(8,128)(2,1)}) custom-call(s32[1]{0:T(128)} %bitcast.1.refs_0_.core, f32[8,384,256]{2,1,0:T(8,128)} %get-tuple-element.35.refs_1_, bf16[3,192,384]{2,1,0:T(8,128)(2,1)} %copy-done.1, bf16[3,192,384]{2,1,0:T(8,128)(2,1)} %copy-done.5), custom_call_target="tpu_custom_call" | custom-call | flops 1000000000 | bytes 5603328 | tf_op jit(solution)/shard_map/pallas_call | solution.py:61
  49.0 7.3 %all-to-all-start = ((bf16[16,5,16,384]{3,2,1,0:T(8,128)(2,1)}), bf16[16,5,16,384]{3,2,1,0:T(8,128)(2,1)S(1)}, u32[]{:S(2)}, u32[]{:S(2)}) async-start(bf16[16,5,16,384]{3,2,1,0:T(8,128)(2,1)} %get-tuple-element.38), calls=%async_computation | async-start | bytes 1966080 | tf_op jit(solution)/shard_map/all_to_all | solution.py:315
  59.0 2.9 %collective-permute-start.6 = (bf16[192,384]{1,0:T(8,128)(2,1)S(1)}, bf16[192,384]{1,0:T(8,128)(2,1)S(1)}, u32[]{:S(2)}, u32[]{:S(2)}) collective-permute-start(bf16[192,384]{1,0:T(8,128)(2,1)S(1)} %get-tuple-element.39), channel_id=1, source_target_pairs={{0,96},{2,98},{4,100},{6,102},{8,104},{10,106},{12,108},{14,110},{... | collective-permute-start | bytes 442376 | tf_op jit(solution)/shard_map/ppermute | solution.py:307
  61.9 4.2 %collective-permute-done.6 = bf16[192,384]{1,0:T(8,128)(2,1)S(1)} collective-permute-done((bf16[192,384]{1,0:T(8,128)(2,1)S(1)}, bf16[192,384]{1,0:T(8,128)(2,1)S(1)}, u32[]{:S(2)}, u32[]{:S(2)}) %collective-permute-start.6) | collective-permute-done | bytes 147488 | tf_op jit(solution)/shard_map/ppermute | solution.py:307
  67.5 4.5 %collective-permute-start.16 = (bf16[192,384]{1,0:T(8,128)(2,1)S(1)}, bf16[192,384]{1,0:T(8,128)(2,1)S(1)}, u32[]{:S(2)}, u32[]{:S(2)}) collective-permute-start(bf16[192,384]{1,0:T(8,128)(2,1)S(1)} %broadcast_select_fusion.2), channel_id=1, source_target_pairs={{0,96},{2,98},{4,100},{6,102},{8,104},{10,106},{12,108},{14,110},{... | collective-permute-start | bytes 442376 | tf_op jit(solution)/shard_map/ppermute | solution.py:307
  72.8 3.4 %collective-permute-start.7 = (bf16[192,384]{1,0:T(8,128)(2,1)S(1)}, bf16[192,384]{1,0:T(8,128)(2,1)S(1)}, u32[]{:S(2)}, u32[]{:S(2)}) collective-permute-start(bf16[192,384]{1,0:T(8,128)(2,1)S(1)} %get-tuple-element.40), channel_id=1, source_target_pairs={{0,224},{2,226},{4,228},{6,230},{8,232},{10,234},{12,236},{14,238}... | collective-permute-start | bytes 442376 | tf_op jit(solution)/shard_map/ppermute | solution.py:307
  77.6 3.0 %collective-permute-start.17 = (bf16[192,384]{1,0:T(8,128)(2,1)S(1)}, bf16[192,384]{1,0:T(8,128)(2,1)S(1)}, u32[]{:S(2)}, u32[]{:S(2)}) collective-permute-start(bf16[192,384]{1,0:T(8,128)(2,1)S(1)} %broadcast_select_fusion), channel_id=1, source_target_pairs={{0,224},{2,226},{4,228},{6,230},{8,232},{10,234},{12,236},{14,238}... | collective-permute-start | bytes 442376 | tf_op jit(solution)/shard_map/ppermute | solution.py:307
  81.6 4.1 %collective-permute-done.17 = bf16[192,384]{1,0:T(8,128)(2,1)S(1)} collective-permute-done((bf16[192,384]{1,0:T(8,128)(2,1)S(1)}, bf16[192,384]{1,0:T(8,128)(2,1)S(1)}, u32[]{:S(2)}, u32[]{:S(2)}) %collective-permute-start.17) | collective-permute-done | bytes 147488 | tf_op jit(solution)/shard_map/ppermute | solution.py:307
  87.8 3.0 %shard_map.107 = (bf16[16,384]{1,0:T(8,128)(2,1)}, bf16[8,4,16,384]{3,2,1,0:T(8,128)(2,1)}) custom-call(s32[1]{0:T(128)} %bitcast.1.refs_0_.core, bf16[16,5,16,384]{3,2,1,0:T(8,128)(2,1)} %copy-done.7, bf16[4,192,384]{2,1,0:T(8,128)(2,1)} %copy-done.4, bf16[4,192,384]{2,1,0:T(8,128)(2,1)} %copy-done.9), custom_call_target="tpu_custom_call" | custom-call | flops 1000000000 | bytes 2568192 | tf_op jit(solution)/shard_map/pallas_call | solution.py:61
  90.9 5.5 %all-to-all-start.1 = ((bf16[8,4,16,384]{3,2,1,0:T(8,128)(2,1)}), bf16[8,4,16,384]{3,2,1,0:T(8,128)(2,1)S(1)}, u32[]{:S(2)}, u32[]{:S(2)}) async-start(bf16[8,4,16,384]{3,2,1,0:T(8,128)(2,1)} %get-tuple-element.41), calls=%async_computation.1 | async-start | bytes 786432 | tf_op jit(solution)/shard_map/all_to_all | solution.py:315
  97.1 10.8 %collective-permute-done.10 = bf16[2,256,384]{2,1,0:T(8,128)(2,1)S(1)} collective-permute-done((bf16[2,256,384]{2,1,0:T(8,128)(2,1)S(1)}, bf16[2,256,384]{2,1,0:T(8,128)(2,1)S(1)}, u32[]{:S(2)}, u32[]{:S(2)}) %collective-permute-start.10) | collective-permute-done | bytes 393248 | tf_op jit(solution)/shard_map/ppermute | solution.py:367
  108.1 3.7 %all-to-all-done.1.refs_2_ = bf16[8,4,16,384]{3,2,1,0:T(8,128)(2,1)S(1)} async-done(((bf16[8,4,16,384]{3,2,1,0:T(8,128)(2,1)}), bf16[8,4,16,384]{3,2,1,0:T(8,128)(2,1)S(1)}, u32[]{:S(2)}, u32[]{:S(2)}) %all-to-all-start.1) | async-done | bytes 393248 | tf_op jit(solution)/shard_map/all_to_all | solution.py:315
  112.5 2.8 %shard_map.108 = bf16[16,5,16,384]{3,2,1,0:T(8,128)(2,1)} custom-call(s32[1]{0:T(128)} %bitcast.1.refs_0_.core, s32[1]{0:T(128)} %bitcast.3.refs_1_, bf16[8,4,16,384]{3,2,1,0:T(8,128)(2,1)} %copy-done.11, bf16[16,384]{1,0:T(8,128)(2,1)} %get-tuple-element.46.refs_3_, bf16[5,192,384]{2,1,0:T(8,128)(2,1)} %bitcast_dynamic-update-slice_fusion.refs_4_, ...), custom_call_target="tpu_custom_call" | custom-call | flops 1000000000 | bytes 2863104 | tf_op jit(solution)/shard_map/pallas_call | solution.py:61
  115.4 7.1 %all-to-all-start.2 = ((bf16[16,5,16,384]{3,2,1,0:T(8,128)(2,1)}), bf16[16,5,16,384]{3,2,1,0:T(8,128)(2,1)S(1)}, u32[]{:S(2)}, u32[]{:S(2)}) async-start(bf16[16,5,16,384]{3,2,1,0:T(8,128)(2,1)} %shard_map.108), calls=%async_computation.2 | async-start | bytes 1966080 | tf_op jit(solution)/shard_map/all_to_all | solution.py:315
  124.2 6.1 %shard_map.109 = (f32[16,128,256]{2,1,0:T(8,128)}, bf16[16,2,128,128]{3,2,1,0:T(8,128)(2,1)}, bf16[8,2,128,384]{3,2,1,0:T(8,128)(2,1)}) custom-call(s32[16,2]{1,0:T(8,128)} %copy.15.cols.refs_0_, s32[8,2]{1,0:T(8,128)} %copy.16.sep_cols.refs_1_, bf16[16,128,256]{2,1,0:T(8,128)(2,1)} %get-tuple-element.58.refs_2_, bf16[16,128,128]{2,1,0:T(8,128)(2,1)} %refs_3_.1, ...), custom_call_target="tpu_custom_call" | custom-call | flops 1000000000 | bytes 8912896 | tf_op jit(solution)/shard_map/pallas_call | solution.py:61
  130.3 9.0 %collective-permute-done.20 = bf16[1,256,384]{2,1,0:T(8,128)(2,1)S(1)} collective-permute-done((bf16[1,256,384]{2,1,0:T(8,128)(2,1)S(1)}, bf16[1,256,384]{2,1,0:T(8,128)(2,1)S(1)}, u32[]{:S(2)}, u32[]{:S(2)}) %collective-permute-start.20) | collective-permute-done | bytes 196640 | tf_op jit(solution)/shard_map/ppermute | solution.py:367
  141.2 9.6 %shard_map.110 = (bf16[16,128,256]{2,1,0:T(8,128)(2,1)}, bf16[384,256]{1,0:T(8,128)(2,1)}) custom-call(s32[16,2]{1,0:T(8,128)} %copy.15.cols.refs_0_, s32[8,2]{1,0:T(8,128)} %copy.16.sep_cols.refs_1_, s32[1]{0:T(128)} %bitcast.1.refs_0_.core, s32[1]{0:T(128)} %bitcast.2.own_level, bf16[16,5,16,384]{3,2,1,0:T(8,128)(2,1)} %copy-done.2, ...), custom_call_target="tpu_custom_call" | custom-call | flops 1000000000 | bytes 11075584 | tf_op jit(solution)/shard_map/pallas_call | solution.py:61
  (93 shorter events, 31.4 us)
Async XLA Ops:
  3.0 12.5 %collective-permute-start = (bf16[192,384]{1,0:T(8,128)(2,1)}, bf16[192,384]{1,0:T(8,128)(2,1)S(1)}, u32[]{:S(2)}, u32[]{:S(2)}) collective-permute-start(bf16[192,384]{1,0:T(8,128)(2,1)} %get-tuple-element.33), channel_id=1, source_target_pairs={{0,2},{2,0},{4,6},{6,4},{8,10},{10,8},{12,14},{14,12},{16,18},{18,... | collective-permute-start | bytes 442376 | tf_op jit(solution)/shard_map/ppermute | solution.py:307
  15.6 5.2 %collective-permute-start.11 = (bf16[192,384]{1,0:T(8,128)(2,1)S(1)}, bf16[192,384]{1,0:T(8,128)(2,1)S(1)}, u32[]{:S(2)}, u32[]{:S(2)}) collective-permute-start(bf16[192,384]{1,0:T(8,128)(2,1)S(1)} %copy-done.12), channel_id=1, source_target_pairs={{0,2},{2,0},{4,6},{6,4},{8,10},{10,8},{12,14},{14,12},{16,18},{18,... | collective-permute-start | bytes 442376 | tf_op jit(solution)/shard_map/ppermute | solution.py:307
  16.3 5.2 %collective-permute-start.1 = (bf16[192,384]{1,0:T(8,128)(2,1)S(1)}, bf16[192,384]{1,0:T(8,128)(2,1)S(1)}, u32[]{:S(2)}, u32[]{:S(2)}) collective-permute-start(bf16[192,384]{1,0:T(8,128)(2,1)S(1)} %get-tuple-element.37), channel_id=1, source_target_pairs={{0,6},{2,4},{4,2},{6,0},{8,14},{10,12},{12,10},{14,8},{16,22},{18,... | collective-permute-start | bytes 442376 | tf_op jit(solution)/shard_map/ppermute | solution.py:307
  21.5 5.2 %collective-permute-start.12 = (bf16[192,384]{1,0:T(8,128)(2,1)S(1)}, bf16[192,384]{1,0:T(8,128)(2,1)S(1)}, u32[]{:S(2)}, u32[]{:S(2)}) collective-permute-start(bf16[192,384]{1,0:T(8,128)(2,1)S(1)} %get-tuple-element.50), channel_id=1, source_target_pairs={{0,6},{2,4},{4,2},{6,0},{8,14},{10,12},{12,10},{14,8},{16,22},{18,... | collective-permute-start | bytes 442376 | tf_op jit(solution)/shard_map/ppermute | solution.py:307
  23.7 5.2 %collective-permute-start.2 = (bf16[192,384]{1,0:T(8,128)(2,1)S(1)}, bf16[192,384]{1,0:T(8,128)(2,1)S(1)}, u32[]{:S(2)}, u32[]{:S(2)}) collective-permute-start(bf16[192,384]{1,0:T(8,128)(2,1)S(1)} %get-tuple-element.81), channel_id=1, source_target_pairs={{0,8},{2,10},{4,12},{6,14},{8,0},{10,2},{12,4},{14,6},{16,24},{18,... | collective-permute-start | bytes 442376 | tf_op jit(solution)/shard_map/ppermute | solution.py:307
  28.9 5.2 %collective-permute-start.13 = (bf16[192,384]{1,0:T(8,128)(2,1)S(1)}, bf16[192,384]{1,0:T(8,128)(2,1)S(1)}, u32[]{:S(2)}, u32[]{:S(2)}) collective-permute-start(bf16[192,384]{1,0:T(8,128)(2,1)S(1)} %get-tuple-element.51), channel_id=1, source_target_pairs={{0,8},{2,10},{4,12},{6,14},{8,0},{10,2},{12,4},{14,6},{16,24},{18,... | collective-permute-start | bytes 442376 | tf_op jit(solution)/shard_map/ppermute | solution.py:307
  31.1 6.4 %collective-permute-start.4 = (bf16[192,384]{1,0:T(8,128)(2,1)S(1)}, bf16[192,384]{1,0:T(8,128)(2,1)S(1)}, u32[]{:S(2)}, u32[]{:S(2)}) collective-permute-start(bf16[192,384]{1,0:T(8,128)(2,1)S(1)} %get-tuple-element.76), channel_id=1, source_target_pairs={{0,24},{2,26},{4,28},{6,30},{8,16},{10,18},{12,20},{14,22},{16,8},... | collective-permute-start | bytes 442376 | tf_op jit(solution)/shard_map/ppermute | solution.py:307
  33.4 10.7 %collective-permute-start.3 = (bf16[3,192,384]{2,1,0:T(8,128)(2,1)S(1)}, bf16[3,192,384]{2,1,0:T(8,128)(2,1)S(1)}, u32[]{:S(2)}, u32[]{:S(2)}) collective-permute-start(bf16[3,192,384]{2,1,0:T(8,128)(2,1)S(1)} %pad_maximum_fusion.1.refs_2_.refs_3_), channel_id=1, source_target_pairs={{0,1},{1,0},{2,3},{3,2},{4,5},{5,4},{6,7},{7,6},{8,9},{9,8},{10,11... | collective-permute-start | bytes 1327112 | tf_op jit(solution)/shard_map/ppermute | solution.py:251
  37.6 6.4 %collective-permute-start.14 = (bf16[192,384]{1,0:T(8,128)(2,1)S(1)}, bf16[192,384]{1,0:T(8,128)(2,1)S(1)}, u32[]{:S(2)}, u32[]{:S(2)}) collective-permute-start(bf16[192,384]{1,0:T(8,128)(2,1)S(1)} %get-tuple-element.52), channel_id=1, source_target_pairs={{0,24},{2,26},{4,28},{6,30},{8,16},{10,18},{12,20},{14,22},{16,8},... | collective-permute-start | bytes 442376 | tf_op jit(solution)/shard_map/ppermute | solution.py:307
  41.7 14.6 %collective-permute-start.5 = (bf16[192,384]{1,0:T(8,128)(2,1)S(1)}, bf16[192,384]{1,0:T(8,128)(2,1)S(1)}, u32[]{:S(2)}, u32[]{:S(2)}) collective-permute-start(bf16[192,384]{1,0:T(8,128)(2,1)S(1)} %get-tuple-element.71), channel_id=1, source_target_pairs={{0,32},{2,34},{4,36},{6,38},{8,40},{10,42},{12,44},{14,46},{16,48}... | collective-permute-start | bytes 442376 | tf_op jit(solution)/shard_map/ppermute | solution.py:307
  49.0 18.5 %all-to-all-start = ((bf16[16,5,16,384]{3,2,1,0:T(8,128)(2,1)}), bf16[16,5,16,384]{3,2,1,0:T(8,128)(2,1)S(1)}, u32[]{:S(2)}, u32[]{:S(2)}) async-start(bf16[16,5,16,384]{3,2,1,0:T(8,128)(2,1)} %get-tuple-element.38), calls=%async_computation | async-start | bytes 1966080 | tf_op jit(solution)/shard_map/all_to_all | solution.py:315
  56.4 5.5 %collective-permute-start.15 = (bf16[192,384]{1,0:T(8,128)(2,1)S(1)}, bf16[192,384]{1,0:T(8,128)(2,1)S(1)}, u32[]{:S(2)}, u32[]{:S(2)}) collective-permute-start(bf16[192,384]{1,0:T(8,128)(2,1)S(1)} %broadcast_select_fusion.4), channel_id=1, source_target_pairs={{0,32},{2,34},{4,36},{6,38},{8,40},{10,42},{12,44},{14,46},{16,48}... | collective-permute-start | bytes 442376 | tf_op jit(solution)/shard_map/ppermute | solution.py:307
  59.0 7.0 %collective-permute-start.6 = (bf16[192,384]{1,0:T(8,128)(2,1)S(1)}, bf16[192,384]{1,0:T(8,128)(2,1)S(1)}, u32[]{:S(2)}, u32[]{:S(2)}) collective-permute-start(bf16[192,384]{1,0:T(8,128)(2,1)S(1)} %get-tuple-element.39), channel_id=1, source_target_pairs={{0,96},{2,98},{4,100},{6,102},{8,104},{10,106},{12,108},{14,110},{... | collective-permute-start | bytes 442376 | tf_op jit(solution)/shard_map/ppermute | solution.py:307
  67.5 10.1 %collective-permute-start.16 = (bf16[192,384]{1,0:T(8,128)(2,1)S(1)}, bf16[192,384]{1,0:T(8,128)(2,1)S(1)}, u32[]{:S(2)}, u32[]{:S(2)}) collective-permute-start(bf16[192,384]{1,0:T(8,128)(2,1)S(1)} %broadcast_select_fusion.2), channel_id=1, source_target_pairs={{0,96},{2,98},{4,100},{6,102},{8,104},{10,106},{12,108},{14,110},{... | collective-permute-start | bytes 442376 | tf_op jit(solution)/shard_map/ppermute | solution.py:307
  72.8 7.8 %collective-permute-start.7 = (bf16[192,384]{1,0:T(8,128)(2,1)S(1)}, bf16[192,384]{1,0:T(8,128)(2,1)S(1)}, u32[]{:S(2)}, u32[]{:S(2)}) collective-permute-start(bf16[192,384]{1,0:T(8,128)(2,1)S(1)} %get-tuple-element.40), channel_id=1, source_target_pairs={{0,224},{2,226},{4,228},{6,230},{8,232},{10,234},{12,236},{14,238}... | collective-permute-start | bytes 442376 | tf_op jit(solution)/shard_map/ppermute | solution.py:307
  76.1 20.3 %collective-permute-start.9 = (bf16[3,256,384]{2,1,0:T(8,128)(2,1)S(1)}, bf16[3,256,384]{2,1,0:T(8,128)(2,1)S(1)}, u32[]{:S(2)}, u32[]{:S(2)}) collective-permute-start(bf16[3,256,384]{2,1,0:T(8,128)(2,1)S(1)} %copy-done.8), channel_id=1, source_target_pairs={{0,2},{2,0},{4,6},{6,4},{8,10},{10,8},{12,14},{14,12},{16,18},{18,... | collective-permute-start | bytes 1769480 | tf_op jit(solution)/shard_map/ppermute | solution.py:367
  77.6 8.0 %collective-permute-start.17 = (bf16[192,384]{1,0:T(8,128)(2,1)S(1)}, bf16[192,384]{1,0:T(8,128)(2,1)S(1)}, u32[]{:S(2)}, u32[]{:S(2)}) collective-permute-start(bf16[192,384]{1,0:T(8,128)(2,1)S(1)} %broadcast_select_fusion), channel_id=1, source_target_pairs={{0,224},{2,226},{4,228},{6,230},{8,232},{10,234},{12,236},{14,238}... | collective-permute-start | bytes 442376 | tf_op jit(solution)/shard_map/ppermute | solution.py:307
  80.7 6.3 %collective-permute-start.8 = (bf16[4,192,384]{2,1,0:T(8,128)(2,1)S(1)}, bf16[4,192,384]{2,1,0:T(8,128)(2,1)S(1)}, u32[]{:S(2)}, u32[]{:S(2)}) collective-permute-start(bf16[4,192,384]{2,1,0:T(8,128)(2,1)S(1)} %pad_maximum_fusion.refs_2_.refs_1_), channel_id=1, source_target_pairs={{0,1},{1,0},{2,3},{3,2},{4,5},{5,4},{6,7},{7,6},{8,9},{9,8},{10,11... | collective-permute-start | bytes 1769480 | tf_op jit(solution)/shard_map/ppermute | solution.py:251
  87.0 24.8 %collective-permute-start.18 = (bf16[5,192,384]{2,1,0:T(8,128)(2,1)}, bf16[5,192,384]{2,1,0:T(8,128)(2,1)}, u32[]{:S(2)}, u32[]{:S(2)}) collective-permute-start(bf16[5,192,384]{2,1,0:T(8,128)(2,1)} %bitcast_dynamic-update-slice_fusion.refs_4_), channel_id=1, source_target_pairs={{0,1},{1,0},{2,3},{3,2},{4,5},{5,4},{6,7},{7,6},{8,9},{9,8},{10,11... | collective-permute-start | bytes 2211848 | tf_op jit(solution)/shard_map/ppermute | solution.py:251
  90.9 20.9 %all-to-all-start.1 = ((bf16[8,4,16,384]{3,2,1,0:T(8,128)(2,1)}), bf16[8,4,16,384]{3,2,1,0:T(8,128)(2,1)S(1)}, u32[]{:S(2)}, u32[]{:S(2)}) async-start(bf16[8,4,16,384]{3,2,1,0:T(8,128)(2,1)} %get-tuple-element.41), calls=%async_computation.1 | async-start | bytes 786432 | tf_op jit(solution)/shard_map/all_to_all | solution.py:315
  96.6 11.3 %collective-permute-start.10 = (bf16[2,256,384]{2,1,0:T(8,128)(2,1)S(1)}, bf16[2,256,384]{2,1,0:T(8,128)(2,1)S(1)}, u32[]{:S(2)}, u32[]{:S(2)}) collective-permute-start(bf16[2,256,384]{2,1,0:T(8,128)(2,1)S(1)} %slice.73), channel_id=1, source_target_pairs={{0,6},{2,4},{4,2},{6,0},{8,14},{10,12},{12,10},{14,8},{16,22},{18,... | collective-permute-start | bytes 1179656 | tf_op jit(solution)/shard_map/ppermute | solution.py:367
  115.4 24.6 %all-to-all-start.2 = ((bf16[16,5,16,384]{3,2,1,0:T(8,128)(2,1)}), bf16[16,5,16,384]{3,2,1,0:T(8,128)(2,1)S(1)}, u32[]{:S(2)}, u32[]{:S(2)}) async-start(bf16[16,5,16,384]{3,2,1,0:T(8,128)(2,1)} %shard_map.108), calls=%async_computation.2 | async-start | bytes 1966080 | tf_op jit(solution)/shard_map/all_to_all | solution.py:315
  122.5 17.5 %collective-permute-start.19 = (bf16[3,192,384]{2,1,0:T(8,128)(2,1)S(1)}, bf16[3,192,384]{2,1,0:T(8,128)(2,1)S(1)}, u32[]{:S(2)}, u32[]{:S(2)}) collective-permute-start(bf16[3,192,384]{2,1,0:T(8,128)(2,1)S(1)} %pad_maximum_fusion.2.refs_5_), channel_id=1, source_target_pairs={{0,1},{1,0},{2,3},{3,2},{4,5},{5,4},{6,7},{7,6},{8,9},{9,8},{10,11... | collective-permute-start | bytes 1327112 | tf_op jit(solution)/shard_map/ppermute | solution.py:251
  122.7 16.6 %collective-permute-start.20 = (bf16[1,256,384]{2,1,0:T(8,128)(2,1)S(1)}, bf16[1,256,384]{2,1,0:T(8,128)(2,1)S(1)}, u32[]{:S(2)}, u32[]{:S(2)}) collective-permute-start(bf16[1,256,384]{2,1,0:T(8,128)(2,1)S(1)} %slice.74), channel_id=1, source_target_pairs={{0,8},{2,10},{4,12},{6,14},{8,0},{10,2},{12,4},{14,6},{16,24},{18,... | collective-permute-start | bytes 589832 | tf_op jit(solution)/shard_map/ppermute | solution.py:367
  (16 other events, 127.6 us)

commit v3 on v2

--- a/solution.py
+++ b/solution.py
@@ -99,31 +99,55 @@
         pieces[piece, index] = turned[piece * rows : (piece + 1) * rows]
 
 
-def forward_kernel(
-    cols,
-    sep_cols,
-    own_level,
-    *refs,
-):
-    far, (solved, partial), near, (folded, sems) = refs[:5], refs[5:7], refs[7:12], refs[12:]
+def solve_rows(cols, first, inverse, lower, rhs, solved, folded, arrive):
+    rows, width, _ = rhs.shape
+    arrive(0)
+    for row in range(rows):
+        if first + row:
+            pair = jnp.concatenate([lower[row, 0], lower[row, 1]], axis=1)
+            folded[row] = dot(inverse[row], pair).astype(BF16)
+    arrive(1)
+    for row in range(rows):
+        base = dot(inverse[row], rhs[row])
+        if first + row:
+            if row == 0:
+                value = solved[first - 1]
+                earlier = solved[cols[first, 1]]
+            elif first + row == 1:
+                earlier = value
+            base = base - dot(folded[row, :, width:], earlier)
+            base = base - dot(folded[row, :, :width], value)
+        if row + 1 < rows and first + row:
+            earlier = solved[cols[first + row + 1, 1]]
+        value = base.astype(BF16)
+        solved[first + row] = value
+
+
+def first_kernel(cols, *refs):
+    far, (solved,), near, (folded, sems) = refs[:3], refs[3:4], refs[4:7], refs[7:]
+    rows = solved.shape[0]
+    inverse, lower, rhs = near
+    copies = start_all([ref.at[pl.ds(0, rows)] for ref in far], near, sems)
+
+    def arrive(stage):
+        for copy in copies[2:] if stage else copies[:2]:
+            copy.wait()
+
+    solve_rows(cols, 0, inverse, lower, rhs, solved, folded, arrive)
+
+
+def second_kernel(cols, sep_cols, own_level, *refs):
+    far, (solved, partial), near, (folded, sems) = refs[:6], refs[6:8], refs[8:13], refs[13:]
     inverse, lower, rhs, sep_blocks, sep_rhs = near
-    copies = start_all(far, near, sems)
-    copies[0].wait()
-    copies[1].wait()
-    rows, width, _ = rhs.shape
-    for row in range(1, rows):
-        pair = jnp.concatenate([lower[row, 0], lower[row, 1]], axis=1)
-        folded[row] = dot(inverse[row], pair).astype(BF16)
-    copies[2].wait()
-    value = dot(inverse[0], rhs[0]).astype(BF16)
-    solved[0] = value
-    earlier = value
-    for row in range(1, rows):
-        base = dot(inverse[row], rhs[row]) - dot(folded[row, :, width:], earlier)
-        if row + 1 < rows:
-            earlier = solved[cols[row + 1, 1]]
-        value = (base - dot(folded[row, :, :width], value)).astype(BF16)
-        solved[row] = value
+    rows = rhs.shape[0]
+    views = [ref.at[pl.ds(rows, rows)] for ref in far[:3]] + list(far[3:5])
+    copies = start_all(views + [far[5]], [*near, solved.at[pl.ds(0, rows)]], sems)
+
+    def arrive(stage):
+        for copy in (copies[2], copies[5]) if stage else copies[:2]:
+            copy.wait()
+
+    solve_rows(cols, rows, inverse, lower, rhs, solved, folded, arrive)
     copies[3].wait()
     copies[4].wait()
     for level in range(sep_blocks.shape[0]):
@@ -314,14 +338,31 @@
     def within(value, members):
         return lax.all_to_all(value, "blk", 0, 0, axis_index_groups=members, tiled=True)
 
-    arrays = [diag_inverse, lower_blocks, after(rhs, gain), sep_blocks, sep_rhs[0]]
+    half_rows = rows // 2
+    halves = [
+        pltpu.VMEM((half_rows, *array.shape[1:]), BF16)
+        for array in (diag_inverse, lower_blocks, rhs)
+    ]
+    folded = pltpu.VMEM((half_rows, width, 2 * width), BF16)
+    (solved_first,) = placed(
+        first_kernel,
+        [shaped((half_rows, width, columns), BF16)],
+        [local_cols],
+        [diag_inverse, lower_blocks, after(rhs, gain)],
+        [*halves, folded, pltpu.SemaphoreType.DMA((3,))],
+    )
     solved, partial = placed(
-        forward_kernel,
+        second_kernel,
         [shaped(rhs.shape, BF16), shaped((count, sep_width, columns), F32)],
         [local_cols, sep_cols, own_level],
-        arrays,
-        [pltpu.VMEM(array.shape, array.dtype) for array in arrays]
-        + [pltpu.VMEM((rows, width, 2 * width), BF16), pltpu.SemaphoreType.DMA((len(arrays),))],
+        [diag_inverse, lower_blocks, rhs, sep_blocks, sep_rhs[0], solved_first],
+        [
+            *halves,
+            pltpu.VMEM(sep_blocks.shape, BF16),
+            pltpu.VMEM(sep_rhs.shape[1:], BF16),
+            folded,
+            pltpu.SemaphoreType.DMA((6,)),
+        ],
     )
     gain_list, finish_list = [], []
 
@@ -335,29 +376,29 @@
         pair, finish = climb(finish, bit)
         finish_list.append(pair)
 
-    def both(bit, event=None):
-        nonlocal gain, finish
+    def both(bit):
+        nonlocal finish
         finish = after(finish, gain)
-        if event is not None:
-            gain, finish = after(gain, event), after(finish, event)
         climb_gain(bit)
-        climb_finish(bit - 1)
+        climb_finish(bit - 2)
 
     climb_gain(0)
-    both(1, solved)
-    for bit in range(2, LOW):
-        both(bit)
+    gain = after(gain, solved_first)
+    climb_gain(1)
+    both(2)
     gains_low = with_other_core(flags[:LOW], gain_list)
     both(LOW)
-    both(LOW + 1)
     low, shares = in_vmem(
         path_kernel,
         [shaped((LOW, columns, sep_width), BF16), shaped((plane, count - LOW, *piece), BF16)],
         [core],
         [partial, *gains_low],
     )
-    both(LOW + 2, shares)
     arrived = within(shares, groups)
+    gain = after(gain, shares)
+    both(LOW + 1)
+    both(LOW + 2)
+    both(LOW + 3)
 
     def added(mine, other):
         return (mine.astype(F32) + other.astype(F32)).astype(BF16)
@@ -367,26 +408,29 @@
         return added(value, lax.ppermute(value, "blk", [(i, i ^ mask) for i in range(size)]))
 
     low1 = swapped(after(low, arrived), 0)
-    both(LOW + 3, arrived)
+    gain_list[-1] = after(gain_list[-1], arrived)
     gains_high = with_other_core(flags[LOW:bits], gain_list[LOW:])
-    climb_finish(bits - 1)
-    finish_list.append((finish, finish))
+    finish = after(finish, gain)
+    climb_finish(bits - 2)
     fourth, above = in_vmem(
         plane_kernel,
         [shaped(piece, BF16), shaped((size // plane, bits - LOW, *piece), BF16)],
         [core],
         [arrived, *gains_high],
     )
+    finish = after(after(finish, above), low1)
+    climb_finish(bits - 1)
+    finish_list.append((finish, finish))
     finish_high = with_other_core(flags[LOW:], finish_list[LOW:])
-    low2 = swapped(after(low1[1:], above), 1)
-    arrived = after(within(above, towers), low2)
+    low2 = swapped(low1[1:], 1)
+    low3 = swapped(low2[1:], 2)
+    arrived = after(within(above, towers), low3)
     (spread,) = in_vmem(
         top_kernel,
         [shaped((plane, count - LOW, *piece), BF16)],
         [core, (device >> PLANE_BITS)[None]],
         [arrived, fourth, *finish_high],
     )
-    low3 = swapped(after(low2[1:], spread), 2)
     finish_low = with_other_core(flags[:LOW], finish_list[:LOW])
     start, chain, couple = in_vmem(
         prepare_kernel,

time: 152 us -> 160 us (1.053)
  waiting for transfers between devices: 44.8 us -> 52.4 us
  Pallas kernels: 35.4 us -> 38.7 us
  starting transfers between devices: 54.4 us -> 51.6 us
    all_to_all x3, waiting for transfers between devices: 5.07 us -> 16.9 us  [within(): lax.all_to_all(value, 'blk', 0, 0, axis_index_groups=members, tiled=True)]
    ppermute x3, waiting for transfers between devices: 19.8 us -> 9.64 us  [swapped(): lax.ppermute(value, 'blk', [(i, i ^ mask) for i in range(size)])]
    ppermute x14, waiting for transfers between devices: 19.9 us -> 25.9 us  [climb(): arrived = lax.ppermute(top, 'blk', [(i, i ^ mask) for i in range(size)])]
    pallas_call x7 -> x8, Pallas kernels: 35.4 us -> 38.7 us  [placed(): pl.pallas_call(kernel, out_shape=tuple(outs), in_specs=[smem] * len(scala...]
    all_to_all x3, starting transfers between devices: 19.9 us -> 17.6 us  [within(): lax.all_to_all(value, 'blk', 0, 0, axis_index_groups=members, tiled=True)]
    unnamed x33 -> x35, local copies, waits for them, and re-layouts: 4.26 us -> 4.29 us
  transfers between devices with their start and end apart: 24 -> 24, of which waited for: 13 -> 12; matrix products, arithmetic and copies ran while one was open for 5% -> 4% of each run, Pallas kernels for 14% -> 15%
where the time goes in v3:
time: 160 us; the launch traced here: 159 us
  waiting for transfers between devices  52.4 us (33%)
  starting transfers between devices  51.6 us (32%)
  Pallas kernels  38.7 us (24%)
  local copies, waits for them, and re-layouts  5.66 us (4%)
  between operations  5.61 us (4%)
  other arithmetic  5.07 us (3%)
    pallas_call x8, Pallas kernels, placed(): pl.pallas_call(kernel, out_shape=tuple(outs), in_specs=[smem] * len(scala...  38.7 us
    ppermute x14, starting transfers between devices, climb(): arrived = lax.ppermute(top, 'blk', [(i, i ^ mask) for i in range(size)])  30.6 us
    ppermute x14, waiting for transfers between devices, climb(): arrived = lax.ppermute(top, 'blk', [(i, i ^ mask) for i in range(size)])  25.9 us
    all_to_all x3, starting transfers between devices, within(): lax.all_to_all(value, 'blk', 0, 0, axis_index_groups=members, tiled=True)  17.6 us
    all_to_all x3, waiting for transfers between devices, within(): lax.all_to_all(value, 'blk', 0, 0, axis_index_groups=members, tiled=True)  16.9 us
    ppermute x3, waiting for transfers between devices, swapped(): lax.ppermute(value, 'blk', [(i, i ^ mask) for i in range(size)])  9.64 us
    unnamed x35, local copies, waits for them, and re-layouts  4.29 us
  transfers between devices with their start and end apart: 24, of which 12 were waited for; matrix products, arithmetic and copies ran while one was open for 4% of the time, Pallas kernels for 15%

profile of v3, /device:TPU:8, one launch (start us, length us, event | category | flops | bytes accessed | tf_op | source)
XLA Modules:
  0.0 159.1 jit_solution(12330785776563859820)
XLA Ops:
  0.6 2.3 %shard_map.104 = (bf16[192,384]{1,0:T(8,128)(2,1)}, bf16[192,384]{1,0:T(8,128)(2,1)}) custom-call(s32[1]{0:T(128)} %bitcast.1.refs_0_.core, bf16[384,384]{1,0:T(8,128)(2,1)} %bitcast.50, bf16[384,384]{1,0:T(8,128)(2,1)} %bitcast.51), custom_call_target="tpu_custom_call" | custom-call | flops 1000000000 | bytes 884736 | tf_op jit(solution)/shard_map/pallas_call | solution.py:61
  3.0 2.3 %collective-permute-start = (bf16[192,384]{1,0:T(8,128)(2,1)}, bf16[192,384]{1,0:T(8,128)(2,1)S(1)}, u32[]{:S(2)}, u32[]{:S(2)}) collective-permute-start(bf16[192,384]{1,0:T(8,128)(2,1)} %get-tuple-element.30), channel_id=1, source_target_pairs={{0,2},{2,0},{4,6},{6,4},{8,10},{10,8},{12,14},{14,12},{16,18},{18,... | collective-permute-start | bytes 442376 | tf_op jit(solution)/shard_map/ppermute | solution.py:331
  7.3 4.4 %shard_map.105.refs_5_ = bf16[8,128,256]{2,1,0:T(8,128)(2,1)} custom-call(s32[16,2]{1,0:T(8,128)} %copy.16.cols.refs_0_, bf16[16,128,128]{2,1,0:T(8,128)(2,1)} %refs_3_.1, bf16[16,2,128,128]{3,2,1,0:T(8,128)(2,1)} %refs_4_.1, bf16[16,128,256]{2,1,0:T(8,128)(2,1)} %refs_2_.2), custom_call_target="tpu_custom_call" | custom-call | flops 1000000000 | bytes 3145728 | tf_op jit(solution)/shard_map/pallas_call | solution.py:61
  13.1 3.8 %collective-permute-done.1 = bf16[192,384]{1,0:T(8,128)(2,1)S(1)} collective-permute-done((bf16[192,384]{1,0:T(8,128)(2,1)S(1)}, bf16[192,384]{1,0:T(8,128)(2,1)S(1)}, u32[]{:S(2)}, u32[]{:S(2)}) %collective-permute-start.1) | collective-permute-done | bytes 147488 | tf_op jit(solution)/shard_map/ppermute | solution.py:331
  21.5 6.5 %shard_map.106 = (bf16[16,128,256]{2,1,0:T(8,128)(2,1)}, f32[8,384,256]{2,1,0:T(8,128)}) custom-call(s32[16,2]{1,0:T(8,128)} %copy.16.cols.refs_0_, s32[8,2]{1,0:T(8,128)} %copy.17.sep_cols.refs_1_, s32[1]{0:T(128)} %bitcast.2.own_level, bf16[16,128,128]{2,1,0:T(8,128)(2,1)} %refs_3_.1, bf16[16,2,128,128]{3,2,1,0:T(8,128)(2,1)} %refs_4_.1, ...), custom_call_target="tpu_custom_call" | custom-call | flops 1000000000 | bytes 9109504 | tf_op jit(solution)/shard_map/pallas_call | solution.py:61
  28.0 2.2 %collective-permute-start.12 = (bf16[192,384]{1,0:T(8,128)(2,1)S(1)}, bf16[192,384]{1,0:T(8,128)(2,1)S(1)}, u32[]{:S(2)}, u32[]{:S(2)}) collective-permute-start(bf16[192,384]{1,0:T(8,128)(2,1)S(1)} %copy-done.12), channel_id=1, source_target_pairs={{0,2},{2,0},{4,6},{6,4},{8,10},{10,8},{12,14},{14,12},{16,18},{18,... | collective-permute-start | bytes 442376 | tf_op jit(solution)/shard_map/ppermute | solution.py:331
  37.6 4.0 %shard_map.107 = (bf16[3,256,384]{2,1,0:T(8,128)(2,1)}, bf16[16,5,16,384]{3,2,1,0:T(8,128)(2,1)}) custom-call(s32[1]{0:T(128)} %bitcast.1.refs_0_.core, f32[8,384,256]{2,1,0:T(8,128)} %get-tuple-element.32.refs_1_, bf16[3,192,384]{2,1,0:T(8,128)(2,1)} %copy-done.1, bf16[3,192,384]{2,1,0:T(8,128)(2,1)} %copy-done.5), custom_call_target="tpu_custom_call" | custom-call | flops 1000000000 | bytes 5603328 | tf_op jit(solution)/shard_map/pallas_call | solution.py:61
  43.6 6.5 %all-to-all-start = ((bf16[16,5,16,384]{3,2,1,0:T(8,128)(2,1)}), bf16[16,5,16,384]{3,2,1,0:T(8,128)(2,1)S(1)}, u32[]{:S(2)}, u32[]{:S(2)}) async-start(bf16[16,5,16,384]{3,2,1,0:T(8,128)(2,1)} %get-tuple-element.34), calls=%async_computation | async-start | bytes 1966080 | tf_op jit(solution)/shard_map/all_to_all | solution.py:339
  51.6 2.9 %collective-permute-start.6 = (bf16[192,384]{1,0:T(8,128)(2,1)S(1)}, bf16[192,384]{1,0:T(8,128)(2,1)S(1)}, u32[]{:S(2)}, u32[]{:S(2)}) collective-permute-start(bf16[192,384]{1,0:T(8,128)(2,1)S(1)} %get-tuple-element.67), channel_id=1, source_target_pairs={{0,96},{2,98},{4,100},{6,102},{8,104},{10,106},{12,108},{14,110},{... | collective-permute-start | bytes 442376 | tf_op jit(solution)/shard_map/ppermute | solution.py:331
  54.5 8.0 %collective-permute-done.14 = bf16[192,384]{1,0:T(8,128)(2,1)S(1)} collective-permute-done((bf16[192,384]{1,0:T(8,128)(2,1)S(1)}, bf16[192,384]{1,0:T(8,128)(2,1)S(1)}, u32[]{:S(2)}, u32[]{:S(2)}) %collective-permute-start.14) | collective-permute-done | bytes 147488 | tf_op jit(solution)/shard_map/ppermute | solution.py:331
  64.7 5.0 %collective-permute-start.7 = (bf16[192,384]{1,0:T(8,128)(2,1)S(1)}, bf16[192,384]{1,0:T(8,128)(2,1)S(1)}, u32[]{:S(2)}, u32[]{:S(2)}) collective-permute-start(bf16[192,384]{1,0:T(8,128)(2,1)S(1)} %get-tuple-element.37), channel_id=1, source_target_pairs={{0,224},{2,226},{4,228},{6,230},{8,232},{10,234},{12,236},{14,238}... | collective-permute-start | bytes 442376 | tf_op jit(solution)/shard_map/ppermute | solution.py:331
  79.2 4.4 %collective-permute-done.17 = bf16[192,384]{1,0:T(8,128)(2,1)S(1)} collective-permute-done((bf16[192,384]{1,0:T(8,128)(2,1)S(1)}, bf16[192,384]{1,0:T(8,128)(2,1)S(1)}, u32[]{:S(2)}, u32[]{:S(2)}) %collective-permute-start.17) | collective-permute-done | bytes 147488 | tf_op jit(solution)/shard_map/ppermute | solution.py:331
  84.4 3.0 %shard_map.108 = (bf16[16,384]{1,0:T(8,128)(2,1)}, bf16[8,4,16,384]{3,2,1,0:T(8,128)(2,1)}) custom-call(s32[1]{0:T(128)} %bitcast.1.refs_0_.core, bf16[16,5,16,384]{3,2,1,0:T(8,128)(2,1)} %copy-done.7, bf16[4,192,384]{2,1,0:T(8,128)(2,1)} %copy-done.4, bf16[4,192,384]{2,1,0:T(8,128)(2,1)} %copy-done.9), custom_call_target="tpu_custom_call" | custom-call | flops 1000000000 | bytes 2568192 | tf_op jit(solution)/shard_map/pallas_call | solution.py:61
  87.4 3.2 %collective-permute-done.9 = bf16[3,256,384]{2,1,0:T(8,128)(2,1)S(1)} collective-permute-done((bf16[3,256,384]{2,1,0:T(8,128)(2,1)S(1)}, bf16[3,256,384]{2,1,0:T(8,128)(2,1)S(1)}, u32[]{:S(2)}, u32[]{:S(2)}) %collective-permute-start.9) | collective-permute-done | bytes 589856 | tf_op jit(solution)/shard_map/ppermute | solution.py:408
  90.8 3.3 %collective-permute-start.18 = (bf16[192,384]{1,0:T(8,128)(2,1)S(1)}, bf16[192,384]{1,0:T(8,128)(2,1)S(1)}, u32[]{:S(2)}, u32[]{:S(2)}) collective-permute-start(bf16[192,384]{1,0:T(8,128)(2,1)S(1)} %broadcast_select_fusion), channel_id=1, source_target_pairs={{0,224},{2,226},{4,228},{6,230},{8,232},{10,234},{12,236},{14,238}... | collective-permute-start | bytes 442376 | tf_op jit(solution)/shard_map/ppermute | solution.py:331
  96.4 4.5 %collective-permute-done.18 = bf16[192,384]{1,0:T(8,128)(2,1)S(1)} collective-permute-done((bf16[192,384]{1,0:T(8,128)(2,1)S(1)}, bf16[192,384]{1,0:T(8,128)(2,1)S(1)}, u32[]{:S(2)}, u32[]{:S(2)}) %collective-permute-start.18) | collective-permute-done | bytes 147488 | tf_op jit(solution)/shard_map/ppermute | solution.py:331
  102.3 5.6 %all-to-all-start.1 = ((bf16[8,4,16,384]{3,2,1,0:T(8,128)(2,1)}), bf16[8,4,16,384]{3,2,1,0:T(8,128)(2,1)S(1)}, u32[]{:S(2)}, u32[]{:S(2)}) async-start(bf16[8,4,16,384]{3,2,1,0:T(8,128)(2,1)} %get-tuple-element.38), calls=%async_computation.1 | async-start | bytes 786432 | tf_op jit(solution)/shard_map/all_to_all | solution.py:339
  108.7 6.4 %collective-permute-done.11 = bf16[1,256,384]{2,1,0:T(8,128)(2,1)S(1)} collective-permute-done((bf16[1,256,384]{2,1,0:T(8,128)(2,1)S(1)}, bf16[1,256,384]{2,1,0:T(8,128)(2,1)S(1)}, u32[]{:S(2)}, u32[]{:S(2)}) %collective-permute-start.11) | collective-permute-done | bytes 196640 | tf_op jit(solution)/shard_map/ppermute | solution.py:408
  115.9 7.3 %all-to-all-done.1.refs_2_ = bf16[8,4,16,384]{3,2,1,0:T(8,128)(2,1)S(1)} async-done(((bf16[8,4,16,384]{3,2,1,0:T(8,128)(2,1)}), bf16[8,4,16,384]{3,2,1,0:T(8,128)(2,1)S(1)}, u32[]{:S(2)}, u32[]{:S(2)}) %all-to-all-start.1) | async-done | bytes 393248 | tf_op jit(solution)/shard_map/all_to_all | solution.py:339
  124.2 2.8 %shard_map.109 = bf16[16,5,16,384]{3,2,1,0:T(8,128)(2,1)} custom-call(s32[1]{0:T(128)} %bitcast.1.refs_0_.core, s32[1]{0:T(128)} %bitcast.3.refs_1_, bf16[8,4,16,384]{3,2,1,0:T(8,128)(2,1)} %copy-done.11, bf16[16,384]{1,0:T(8,128)(2,1)} %get-tuple-element.42.refs_3_, bf16[5,192,384]{2,1,0:T(8,128)(2,1)} %bitcast_dynamic-update-slice_fusion.refs_4_, ...), custom_call_target="tpu_custom_call" | custom-call | flops 1000000000 | bytes 2863104 | tf_op jit(solution)/shard_map/pallas_call | solution.py:61
  127.1 5.5 %all-to-all-start.2 = ((bf16[16,5,16,384]{3,2,1,0:T(8,128)(2,1)}), bf16[16,5,16,384]{3,2,1,0:T(8,128)(2,1)S(1)}, u32[]{:S(2)}, u32[]{:S(2)}) async-start(bf16[16,5,16,384]{3,2,1,0:T(8,128)(2,1)} %shard_map.109), calls=%async_computation.2 | async-start | bytes 1966080 | tf_op jit(solution)/shard_map/all_to_all | solution.py:339
  132.7 6.1 %shard_map.110 = (f32[16,128,256]{2,1,0:T(8,128)}, bf16[16,2,128,128]{3,2,1,0:T(8,128)(2,1)}, bf16[8,2,128,384]{3,2,1,0:T(8,128)(2,1)}) custom-call(s32[16,2]{1,0:T(8,128)} %copy.16.cols.refs_0_, s32[8,2]{1,0:T(8,128)} %copy.17.sep_cols.refs_1_, bf16[16,128,256]{2,1,0:T(8,128)(2,1)} %get-tuple-element.52.refs_2_, bf16[16,128,128]{2,1,0:T(8,128)(2,1)} %refs_3_.1, ...), custom_call_target="tpu_custom_call" | custom-call | flops 1000000000 | bytes 8912896 | tf_op jit(solution)/shard_map/pallas_call | solution.py:61
  138.8 9.6 %all-to-all-done.2.refs_0_ = bf16[16,5,16,384]{3,2,1,0:T(8,128)(2,1)S(1)} async-done(((bf16[16,5,16,384]{3,2,1,0:T(8,128)(2,1)}), bf16[16,5,16,384]{3,2,1,0:T(8,128)(2,1)S(1)}, u32[]{:S(2)}, u32[]{:S(2)}) %all-to-all-start.2) | async-done | bytes 983072 | tf_op jit(solution)/shard_map/all_to_all | solution.py:339
  149.4 9.6 %shard_map.111 = (bf16[16,128,256]{2,1,0:T(8,128)(2,1)}, bf16[384,256]{1,0:T(8,128)(2,1)}) custom-call(s32[16,2]{1,0:T(8,128)} %copy.16.cols.refs_0_, s32[8,2]{1,0:T(8,128)} %copy.17.sep_cols.refs_1_, s32[1]{0:T(128)} %bitcast.1.refs_0_.core, s32[1]{0:T(128)} %bitcast.2.own_level, bf16[16,5,16,384]{3,2,1,0:T(8,128)(2,1)} %copy-done.2, ...), custom_call_target="tpu_custom_call" | custom-call | flops 1000000000 | bytes 11075584 | tf_op jit(solution)/shard_map/pallas_call | solution.py:61
  (96 shorter events, 34.3 us)
Async XLA Ops:
  3.0 8.7 %collective-permute-start = (bf16[192,384]{1,0:T(8,128)(2,1)}, bf16[192,384]{1,0:T(8,128)(2,1)S(1)}, u32[]{:S(2)}, u32[]{:S(2)}) collective-permute-start(bf16[192,384]{1,0:T(8,128)(2,1)} %get-tuple-element.30), channel_id=1, source_target_pairs={{0,2},{2,0},{4,6},{6,4},{8,10},{10,8},{12,14},{14,12},{16,18},{18,... | collective-permute-start | bytes 442376 | tf_op jit(solution)/shard_map/ppermute | solution.py:331
  11.7 5.2 %collective-permute-start.1 = (bf16[192,384]{1,0:T(8,128)(2,1)S(1)}, bf16[192,384]{1,0:T(8,128)(2,1)S(1)}, u32[]{:S(2)}, u32[]{:S(2)}) collective-permute-start(bf16[192,384]{1,0:T(8,128)(2,1)S(1)} %get-tuple-element.33), channel_id=1, source_target_pairs={{0,6},{2,4},{4,2},{6,0},{8,14},{10,12},{12,10},{14,8},{16,22},{18,... | collective-permute-start | bytes 442376 | tf_op jit(solution)/shard_map/ppermute | solution.py:331
  17.0 13.2 %collective-permute-start.2 = (bf16[192,384]{1,0:T(8,128)(2,1)S(1)}, bf16[192,384]{1,0:T(8,128)(2,1)S(1)}, u32[]{:S(2)}, u32[]{:S(2)}) collective-permute-start(bf16[192,384]{1,0:T(8,128)(2,1)S(1)} %get-tuple-element.75), channel_id=1, source_target_pairs={{0,8},{2,10},{4,12},{6,14},{8,0},{10,2},{12,4},{14,6},{16,24},{18,... | collective-permute-start | bytes 442376 | tf_op jit(solution)/shard_map/ppermute | solution.py:331
  28.0 5.3 %collective-permute-start.12 = (bf16[192,384]{1,0:T(8,128)(2,1)S(1)}, bf16[192,384]{1,0:T(8,128)(2,1)S(1)}, u32[]{:S(2)}, u32[]{:S(2)}) collective-permute-start(bf16[192,384]{1,0:T(8,128)(2,1)S(1)} %copy-done.12), channel_id=1, source_target_pairs={{0,2},{2,0},{4,6},{6,4},{8,10},{10,8},{12,14},{14,12},{16,18},{18,... | collective-permute-start | bytes 442376 | tf_op jit(solution)/shard_map/ppermute | solution.py:331
  30.2 6.4 %collective-permute-start.4 = (bf16[192,384]{1,0:T(8,128)(2,1)S(1)}, bf16[192,384]{1,0:T(8,128)(2,1)S(1)}, u32[]{:S(2)}, u32[]{:S(2)}) collective-permute-start(bf16[192,384]{1,0:T(8,128)(2,1)S(1)} %get-tuple-element.70), channel_id=1, source_target_pairs={{0,24},{2,26},{4,28},{6,30},{8,16},{10,18},{12,20},{14,22},{16,8},... | collective-permute-start | bytes 442376 | tf_op jit(solution)/shard_map/ppermute | solution.py:331
  32.5 4.2 %collective-permute-start.3 = (bf16[3,192,384]{2,1,0:T(8,128)(2,1)S(1)}, bf16[3,192,384]{2,1,0:T(8,128)(2,1)S(1)}, u32[]{:S(2)}, u32[]{:S(2)}) collective-permute-start(bf16[3,192,384]{2,1,0:T(8,128)(2,1)S(1)} %pad_maximum_fusion.1.refs_2_.refs_3_), channel_id=1, source_target_pairs={{0,1},{1,0},{2,3},{3,2},{4,5},{5,4},{6,7},{7,6},{8,9},{9,8},{10,11... | collective-permute-start | bytes 1327112 | tf_op jit(solution)/shard_map/ppermute | solution.py:275
  33.4 10.2 %collective-permute-start.13 = (bf16[192,384]{1,0:T(8,128)(2,1)S(1)}, bf16[192,384]{1,0:T(8,128)(2,1)S(1)}, u32[]{:S(2)}, u32[]{:S(2)}) collective-permute-start(bf16[192,384]{1,0:T(8,128)(2,1)S(1)} %get-tuple-element.45), channel_id=1, source_target_pairs={{0,6},{2,4},{4,2},{6,0},{8,14},{10,12},{12,10},{14,8},{16,22},{18,... | collective-permute-start | bytes 442376 | tf_op jit(solution)/shard_map/ppermute | solution.py:331
  41.6 10.0 %collective-permute-start.5 = (bf16[192,384]{1,0:T(8,128)(2,1)S(1)}, bf16[192,384]{1,0:T(8,128)(2,1)S(1)}, u32[]{:S(2)}, u32[]{:S(2)}) collective-permute-start(bf16[192,384]{1,0:T(8,128)(2,1)S(1)} %get-tuple-element.35), channel_id=1, source_target_pairs={{0,32},{2,34},{4,36},{6,38},{8,40},{10,42},{12,44},{14,46},{16,48}... | collective-permute-start | bytes 442376 | tf_op jit(solution)/shard_map/ppermute | solution.py:331
  43.6 30.8 %all-to-all-start = ((bf16[16,5,16,384]{3,2,1,0:T(8,128)(2,1)}), bf16[16,5,16,384]{3,2,1,0:T(8,128)(2,1)S(1)}, u32[]{:S(2)}, u32[]{:S(2)}) async-start(bf16[16,5,16,384]{3,2,1,0:T(8,128)(2,1)} %get-tuple-element.34), calls=%async_computation | async-start | bytes 1966080 | tf_op jit(solution)/shard_map/all_to_all | solution.py:339
  50.1 12.4 %collective-permute-start.14 = (bf16[192,384]{1,0:T(8,128)(2,1)S(1)}, bf16[192,384]{1,0:T(8,128)(2,1)S(1)}, u32[]{:S(2)}, u32[]{:S(2)}) collective-permute-start(bf16[192,384]{1,0:T(8,128)(2,1)S(1)} %get-tuple-element.46), channel_id=1, source_target_pairs={{0,8},{2,10},{4,12},{6,14},{8,0},{10,2},{12,4},{14,6},{16,24},{18,... | collective-permute-start | bytes 442376 | tf_op jit(solution)/shard_map/ppermute | solution.py:331
  51.6 13.0 %collective-permute-start.6 = (bf16[192,384]{1,0:T(8,128)(2,1)S(1)}, bf16[192,384]{1,0:T(8,128)(2,1)S(1)}, u32[]{:S(2)}, u32[]{:S(2)}) collective-permute-start(bf16[192,384]{1,0:T(8,128)(2,1)S(1)} %get-tuple-element.67), channel_id=1, source_target_pairs={{0,96},{2,98},{4,100},{6,102},{8,104},{10,106},{12,108},{14,110},{... | collective-permute-start | bytes 442376 | tf_op jit(solution)/shard_map/ppermute | solution.py:331
  62.6 7.2 %collective-permute-start.15 = (bf16[192,384]{1,0:T(8,128)(2,1)S(1)}, bf16[192,384]{1,0:T(8,128)(2,1)S(1)}, u32[]{:S(2)}, u32[]{:S(2)}) collective-permute-start(bf16[192,384]{1,0:T(8,128)(2,1)S(1)} %get-tuple-element.47), channel_id=1, source_target_pairs={{0,24},{2,26},{4,28},{6,30},{8,16},{10,18},{12,20},{14,22},{16,8},... | collective-permute-start | bytes 442376 | tf_op jit(solution)/shard_map/ppermute | solution.py:331
  64.7 9.7 %collective-permute-start.7 = (bf16[192,384]{1,0:T(8,128)(2,1)S(1)}, bf16[192,384]{1,0:T(8,128)(2,1)S(1)}, u32[]{:S(2)}, u32[]{:S(2)}) collective-permute-start(bf16[192,384]{1,0:T(8,128)(2,1)S(1)} %get-tuple-element.37), channel_id=1, source_target_pairs={{0,224},{2,226},{4,228},{6,230},{8,232},{10,234},{12,236},{14,238}... | collective-permute-start | bytes 442376 | tf_op jit(solution)/shard_map/ppermute | solution.py:331
  69.8 6.6 %collective-permute-start.16 = (bf16[192,384]{1,0:T(8,128)(2,1)S(1)}, bf16[192,384]{1,0:T(8,128)(2,1)S(1)}, u32[]{:S(2)}, u32[]{:S(2)}) collective-permute-start(bf16[192,384]{1,0:T(8,128)(2,1)S(1)} %broadcast_select_fusion.4), channel_id=1, source_target_pairs={{0,32},{2,34},{4,36},{6,38},{8,40},{10,42},{12,44},{14,46},{16,48}... | collective-permute-start | bytes 442376 | tf_op jit(solution)/shard_map/ppermute | solution.py:331
  74.6 9.0 %collective-permute-start.8 = (bf16[4,192,384]{2,1,0:T(8,128)(2,1)S(1)}, bf16[4,192,384]{2,1,0:T(8,128)(2,1)S(1)}, u32[]{:S(2)}, u32[]{:S(2)}) collective-permute-start(bf16[4,192,384]{2,1,0:T(8,128)(2,1)S(1)} %pad_maximum_fusion.refs_2_.refs_1_), channel_id=1, source_target_pairs={{0,1},{1,0},{2,3},{3,2},{4,5},{5,4},{6,7},{7,6},{8,9},{9,8},{10,11... | collective-permute-start | bytes 1769480 | tf_op jit(solution)/shard_map/ppermute | solution.py:275
  74.9 15.7 %collective-permute-start.9 = (bf16[3,256,384]{2,1,0:T(8,128)(2,1)S(1)}, bf16[3,256,384]{2,1,0:T(8,128)(2,1)S(1)}, u32[]{:S(2)}, u32[]{:S(2)}) collective-permute-start(bf16[3,256,384]{2,1,0:T(8,128)(2,1)S(1)} %copy-done.8), channel_id=1, source_target_pairs={{0,2},{2,0},{4,6},{6,4},{8,10},{10,8},{12,14},{14,12},{16,18},{18,... | collective-permute-start | bytes 1769480 | tf_op jit(solution)/shard_map/ppermute | solution.py:408
  76.5 7.1 %collective-permute-start.17 = (bf16[192,384]{1,0:T(8,128)(2,1)S(1)}, bf16[192,384]{1,0:T(8,128)(2,1)S(1)}, u32[]{:S(2)}, u32[]{:S(2)}) collective-permute-start(bf16[192,384]{1,0:T(8,128)(2,1)S(1)} %broadcast_select_fusion.2), channel_id=1, source_target_pairs={{0,96},{2,98},{4,100},{6,102},{8,104},{10,106},{12,108},{14,110},{... | collective-permute-start | bytes 442376 | tf_op jit(solution)/shard_map/ppermute | solution.py:331
  90.8 10.1 %collective-permute-start.18 = (bf16[192,384]{1,0:T(8,128)(2,1)S(1)}, bf16[192,384]{1,0:T(8,128)(2,1)S(1)}, u32[]{:S(2)}, u32[]{:S(2)}) collective-permute-start(bf16[192,384]{1,0:T(8,128)(2,1)S(1)} %broadcast_select_fusion), channel_id=1, source_target_pairs={{0,224},{2,226},{4,228},{6,230},{8,232},{10,234},{12,236},{14,238}... | collective-permute-start | bytes 442376 | tf_op jit(solution)/shard_map/ppermute | solution.py:331
  94.8 13.0 %collective-permute-start.10 = (bf16[2,256,384]{2,1,0:T(8,128)(2,1)S(1)}, bf16[2,256,384]{2,1,0:T(8,128)(2,1)S(1)}, u32[]{:S(2)}, u32[]{:S(2)}) collective-permute-start(bf16[2,256,384]{2,1,0:T(8,128)(2,1)S(1)} %slice.74), channel_id=1, source_target_pairs={{0,6},{2,4},{4,2},{6,0},{8,14},{10,12},{12,10},{14,8},{16,22},{18,... | collective-permute-start | bytes 1179656 | tf_op jit(solution)/shard_map/ppermute | solution.py:408
  102.3 20.9 %collective-permute-start.19 = (bf16[5,192,384]{2,1,0:T(8,128)(2,1)}, bf16[5,192,384]{2,1,0:T(8,128)(2,1)S(1)}, u32[]{:S(2)}, u32[]{:S(2)}) collective-permute-start(bf16[5,192,384]{2,1,0:T(8,128)(2,1)} %bitcast_dynamic-update-slice_fusion.refs_4_), channel_id=1, source_target_pairs={{0,1},{1,0},{2,3},{3,2},{4,5},{5,4},{6,7},{7,6},{8,9},{9,8},{10,11... | collective-permute-start | bytes 2211848 | tf_op jit(solution)/shard_map/ppermute | solution.py:275
  102.3 20.9 %all-to-all-start.1 = ((bf16[8,4,16,384]{3,2,1,0:T(8,128)(2,1)}), bf16[8,4,16,384]{3,2,1,0:T(8,128)(2,1)S(1)}, u32[]{:S(2)}, u32[]{:S(2)}) async-start(bf16[8,4,16,384]{3,2,1,0:T(8,128)(2,1)} %get-tuple-element.38), calls=%async_computation.1 | async-start | bytes 786432 | tf_op jit(solution)/shard_map/all_to_all | solution.py:339
  108.1 7.1 %collective-permute-start.11 = (bf16[1,256,384]{2,1,0:T(8,128)(2,1)S(1)}, bf16[1,256,384]{2,1,0:T(8,128)(2,1)S(1)}, u32[]{:S(2)}, u32[]{:S(2)}) collective-permute-start(bf16[1,256,384]{2,1,0:T(8,128)(2,1)S(1)} %slice.75), channel_id=1, source_target_pairs={{0,8},{2,10},{4,12},{6,14},{8,0},{10,2},{12,4},{14,6},{16,24},{18,... | collective-permute-start | bytes 589832 | tf_op jit(solution)/shard_map/ppermute | solution.py:408
  127.1 21.3 %all-to-all-start.2 = ((bf16[16,5,16,384]{3,2,1,0:T(8,128)(2,1)}), bf16[16,5,16,384]{3,2,1,0:T(8,128)(2,1)S(1)}, u32[]{:S(2)}, u32[]{:S(2)}) async-start(bf16[16,5,16,384]{3,2,1,0:T(8,128)(2,1)} %shard_map.109), calls=%async_computation.2 | async-start | bytes 1966080 | tf_op jit(solution)/shard_map/all_to_all | solution.py:339
  132.6 6.2 %collective-permute-start.20 = (bf16[3,192,384]{2,1,0:T(8,128)(2,1)S(1)}, bf16[3,192,384]{2,1,0:T(8,128)(2,1)S(1)}, u32[]{:S(2)}, u32[]{:S(2)}) collective-permute-start(bf16[3,192,384]{2,1,0:T(8,128)(2,1)S(1)} %pad_maximum_fusion.2.refs_5_), channel_id=1, source_target_pairs={{0,1},{1,0},{2,3},{3,2},{4,5},{5,4},{6,7},{7,6},{8,9},{9,8},{10,11... | collective-permute-start | bytes 1327112 | tf_op jit(solution)/shard_map/ppermute | solution.py:275
  (17 other events, 120.9 us)

commit v4 on v3

--- a/solution.py
+++ b/solution.py
@@ -28,6 +28,23 @@
     for copy in copies:
         copy.start()
     return copies
+
+
+def start_picked(flags, pairs, near, sems):
+    for index, (first, second) in enumerate(pairs):
+
+        @pl.when(flags[index] == 0)
+        def _():
+            pltpu.make_async_copy(first, near.at[index], sems.at[index]).start()
+
+        @pl.when(flags[index] != 0)
+        def _():
+            pltpu.make_async_copy(second, near.at[index], sems.at[index]).start()
+
+    return [
+        pltpu.make_async_copy(pair[0], near.at[index], sems.at[index])
+        for index, pair in enumerate(pairs)
+    ]
 
 
 def in_vmem(kernel, outs, scalars, arrays, scratch=()):
@@ -84,12 +101,10 @@
 
 def gain_kernel(core, inverse, link, gain, finish, full):
     own = inverse[...]
-    full[0] = dot(link[...], own).astype(BF16)
-    full[1] = dot_t(own, own).astype(BF16)
+    full[...] = dot(link[...], own).astype(BF16)
     rows = gain.shape[0]
-    first = pl.multiple_of(core[0] * rows, rows)
-    gain[...] = full[0, pl.ds(first, rows)]
-    finish[...] = full[1, pl.ds(first, rows)]
+    gain[...] = full[pl.ds(pl.multiple_of(core[0] * rows, rows), rows)]
+    finish[...] = dot_t(own, own).astype(BF16)
 
 
 def spread_out(pieces, index, value):
@@ -182,7 +197,13 @@
             above[piece, index] = value
 
 
-def top_kernel(core, place, arrived, fourth, mine, other, spread):
+def top_kernel(place, flags, *refs):
+    far, spread, (arrived, fourth, finish, sems) = refs[:-5], refs[-5], refs[-4:]
+    copies = start_all(far[:2], (arrived, fourth), sems)
+    pairs = list(zip(far[2::2], far[3::2]))
+    copies += start_picked(flags, pairs, finish, sems.at[pl.ds(2, len(pairs))])
+    for copy in copies:
+        copy.wait()
     planes = arrived.shape[0]
     for level in range(spread.shape[1]):
         if level == 0:
@@ -197,7 +218,7 @@
                     share = jnp.where(near, share, 0.0)
                 total = total + share
             total = total.astype(BF16)
-        value = -dot(total, whole(core, mine, other, level))
+        value = -dot(total, finish[level])
         value = value.astype(BF16)
         for piece in range(spread.shape[0]):
             spread[piece, level] = value
@@ -217,27 +238,29 @@
             couple[level, slot] = product.astype(BF16).T
 
 
-def backward_kernel(cols, sep_cols, core, own_level, *refs):
-    far, (solution, own), near, (pending, nodes, sems) = (
-        refs[:13],
-        refs[13:15],
-        refs[15:-3],
-        refs[-3:],
-    )
-    far = far[:7] + tuple(stack.at[0] for stack in far[7:10]) + far[10:]
-    copies = start_all(far, near, sems)
+def backward_kernel(cols, sep_cols, core, own_level, flags, *refs):
+    far, (solution, own), near, (finish, pending, nodes, sems) = (
+        refs[:17],
+        refs[17:19],
+        refs[19:-4],
+        refs[-4:],
+    )
+    direct = far[:5] + tuple(stack.at[0] for stack in far[5:8]) + far[8:11]
+    copies = start_all(direct[:8], near[:8], sems)
+    pairs = list(zip(far[11::2], far[12::2]))
+    copies += start_picked(flags, pairs, finish, sems.at[pl.ds(11, LOW)])
+    later = start_all(direct[8:], near[8:], sems.at[pl.ds(8, 3)])
     high, gains_high, gains_high_other, gains_low, gains_low_other = near[:5]
-    finish, finish_other = near[5:7]
-    low = near[7:10]
-    couple, start, chain = near[10:]
+    low = near[5:8]
+    couple, start, chain = near[8:]
     rows = start.shape[0]
     count = nodes.shape[0]
     split = gains_low.shape[0]
-    for copy in copies[:10]:
+    for copy in copies:
         copy.wait()
     for level in range(count - 1, -1, -1):
         if level < LOW:
-            node = -dot(low[level][...], whole(core, finish, finish_other, level))
+            node = -dot(low[level][...], finish[level])
         else:
             pieces = [high[piece, level - LOW] for piece in range(high.shape[0])]
             node = jnp.concatenate(pieces, axis=0).astype(F32)
@@ -250,7 +273,7 @@
         vector = node.astype(BF16)
         nodes[level] = vector
     own[...] = nodes[own_level[0]].T
-    for copy in copies[10:]:
+    for copy in later:
         copy.wait()
     pending[...] = start[...]
     for level in range(count - 1, -1, -1):
@@ -315,13 +338,12 @@
         return (2 << bit) - (1 << base)
 
     core = lax.axis_index("cols")[None]
-    half = shaped((sep_width // cores, sep_width), BF16)
     gain, finish = in_vmem(
         gain_kernel,
-        [half, half],
+        [shaped((sep_width // cores, sep_width), BF16), shaped((sep_width, sep_width), BF16)],
         [core],
         [sep_inverse[0], sep_link[0]],
-        [pltpu.VMEM((2, sep_width, sep_width), BF16)],
+        [pltpu.VMEM((sep_width, sep_width), BF16)],
     )
 
     flags = (device >> jnp.arange(count, dtype=jnp.int32)) & 1
@@ -380,11 +402,11 @@
         nonlocal finish
         finish = after(finish, gain)
         climb_gain(bit)
-        climb_finish(bit - 2)
+        climb_finish(bit - 1)
 
     climb_gain(0)
     gain = after(gain, solved_first)
-    climb_gain(1)
+    both(1)
     both(2)
     gains_low = with_other_core(flags[:LOW], gain_list)
     both(LOW)
@@ -407,31 +429,34 @@
         mask = step_mask(bit)
         return added(value, lax.ppermute(value, "blk", [(i, i ^ mask) for i in range(size)]))
 
-    low1 = swapped(after(low, arrived), 0)
+    low1 = swapped(low, 0)
+    low2 = swapped(low1[1:], 1)
+    low3 = swapped(low2[1:], 2)
     gain_list[-1] = after(gain_list[-1], arrived)
     gains_high = with_other_core(flags[LOW:bits], gain_list[LOW:])
     finish = after(finish, gain)
-    climb_finish(bits - 2)
+    climb_finish(bits - 1)
+    finish_list.append((finish, finish))
     fourth, above = in_vmem(
         plane_kernel,
         [shaped(piece, BF16), shaped((size // plane, bits - LOW, *piece), BF16)],
         [core],
-        [arrived, *gains_high],
-    )
-    finish = after(after(finish, above), low1)
-    climb_finish(bits - 1)
-    finish_list.append((finish, finish))
-    finish_high = with_other_core(flags[LOW:], finish_list[LOW:])
-    low2 = swapped(low1[1:], 1)
-    low3 = swapped(low2[1:], 2)
-    arrived = after(within(above, towers), low3)
-    (spread,) = in_vmem(
+        [after(arrived, (low3, finish)), *gains_high],
+    )
+    arrived = within(above, towers)
+    matrix = (sep_width, sep_width)
+    (spread,) = placed(
         top_kernel,
         [shaped((plane, count - LOW, *piece), BF16)],
-        [core, (device >> PLANE_BITS)[None]],
-        [arrived, fourth, *finish_high],
-    )
-    finish_low = with_other_core(flags[:LOW], finish_list[:LOW])
+        [(device >> PLANE_BITS)[None], flags[LOW:]],
+        [arrived, fourth, *[array for pair in finish_list[LOW:] for array in pair]],
+        [
+            pltpu.VMEM(arrived.shape, BF16),
+            pltpu.VMEM(piece, BF16),
+            pltpu.VMEM((count - LOW, *matrix), BF16),
+            pltpu.SemaphoreType.DMA((2 + count - LOW,)),
+        ],
+    )
     start, chain, couple = in_vmem(
         prepare_kernel,
         [
@@ -443,18 +468,19 @@
         [after(solved, spread), diag_inverse, lower_blocks, sep_blocks],
     )
     high = within(spread, groups)
-    far = [high, *gains_high, *gains_low, *finish_low, low1, low2, low3, couple, start, chain]
-    shapes = [array.shape[1:] if 7 <= i < 10 else array.shape for i, array in enumerate(far)]
+    far = [high, *gains_high, *gains_low, low1, low2, low3, couple, start, chain]
+    shapes = [array.shape[1:] if 5 <= i < 8 else array.shape for i, array in enumerate(far)]
     solution, own = placed(
         backward_kernel,
         [shaped(rhs.shape, BF16), shaped((sep_width, columns), BF16)],
-        [local_cols, sep_cols, core, own_level],
-        far,
+        [local_cols, sep_cols, core, own_level, flags],
+        far + [array for pair in finish_list[:LOW] for array in pair],
         [pltpu.VMEM(shape, array.dtype) for shape, array in zip(shapes, far)]
         + [
+            pltpu.VMEM((LOW, *matrix), BF16),
             pltpu.VMEM(rhs.shape, F32),
             pltpu.VMEM((count, columns, sep_width), BF16),
-            pltpu.SemaphoreType.DMA((len(far),)),
+            pltpu.SemaphoreType.DMA((len(far) + LOW,)),
         ],
     )
     return solution, own[None]

time: 160 us -> 157 us (0.981)
  waiting for transfers between devices: 52.4 us -> 45.9 us
  starting transfers between devices: 51.6 us -> 57.5 us
  other arithmetic: 5.07 us -> 2.38 us
    ppermute x14, waiting for transfers between devices: 25.9 us -> 19.8 us  [climb(): arrived = lax.ppermute(top, 'blk', [(i, i ^ mask) for i in range(size)])]
    unnamed x4 -> x0, other arithmetic: 2.79 us -> none
    ppermute x14, starting transfers between devices: 30.6 us -> 33.3 us  [climb(): arrived = lax.ppermute(top, 'blk', [(i, i ^ mask) for i in range(size)])]
    ppermute x3, starting transfers between devices: 2.94 us -> 5.32 us  [swapped(): lax.ppermute(value, 'blk', [(i, i ^ mask) for i in range(size)])]
    unnamed x35 -> x55, local copies, waits for them, and re-layouts: 4.29 us -> 4.17 us
  transfers between devices with their start and end apart: 24 -> 22, of which waited for: 12 -> 9; matrix products, arithmetic and copies ran while one was open for 4% -> 3% of each run, Pallas kernels for 15% -> 13%
where the time goes in v4:
time: 157 us
  starting transfers between devices  57.5 us (37%)
  waiting for transfers between devices  45.9 us (29%)
  Pallas kernels  39.3 us (25%)
  local copies, waits for them, and re-layouts  6.16 us (4%)
  between operations  5.55 us (4%)
  other arithmetic  2.38 us (2%)
    pallas_call x8, Pallas kernels, placed(): pl.pallas_call(kernel, out_shape=tuple(outs), in_specs=[smem] * len(scala...  39.3 us
    ppermute x14, starting transfers between devices, climb(): arrived = lax.ppermute(top, 'blk', [(i, i ^ mask) for i in range(size)])  33.3 us
    ppermute x14, waiting for transfers between devices, climb(): arrived = lax.ppermute(top, 'blk', [(i, i ^ mask) for i in range(size)])  19.8 us
    all_to_all x3, starting transfers between devices, within(): lax.all_to_all(value, 'blk', 0, 0, axis_index_groups=members, tiled=True)  18.7 us
    all_to_all x3, waiting for transfers between devices, within(): lax.all_to_all(value, 'blk', 0, 0, axis_index_groups=members, tiled=True)  16.5 us
    ppermute x3, waiting for transfers between devices, swapped(): lax.ppermute(value, 'blk', [(i, i ^ mask) for i in range(size)])  9.63 us
    ppermute x3, starting transfers between devices, swapped(): lax.ppermute(value, 'blk', [(i, i ^ mask) for i in range(size)])  5.32 us
    unnamed x55, local copies, waits for them, and re-layouts  4.17 us
  transfers between devices with their start and end apart: 22, of which 9 were waited for; matrix products, arithmetic and copies ran while one was open for 3% of the time, Pallas kernels for 13%

profile of v4, /device:TPU:8, one launch (start us, length us, event | category | flops | bytes accessed | tf_op | source)
XLA Modules:
  0.0 156.8 jit_solution(18007886642413702626)
XLA Ops:
  7.3 4.4 %shard_map.105.refs_5_ = bf16[8,128,256]{2,1,0:T(8,128)(2,1)} custom-call(s32[16,2]{1,0:T(8,128)} %copy.16.cols.refs_0_, bf16[16,128,128]{2,1,0:T(8,128)(2,1)} %refs_3_.1, bf16[16,2,128,128]{3,2,1,0:T(8,128)(2,1)} %refs_4_.1, bf16[16,128,256]{2,1,0:T(8,128)(2,1)} %refs_2_.2), custom_call_target="tpu_custom_call" | custom-call | flops 1000000000 | bytes 3145728 | tf_op jit(solution)/shard_map/pallas_call | solution.py:78
  16.4 6.4 %shard_map.106 = (bf16[16,128,256]{2,1,0:T(8,128)(2,1)}, f32[8,384,256]{2,1,0:T(8,128)}) custom-call(s32[16,2]{1,0:T(8,128)} %copy.16.cols.refs_0_, s32[8,2]{1,0:T(8,128)} %copy.17.sep_cols.refs_1_, s32[1]{0:T(128)} %bitcast.2.own_level, bf16[16,128,128]{2,1,0:T(8,128)(2,1)} %refs_3_.1, bf16[16,2,128,128]{3,2,1,0:T(8,128)(2,1)} %refs_4_.1, ...), custom_call_target="tpu_custom_call" | custom-call | flops 1000000000 | bytes 9109504 | tf_op jit(solution)/shard_map/pallas_call | solution.py:78
  25.0 3.1 %collective-permute-done.2 = bf16[192,384]{1,0:T(8,128)(2,1)S(1)} collective-permute-done((bf16[192,384]{1,0:T(8,128)(2,1)S(1)}, bf16[192,384]{1,0:T(8,128)(2,1)S(1)}, u32[]{:S(2)}, u32[]{:S(2)}) %collective-permute-start.2) | collective-permute-done | bytes 147488 | tf_op jit(solution)/shard_map/ppermute | solution.py:353
  28.1 2.8 %collective-permute-start.10 = (bf16[192,384]{1,0:T(8,128)(2,1)S(1)}, bf16[192,384]{1,0:T(8,128)(2,1)S(1)}, u32[]{:S(2)}, u32[]{:S(2)}) collective-permute-start(bf16[192,384]{1,0:T(8,128)(2,1)S(1)} %get-tuple-element.60), channel_id=1, source_target_pairs={{0,24},{2,26},{4,28},{6,30},{8,16},{10,18},{12,20},{14,22},{16,8},... | collective-permute-start | bytes 442376 | tf_op jit(solution)/shard_map/ppermute | solution.py:353
  35.4 4.1 %shard_map.107 = (bf16[3,256,384]{2,1,0:T(8,128)(2,1)}, bf16[16,5,16,384]{3,2,1,0:T(8,128)(2,1)}) custom-call(s32[1]{0:T(128)} %bitcast.1.refs_0_.core, f32[8,384,256]{2,1,0:T(8,128)} %get-tuple-element.30.refs_1_, bf16[3,192,384]{2,1,0:T(8,128)(2,1)} %copy-done.1, bf16[3,192,384]{2,1,0:T(8,128)(2,1)} %copy-done.11), custom_call_target="tpu_custom_call" | custom-call | flops 1000000000 | bytes 5603328 | tf_op jit(solution)/shard_map/pallas_call | solution.py:78
  41.5 2.8 %collective-permute-start.11 = (bf16[384,384]{1,0:T(8,128)(2,1)S(1)}, bf16[384,384]{1,0:T(8,128)(2,1)S(1)}, u32[]{:S(2)}, u32[]{:S(2)}) collective-permute-start(bf16[384,384]{1,0:T(8,128)(2,1)S(1)} %broadcast_select_fusion.2.refs_2_), channel_id=1, source_target_pairs={{0,24},{2,26},{4,28},{6,30},{8,16},{10,18},{12,20},{14,22},{16,8},... | collective-permute-start | bytes 884744 | tf_op jit(solution)/shard_map/ppermute | solution.py:353
  46.2 4.8 %all-to-all-start = ((bf16[16,5,16,384]{3,2,1,0:T(8,128)(2,1)}), bf16[16,5,16,384]{3,2,1,0:T(8,128)(2,1)}, u32[]{:S(2)}, u32[]{:S(2)}) async-start(bf16[16,5,16,384]{3,2,1,0:T(8,128)(2,1)} %get-tuple-element.32), calls=%async_computation | async-start | bytes 1966080 | tf_op jit(solution)/shard_map/all_to_all | solution.py:361
  51.4 2.9 %collective-permute-start.14 = (bf16[192,384]{1,0:T(8,128)(2,1)S(1)}, bf16[192,384]{1,0:T(8,128)(2,1)S(1)}, u32[]{:S(2)}, u32[]{:S(2)}) collective-permute-start(bf16[192,384]{1,0:T(8,128)(2,1)S(1)} %get-tuple-element.57), channel_id=1, source_target_pairs={{0,96},{2,98},{4,100},{6,102},{8,104},{10,106},{12,108},{14,110},{... | collective-permute-start | bytes 442376 | tf_op jit(solution)/shard_map/ppermute | solution.py:353
  55.4 3.7 %collective-permute-done.14 = bf16[192,384]{1,0:T(8,128)(2,1)S(1)} collective-permute-done((bf16[192,384]{1,0:T(8,128)(2,1)S(1)}, bf16[192,384]{1,0:T(8,128)(2,1)S(1)}, u32[]{:S(2)}, u32[]{:S(2)}) %collective-permute-start.14) | collective-permute-done | bytes 147488 | tf_op jit(solution)/shard_map/ppermute | solution.py:353
  59.2 5.0 %collective-permute-start.17 = (bf16[192,384]{1,0:T(8,128)(2,1)S(1)}, bf16[192,384]{1,0:T(8,128)(2,1)S(1)}, u32[]{:S(2)}, u32[]{:S(2)}) collective-permute-start(bf16[192,384]{1,0:T(8,128)(2,1)S(1)} %get-tuple-element.44), channel_id=1, source_target_pairs={{0,224},{2,226},{4,228},{6,230},{8,232},{10,234},{12,236},{14,238}... | collective-permute-start | bytes 442376 | tf_op jit(solution)/shard_map/ppermute | solution.py:353
  64.2 7.7 %collective-permute-done.4 = bf16[3,256,384]{2,1,0:T(8,128)(2,1)S(1)} collective-permute-done((bf16[3,256,384]{2,1,0:T(8,128)(2,1)S(1)}, bf16[3,256,384]{2,1,0:T(8,128)(2,1)S(1)}, u32[]{:S(2)}, u32[]{:S(2)}) %collective-permute-start.4) | collective-permute-done | bytes 589856 | tf_op jit(solution)/shard_map/ppermute | solution.py:430
  72.1 2.5 %collective-permute-start.5 = (bf16[2,256,384]{2,1,0:T(8,128)(2,1)S(1)}, bf16[2,256,384]{2,1,0:T(8,128)(2,1)S(1)}, u32[]{:S(2)}, u32[]{:S(2)}) collective-permute-start(bf16[2,256,384]{2,1,0:T(8,128)(2,1)S(1)} %slice.63), channel_id=1, source_target_pairs={{0,6},{2,4},{4,2},{6,0},{8,14},{10,12},{12,10},{14,8},{16,22},{18,... | collective-permute-start | bytes 1179656 | tf_op jit(solution)/shard_map/ppermute | solution.py:430
  74.7 4.1 %collective-permute-start.15 = (bf16[384,384]{1,0:T(8,128)(2,1)S(1)}, bf16[384,384]{1,0:T(8,128)(2,1)S(1)}, u32[]{:S(2)}, u32[]{:S(2)}) collective-permute-start(bf16[384,384]{1,0:T(8,128)(2,1)S(1)} %broadcast_select_fusion.4.refs_6_), channel_id=1, source_target_pairs={{0,96},{2,98},{4,100},{6,102},{8,104},{10,106},{12,108},{14,110},{... | collective-permute-start | bytes 884744 | tf_op jit(solution)/shard_map/ppermute | solution.py:353
  81.0 2.4 %collective-permute-start.6 = (bf16[1,256,384]{2,1,0:T(8,128)(2,1)S(1)}, bf16[1,256,384]{2,1,0:T(8,128)(2,1)S(1)}, u32[]{:S(2)}, u32[]{:S(2)}) collective-permute-start(bf16[1,256,384]{2,1,0:T(8,128)(2,1)S(1)} %slice.64), channel_id=1, source_target_pairs={{0,8},{2,10},{4,12},{6,14},{8,0},{10,2},{12,4},{14,6},{16,24},{18,... | collective-permute-start | bytes 589832 | tf_op jit(solution)/shard_map/ppermute | solution.py:430
  83.5 5.4 %collective-permute-start.16 = (bf16[384,384]{1,0:T(8,128)(2,1)S(1)}, bf16[384,384]{1,0:T(8,128)(2,1)S(1)}, u32[]{:S(2)}, u32[]{:S(2)}) collective-permute-start(bf16[384,384]{1,0:T(8,128)(2,1)S(1)} %broadcast_select_fusion.5.refs_8_), channel_id=1, source_target_pairs={{0,224},{2,226},{4,228},{6,230},{8,232},{10,234},{12,236},{14,238}... | collective-permute-start | bytes 884744 | tf_op jit(solution)/shard_map/ppermute | solution.py:353
  89.7 10.3 %collective-permute-done.16.refs_9_ = bf16[384,384]{1,0:T(8,128)(2,1)S(1)} collective-permute-done((bf16[384,384]{1,0:T(8,128)(2,1)S(1)}, bf16[384,384]{1,0:T(8,128)(2,1)S(1)}, u32[]{:S(2)}, u32[]{:S(2)}) %collective-permute-start.16) | collective-permute-done | bytes 294944 | tf_op jit(solution)/shard_map/ppermute | solution.py:353
  101.7 3.0 %shard_map.108 = (bf16[16,384]{1,0:T(8,128)(2,1)}, bf16[8,4,16,384]{3,2,1,0:T(8,128)(2,1)}) custom-call(s32[1]{0:T(128)} %bitcast.1.refs_0_.core, bf16[16,5,16,384]{3,2,1,0:T(8,128)(2,1)} %all-to-all-done.refs_1_, bf16[4,192,384]{2,1,0:T(8,128)(2,1)} %copy-done.10, bf16[4,192,384]{2,1,0:T(8,128)(2,1)} %copy-done.21), custom_call_target="tpu_custom_call" | custom-call | flops 1000000000 | bytes 2568192 | tf_op jit(solution)/shard_map/pallas_call | solution.py:78
  104.7 5.9 %all-to-all-start.1 = ((bf16[8,4,16,384]{3,2,1,0:T(8,128)(2,1)}), bf16[8,4,16,384]{3,2,1,0:T(8,128)(2,1)S(1)}, u32[]{:S(2)}, u32[]{:S(2)}) async-start(bf16[8,4,16,384]{3,2,1,0:T(8,128)(2,1)} %get-tuple-element.45), calls=%async_computation.1 | async-start | bytes 786432 | tf_op jit(solution)/shard_map/all_to_all | solution.py:361
  111.2 11.3 %all-to-all-done.1.refs_0_ = bf16[8,4,16,384]{3,2,1,0:T(8,128)(2,1)S(1)} async-done(((bf16[8,4,16,384]{3,2,1,0:T(8,128)(2,1)}), bf16[8,4,16,384]{3,2,1,0:T(8,128)(2,1)S(1)}, u32[]{:S(2)}, u32[]{:S(2)}) %all-to-all-start.1) | async-done | bytes 393248 | tf_op jit(solution)/shard_map/all_to_all | solution.py:361
  123.4 3.5 %shard_map.109 = bf16[16,5,16,384]{3,2,1,0:T(8,128)(2,1)} custom-call(s32[1]{0:T(128)} %bitcast.3.place, s32[5]{0:T(128)} %slice.53.flags, bf16[8,4,16,384]{3,2,1,0:T(8,128)(2,1)} %copy-done.12, bf16[16,384]{1,0:T(8,128)(2,1)} %get-tuple-element.46.refs_1_, bf16[384,384]{1,0:T(8,128)(2,1)} %copy-done.6, bf16[384,384]{1,0:T(8,128)(2,1)} %copy-done.17, ...), custom_call_target="tpu_custom_call" | custom-call | flops 1000000000 | bytes 4337664 | tf_op jit(solution)/shard_map/pallas_call | solution.py:78
  126.8 8.1 %all-to-all-start.2 = ((bf16[16,5,16,384]{3,2,1,0:T(8,128)(2,1)}), bf16[16,5,16,384]{3,2,1,0:T(8,128)(2,1)S(1)}, u32[]{:S(2)}, u32[]{:S(2)}) async-start(bf16[16,5,16,384]{3,2,1,0:T(8,128)(2,1)} %shard_map.109), calls=%async_computation.2 | async-start | bytes 1966080 | tf_op jit(solution)/shard_map/all_to_all | solution.py:361
  134.9 6.0 %shard_map.110 = (f32[16,128,256]{2,1,0:T(8,128)}, bf16[16,2,128,128]{3,2,1,0:T(8,128)(2,1)}, bf16[8,2,128,384]{3,2,1,0:T(8,128)(2,1)}) custom-call(s32[16,2]{1,0:T(8,128)} %copy.16.cols.refs_0_, s32[8,2]{1,0:T(8,128)} %copy.17.sep_cols.refs_1_, bf16[16,128,256]{2,1,0:T(8,128)(2,1)} %get-tuple-element.48.refs_2_, bf16[16,128,128]{2,1,0:T(8,128)(2,1)} %refs_3_.1, ...), custom_call_target="tpu_custom_call" | custom-call | flops 1000000000 | bytes 8912896 | tf_op jit(solution)/shard_map/pallas_call | solution.py:78
  141.0 5.1 %all-to-all-done.2.refs_0_ = bf16[16,5,16,384]{3,2,1,0:T(8,128)(2,1)S(1)} async-done(((bf16[16,5,16,384]{3,2,1,0:T(8,128)(2,1)}), bf16[16,5,16,384]{3,2,1,0:T(8,128)(2,1)S(1)}, u32[]{:S(2)}, u32[]{:S(2)}) %all-to-all-start.2) | async-done | bytes 983072 | tf_op jit(solution)/shard_map/all_to_all | solution.py:361
  147.1 9.6 %shard_map.111 = (bf16[16,128,256]{2,1,0:T(8,128)(2,1)}, bf16[384,256]{1,0:T(8,128)(2,1)}) custom-call(s32[16,2]{1,0:T(8,128)} %copy.16.cols.refs_0_, s32[8,2]{1,0:T(8,128)} %copy.17.sep_cols.refs_1_, s32[1]{0:T(128)} %bitcast.1.refs_0_.core, s32[1]{0:T(128)} %bitcast.2.own_level, s32[8]{0:T(128)} %copy-done.24, bf16[16,5,16,384]{3,2,1,0:T(8,128)(2,1)} %copy-done.2, ...), custom_call_target="tpu_custom_call" | custom-call | flops 1000000000 | bytes 11960320 | tf_op jit(solution)/shard_map/pallas_call | solution.py:78
  (108 shorter events, 26.3 us)
Async XLA Ops:
  3.0 8.7 %collective-permute-start = (bf16[192,384]{1,0:T(8,128)(2,1)}, bf16[192,384]{1,0:T(8,128)(2,1)S(1)}, u32[]{:S(2)}, u32[]{:S(2)}) collective-permute-start(bf16[192,384]{1,0:T(8,128)(2,1)} %get-tuple-element.28), channel_id=1, source_target_pairs={{0,2},{2,0},{4,6},{6,4},{8,10},{10,8},{12,14},{14,12},{16,18},{18,... | collective-permute-start | bytes 442376 | tf_op jit(solution)/shard_map/ppermute | solution.py:353
  5.2 105.4 %copy-start.24 = (s32[8]{0:T(128)}, s32[8]{0:T(128)S(1)}, u32[]{:S(2)}) copy-start(s32[8]{0:T(128)S(1)} %shift-right-arithmetic_and_fusion.flags) | copy-start | bytes 100
  11.7 11.0 %collective-permute-start.1 = (bf16[192,384]{1,0:T(8,128)(2,1)S(1)}, bf16[192,384]{1,0:T(8,128)(2,1)S(1)}, u32[]{:S(2)}, u32[]{:S(2)}) collective-permute-start(bf16[192,384]{1,0:T(8,128)(2,1)S(1)} %get-tuple-element.31), channel_id=1, source_target_pairs={{0,6},{2,4},{4,2},{6,0},{8,14},{10,12},{12,10},{14,8},{16,22},{18,... | collective-permute-start | bytes 442376 | tf_op jit(solution)/shard_map/ppermute | solution.py:353
  15.0 9.4 %collective-permute-start.7 = (bf16[384,384]{1,0:T(8,128)(2,1)S(1)}, bf16[384,384]{1,0:T(8,128)(2,1)S(1)}, u32[]{:S(2)}, u32[]{:S(2)}) collective-permute-start(bf16[384,384]{1,0:T(8,128)(2,1)S(1)} %copy-done.13), channel_id=1, source_target_pairs={{0,2},{2,0},{4,6},{6,4},{8,10},{10,8},{12,14},{14,12},{16,18},{18,... | collective-permute-start | bytes 884744 | tf_op jit(solution)/shard_map/ppermute | solution.py:353
  22.8 5.2 %collective-permute-start.2 = (bf16[192,384]{1,0:T(8,128)(2,1)S(1)}, bf16[192,384]{1,0:T(8,128)(2,1)S(1)}, u32[]{:S(2)}, u32[]{:S(2)}) collective-permute-start(bf16[192,384]{1,0:T(8,128)(2,1)S(1)} %get-tuple-element.65), channel_id=1, source_target_pairs={{0,8},{2,10},{4,12},{6,14},{8,0},{10,2},{12,4},{14,6},{16,24},{18,... | collective-permute-start | bytes 442376 | tf_op jit(solution)/shard_map/ppermute | solution.py:353
  24.4 7.7 %collective-permute-start.8 = (bf16[384,384]{1,0:T(8,128)(2,1)S(1)}, bf16[384,384]{1,0:T(8,128)(2,1)S(1)}, u32[]{:S(2)}, u32[]{:S(2)}) collective-permute-start(bf16[384,384]{1,0:T(8,128)(2,1)S(1)} %broadcast_select_fusion.refs_13_), channel_id=1, source_target_pairs={{0,6},{2,4},{4,2},{6,0},{8,14},{10,12},{12,10},{14,8},{16,22},{18,... | collective-permute-start | bytes 884744 | tf_op jit(solution)/shard_map/ppermute | solution.py:353
  28.1 6.4 %collective-permute-start.10 = (bf16[192,384]{1,0:T(8,128)(2,1)S(1)}, bf16[192,384]{1,0:T(8,128)(2,1)S(1)}, u32[]{:S(2)}, u32[]{:S(2)}) collective-permute-start(bf16[192,384]{1,0:T(8,128)(2,1)S(1)} %get-tuple-element.60), channel_id=1, source_target_pairs={{0,24},{2,26},{4,28},{6,30},{8,16},{10,18},{12,20},{14,22},{16,8},... | collective-permute-start | bytes 442376 | tf_op jit(solution)/shard_map/ppermute | solution.py:353
  31.0 3.6 %collective-permute-start.3 = (bf16[3,192,384]{2,1,0:T(8,128)(2,1)S(1)}, bf16[3,192,384]{2,1,0:T(8,128)(2,1)S(1)}, u32[]{:S(2)}, u32[]{:S(2)}) collective-permute-start(bf16[3,192,384]{2,1,0:T(8,128)(2,1)S(1)} %pad_maximum_fusion.1.refs_2_.refs_3_), channel_id=1, source_target_pairs={{0,1},{1,0},{2,3},{3,2},{4,5},{5,4},{6,7},{7,6},{8,9},{9,8},{10,11... | collective-permute-start | bytes 1327112 | tf_op jit(solution)/shard_map/ppermute | solution.py:298
  32.2 9.3 %collective-permute-start.9 = (bf16[384,384]{1,0:T(8,128)(2,1)S(1)}, bf16[384,384]{1,0:T(8,128)(2,1)S(1)}, u32[]{:S(2)}, u32[]{:S(2)}) collective-permute-start(bf16[384,384]{1,0:T(8,128)(2,1)S(1)} %broadcast_select_fusion.1.refs_15_), channel_id=1, source_target_pairs={{0,8},{2,10},{4,12},{6,14},{8,0},{10,2},{12,4},{14,6},{16,24},{18,... | collective-permute-start | bytes 884744 | tf_op jit(solution)/shard_map/ppermute | solution.py:353
  39.5 11.8 %collective-permute-start.12 = (bf16[192,384]{1,0:T(8,128)(2,1)S(1)}, bf16[192,384]{1,0:T(8,128)(2,1)S(1)}, u32[]{:S(2)}, u32[]{:S(2)}) collective-permute-start(bf16[192,384]{1,0:T(8,128)(2,1)S(1)} %get-tuple-element.38), channel_id=1, source_target_pairs={{0,32},{2,34},{4,36},{6,38},{8,40},{10,42},{12,44},{14,46},{16,48}... | collective-permute-start | bytes 442376 | tf_op jit(solution)/shard_map/ppermute | solution.py:353
  41.5 12.7 %collective-permute-start.11 = (bf16[384,384]{1,0:T(8,128)(2,1)S(1)}, bf16[384,384]{1,0:T(8,128)(2,1)S(1)}, u32[]{:S(2)}, u32[]{:S(2)}) collective-permute-start(bf16[384,384]{1,0:T(8,128)(2,1)S(1)} %broadcast_select_fusion.2.refs_2_), channel_id=1, source_target_pairs={{0,24},{2,26},{4,28},{6,30},{8,16},{10,18},{12,20},{14,22},{16,8},... | collective-permute-start | bytes 884744 | tf_op jit(solution)/shard_map/ppermute | solution.py:353
  46.2 32.5 %all-to-all-start = ((bf16[16,5,16,384]{3,2,1,0:T(8,128)(2,1)}), bf16[16,5,16,384]{3,2,1,0:T(8,128)(2,1)}, u32[]{:S(2)}, u32[]{:S(2)}) async-start(bf16[16,5,16,384]{3,2,1,0:T(8,128)(2,1)} %get-tuple-element.32), calls=%async_computation | async-start | bytes 1966080 | tf_op jit(solution)/shard_map/all_to_all | solution.py:361
  51.0 20.9 %collective-permute-start.4 = (bf16[3,256,384]{2,1,0:T(8,128)(2,1)S(1)}, bf16[3,256,384]{2,1,0:T(8,128)(2,1)S(1)}, u32[]{:S(2)}, u32[]{:S(2)}) collective-permute-start(bf16[3,256,384]{2,1,0:T(8,128)(2,1)S(1)} %copy-done.22), channel_id=1, source_target_pairs={{0,2},{2,0},{4,6},{6,4},{8,10},{10,8},{12,14},{14,12},{16,18},{18,... | collective-permute-start | bytes 1769480 | tf_op jit(solution)/shard_map/ppermute | solution.py:430
  51.4 7.8 %collective-permute-start.14 = (bf16[192,384]{1,0:T(8,128)(2,1)S(1)}, bf16[192,384]{1,0:T(8,128)(2,1)S(1)}, u32[]{:S(2)}, u32[]{:S(2)}) collective-permute-start(bf16[192,384]{1,0:T(8,128)(2,1)S(1)} %get-tuple-element.57), channel_id=1, source_target_pairs={{0,96},{2,98},{4,100},{6,102},{8,104},{10,106},{12,108},{14,110},{... | collective-permute-start | bytes 442376 | tf_op jit(solution)/shard_map/ppermute | solution.py:353
  54.4 20.3 %collective-permute-start.13 = (bf16[384,384]{1,0:T(8,128)(2,1)S(1)}, bf16[384,384]{1,0:T(8,128)(2,1)S(1)}, u32[]{:S(2)}, u32[]{:S(2)}) collective-permute-start(bf16[384,384]{1,0:T(8,128)(2,1)S(1)} %broadcast_select_fusion.3.refs_4_), channel_id=1, source_target_pairs={{0,32},{2,34},{4,36},{6,38},{8,40},{10,42},{12,44},{14,46},{16,48}... | collective-permute-start | bytes 884744 | tf_op jit(solution)/shard_map/ppermute | solution.py:353
  59.2 19.6 %collective-permute-start.17 = (bf16[192,384]{1,0:T(8,128)(2,1)S(1)}, bf16[192,384]{1,0:T(8,128)(2,1)S(1)}, u32[]{:S(2)}, u32[]{:S(2)}) collective-permute-start(bf16[192,384]{1,0:T(8,128)(2,1)S(1)} %get-tuple-element.44), channel_id=1, source_target_pairs={{0,224},{2,226},{4,228},{6,230},{8,232},{10,234},{12,236},{14,238}... | collective-permute-start | bytes 442376 | tf_op jit(solution)/shard_map/ppermute | solution.py:353
  72.1 8.8 %collective-permute-start.5 = (bf16[2,256,384]{2,1,0:T(8,128)(2,1)S(1)}, bf16[2,256,384]{2,1,0:T(8,128)(2,1)S(1)}, u32[]{:S(2)}, u32[]{:S(2)}) collective-permute-start(bf16[2,256,384]{2,1,0:T(8,128)(2,1)S(1)} %slice.63), channel_id=1, source_target_pairs={{0,6},{2,4},{4,2},{6,0},{8,14},{10,12},{12,10},{14,8},{16,22},{18,... | collective-permute-start | bytes 1179656 | tf_op jit(solution)/shard_map/ppermute | solution.py:430
  74.7 8.8 %collective-permute-start.15 = (bf16[384,384]{1,0:T(8,128)(2,1)S(1)}, bf16[384,384]{1,0:T(8,128)(2,1)S(1)}, u32[]{:S(2)}, u32[]{:S(2)}) collective-permute-start(bf16[384,384]{1,0:T(8,128)(2,1)S(1)} %broadcast_select_fusion.4.refs_6_), channel_id=1, source_target_pairs={{0,96},{2,98},{4,100},{6,102},{8,104},{10,106},{12,108},{14,110},{... | collective-permute-start | bytes 884744 | tf_op jit(solution)/shard_map/ppermute | solution.py:353
  78.9 21.9 %collective-permute-start.18 = (bf16[4,192,384]{2,1,0:T(8,128)(2,1)S(1)}, bf16[4,192,384]{2,1,0:T(8,128)(2,1)S(1)}, u32[]{:S(2)}, u32[]{:S(2)}) collective-permute-start(bf16[4,192,384]{2,1,0:T(8,128)(2,1)S(1)} %pad_maximum_fusion.refs_2_.refs_1_), channel_id=1, source_target_pairs={{0,1},{1,0},{2,3},{3,2},{4,5},{5,4},{6,7},{7,6},{8,9},{9,8},{10,11... | collective-permute-start | bytes 1769480 | tf_op jit(solution)/shard_map/ppermute | solution.py:298
  81.0 23.7 %copy-start.3 = (bf16[2,256,384]{2,1,0:T(8,128)(2,1)}, bf16[2,256,384]{2,1,0:T(8,128)(2,1)S(1)}, u32[]{:S(2)}) copy-start(bf16[2,256,384]{2,1,0:T(8,128)(2,1)S(1)} %add_convert_fusion.1.refs_6_) | copy-start | bytes 1179652
  81.0 8.0 %collective-permute-start.6 = (bf16[1,256,384]{2,1,0:T(8,128)(2,1)S(1)}, bf16[1,256,384]{2,1,0:T(8,128)(2,1)S(1)}, u32[]{:S(2)}, u32[]{:S(2)}) collective-permute-start(bf16[1,256,384]{2,1,0:T(8,128)(2,1)S(1)} %slice.64), channel_id=1, source_target_pairs={{0,8},{2,10},{4,12},{6,14},{8,0},{10,2},{12,4},{14,6},{16,24},{18,... | collective-permute-start | bytes 589832 | tf_op jit(solution)/shard_map/ppermute | solution.py:430
  83.5 16.4 %collective-permute-start.16 = (bf16[384,384]{1,0:T(8,128)(2,1)S(1)}, bf16[384,384]{1,0:T(8,128)(2,1)S(1)}, u32[]{:S(2)}, u32[]{:S(2)}) collective-permute-start(bf16[384,384]{1,0:T(8,128)(2,1)S(1)} %broadcast_select_fusion.5.refs_8_), channel_id=1, source_target_pairs={{0,224},{2,226},{4,228},{6,230},{8,232},{10,234},{12,236},{14,238}... | collective-permute-start | bytes 884744 | tf_op jit(solution)/shard_map/ppermute | solution.py:353
  104.7 17.8 %all-to-all-start.1 = ((bf16[8,4,16,384]{3,2,1,0:T(8,128)(2,1)}), bf16[8,4,16,384]{3,2,1,0:T(8,128)(2,1)S(1)}, u32[]{:S(2)}, u32[]{:S(2)}) async-start(bf16[8,4,16,384]{3,2,1,0:T(8,128)(2,1)} %get-tuple-element.45), calls=%async_computation.1 | async-start | bytes 786432 | tf_op jit(solution)/shard_map/all_to_all | solution.py:361
  126.8 19.3 %all-to-all-start.2 = ((bf16[16,5,16,384]{3,2,1,0:T(8,128)(2,1)}), bf16[16,5,16,384]{3,2,1,0:T(8,128)(2,1)S(1)}, u32[]{:S(2)}, u32[]{:S(2)}) async-start(bf16[16,5,16,384]{3,2,1,0:T(8,128)(2,1)} %shard_map.109), calls=%async_computation.2 | async-start | bytes 1966080 | tf_op jit(solution)/shard_map/all_to_all | solution.py:361
  (25 other events, 236.3 us)

commit v5 on v3

--- a/solution.py
+++ b/solution.py
@@ -376,29 +376,29 @@
         pair, finish = climb(finish, bit)
         finish_list.append(pair)
 
-    def both(bit):
-        nonlocal finish
+    def both(bit, event=None):
+        nonlocal gain, finish
         finish = after(finish, gain)
+        if event is not None:
+            gain, finish = after(gain, event), after(finish, event)
         climb_gain(bit)
-        climb_finish(bit - 2)
+        climb_finish(bit - 1)
 
     climb_gain(0)
-    gain = after(gain, solved_first)
-    climb_gain(1)
-    both(2)
+    both(1, solved_first)
+    for bit in range(2, LOW):
+        both(bit)
     gains_low = with_other_core(flags[:LOW], gain_list)
     both(LOW)
+    both(LOW + 1)
     low, shares = in_vmem(
         path_kernel,
         [shaped((LOW, columns, sep_width), BF16), shaped((plane, count - LOW, *piece), BF16)],
         [core],
         [partial, *gains_low],
     )
+    both(LOW + 2, shares)
     arrived = within(shares, groups)
-    gain = after(gain, shares)
-    both(LOW + 1)
-    both(LOW + 2)
-    both(LOW + 3)
 
     def added(mine, other):
         return (mine.astype(F32) + other.astype(F32)).astype(BF16)
@@ -408,19 +408,16 @@
         return added(value, lax.ppermute(value, "blk", [(i, i ^ mask) for i in range(size)]))
 
     low1 = swapped(after(low, arrived), 0)
-    gain_list[-1] = after(gain_list[-1], arrived)
+    both(LOW + 3, arrived)
     gains_high = with_other_core(flags[LOW:bits], gain_list[LOW:])
-    finish = after(finish, gain)
-    climb_finish(bits - 2)
+    climb_finish(bits - 1)
+    finish_list.append((finish, finish))
     fourth, above = in_vmem(
         plane_kernel,
         [shaped(piece, BF16), shaped((size // plane, bits - LOW, *piece), BF16)],
         [core],
-        [arrived, *gains_high],
-    )
-    finish = after(after(finish, above), low1)
-    climb_finish(bits - 1)
-    finish_list.append((finish, finish))
+        [after(arrived, low1), *gains_high],
+    )
     finish_high = with_other_core(flags[LOW:], finish_list[LOW:])
     low2 = swapped(low1[1:], 1)
     low3 = swapped(low2[1:], 2)

time: 160 us -> 152 us (0.950)
  waiting for transfers between devices: 52.4 us -> 43.4 us
    ppermute x14, waiting for transfers between devices: 25.9 us -> 15.9 us  [climb(): arrived = lax.ppermute(top, 'blk', [(i, i ^ mask) for i in range(size)])]
  transfers between devices with their start and end apart: 24 -> 24, of which waited for: 12 -> 12; matrix products, arithmetic and copies ran while one was open for 4% -> 5% of each run, Pallas kernels for 15% -> 16%
where the time goes in v5:
time: 152 us; the launch traced here: 151 us
  starting transfers between devices  51.5 us (34%)
  waiting for transfers between devices  43.4 us (29%)
  Pallas kernels  38.6 us (25%)
  local copies, waits for them, and re-layouts  6.6 us (4%)
  between operations  5.71 us (4%)
  other arithmetic  5.17 us (3%)
    pallas_call x8, Pallas kernels, placed(): pl.pallas_call(kernel, out_shape=tuple(outs), in_specs=[smem] * len(scala...  38.6 us
    ppermute x14, starting transfers between devices, climb(): arrived = lax.ppermute(top, 'blk', [(i, i ^ mask) for i in range(size)])  29.8 us
    all_to_all x3, waiting for transfers between devices, within(): lax.all_to_all(value, 'blk', 0, 0, axis_index_groups=members, tiled=True)  17.8 us
    all_to_all x3, starting transfers between devices, within(): lax.all_to_all(value, 'blk', 0, 0, axis_index_groups=members, tiled=True)  17.7 us
    ppermute x14, waiting for transfers between devices, climb(): arrived = lax.ppermute(top, 'blk', [(i, i ^ mask) for i in range(size)])  15.9 us
    ppermute x3, waiting for transfers between devices, swapped(): lax.ppermute(value, 'blk', [(i, i ^ mask) for i in range(size)])  9.57 us
    unnamed x35, local copies, waits for them, and re-layouts  4.36 us
    ppermute x3, starting transfers between devices, swapped(): lax.ppermute(value, 'blk', [(i, i ^ mask) for i in range(size)])  3.78 us
  transfers between devices with their start and end apart: 24, of which 12 were waited for; matrix products, arithmetic and copies ran while one was open for 5% of the time, Pallas kernels for 16%

profile of v5, /device:TPU:8, one launch (start us, length us, event | category | flops | bytes accessed | tf_op | source)
XLA Modules:
  0.0 151.0 jit_solution(15979486226653505732)
XLA Ops:
  0.6 2.3 %shard_map.104 = (bf16[192,384]{1,0:T(8,128)(2,1)}, bf16[192,384]{1,0:T(8,128)(2,1)}) custom-call(s32[1]{0:T(128)} %bitcast.1.refs_0_.core, bf16[384,384]{1,0:T(8,128)(2,1)} %bitcast.50, bf16[384,384]{1,0:T(8,128)(2,1)} %bitcast.51), custom_call_target="tpu_custom_call" | custom-call | flops 1000000000 | bytes 884736 | tf_op jit(solution)/shard_map/pallas_call | solution.py:61
  3.0 2.3 %collective-permute-start = (bf16[192,384]{1,0:T(8,128)(2,1)}, bf16[192,384]{1,0:T(8,128)(2,1)S(1)}, u32[]{:S(2)}, u32[]{:S(2)}) collective-permute-start(bf16[192,384]{1,0:T(8,128)(2,1)} %get-tuple-element.32), channel_id=1, source_target_pairs={{0,2},{2,0},{4,6},{6,4},{8,10},{10,8},{12,14},{14,12},{16,18},{18,... | collective-permute-start | bytes 442376 | tf_op jit(solution)/shard_map/ppermute | solution.py:331
  7.2 4.4 %shard_map.105.refs_5_ = bf16[8,128,256]{2,1,0:T(8,128)(2,1)} custom-call(s32[16,2]{1,0:T(8,128)} %copy.16.cols.refs_0_, bf16[16,128,128]{2,1,0:T(8,128)(2,1)} %refs_3_.1, bf16[16,2,128,128]{3,2,1,0:T(8,128)(2,1)} %refs_4_.1, bf16[16,128,256]{2,1,0:T(8,128)(2,1)} %refs_2_.2), custom_call_target="tpu_custom_call" | custom-call | flops 1000000000 | bytes 3145728 | tf_op jit(solution)/shard_map/pallas_call | solution.py:61
  13.9 3.0 %collective-permute-done.12 = bf16[192,384]{1,0:T(8,128)(2,1)S(1)} collective-permute-done((bf16[192,384]{1,0:T(8,128)(2,1)S(1)}, bf16[192,384]{1,0:T(8,128)(2,1)S(1)}, u32[]{:S(2)}, u32[]{:S(2)}) %collective-permute-start.12) | collective-permute-done | bytes 147488 | tf_op jit(solution)/shard_map/ppermute | solution.py:331
  30.4 3.4 %collective-permute-done.5 = bf16[192,384]{1,0:T(8,128)(2,1)S(1)} collective-permute-done((bf16[192,384]{1,0:T(8,128)(2,1)S(1)}, bf16[192,384]{1,0:T(8,128)(2,1)S(1)}, u32[]{:S(2)}, u32[]{:S(2)}) %collective-permute-start.5) | collective-permute-done | bytes 147488 | tf_op jit(solution)/shard_map/ppermute | solution.py:331
  33.8 2.4 %collective-permute-start.15 = (bf16[192,384]{1,0:T(8,128)(2,1)S(1)}, bf16[192,384]{1,0:T(8,128)(2,1)S(1)}, u32[]{:S(2)}, u32[]{:S(2)}) collective-permute-start(bf16[192,384]{1,0:T(8,128)(2,1)S(1)} %get-tuple-element.50), channel_id=1, source_target_pairs={{0,24},{2,26},{4,28},{6,30},{8,16},{10,18},{12,20},{14,22},{16,8},... | collective-permute-start | bytes 442376 | tf_op jit(solution)/shard_map/ppermute | solution.py:331
  38.9 6.4 %shard_map.106 = (bf16[16,128,256]{2,1,0:T(8,128)(2,1)}, f32[8,384,256]{2,1,0:T(8,128)}) custom-call(s32[16,2]{1,0:T(8,128)} %copy.16.cols.refs_0_, s32[8,2]{1,0:T(8,128)} %copy.17.sep_cols.refs_1_, s32[1]{0:T(128)} %bitcast.2.own_level, bf16[16,128,128]{2,1,0:T(8,128)(2,1)} %refs_3_.1, bf16[16,2,128,128]{3,2,1,0:T(8,128)(2,1)} %refs_4_.1, ...), custom_call_target="tpu_custom_call" | custom-call | flops 1000000000 | bytes 9109504 | tf_op jit(solution)/shard_map/pallas_call | solution.py:61
  48.1 4.0 %shard_map.107 = (bf16[3,256,384]{2,1,0:T(8,128)(2,1)}, bf16[16,5,16,384]{3,2,1,0:T(8,128)(2,1)}) custom-call(s32[1]{0:T(128)} %bitcast.1.refs_0_.core, f32[8,384,256]{2,1,0:T(8,128)} %get-tuple-element.34.refs_1_, bf16[3,192,384]{2,1,0:T(8,128)(2,1)} %copy-done.1, bf16[3,192,384]{2,1,0:T(8,128)(2,1)} %copy-done.5), custom_call_target="tpu_custom_call" | custom-call | flops 1000000000 | bytes 5603328 | tf_op jit(solution)/shard_map/pallas_call | solution.py:61
  52.2 7.2 %all-to-all-start = ((bf16[16,5,16,384]{3,2,1,0:T(8,128)(2,1)}), bf16[16,5,16,384]{3,2,1,0:T(8,128)(2,1)S(1)}, u32[]{:S(2)}, u32[]{:S(2)}) async-start(bf16[16,5,16,384]{3,2,1,0:T(8,128)(2,1)} %get-tuple-element.36), calls=%async_computation | async-start | bytes 1966080 | tf_op jit(solution)/shard_map/all_to_all | solution.py:339
  60.8 4.1 %collective-permute-start.7 = (bf16[192,384]{1,0:T(8,128)(2,1)S(1)}, bf16[192,384]{1,0:T(8,128)(2,1)S(1)}, u32[]{:S(2)}, u32[]{:S(2)}) collective-permute-start(bf16[192,384]{1,0:T(8,128)(2,1)S(1)} %get-tuple-element.40), channel_id=1, source_target_pairs={{0,96},{2,98},{4,100},{6,102},{8,104},{10,106},{12,108},{14,110},{... | collective-permute-start | bytes 442376 | tf_op jit(solution)/shard_map/ppermute | solution.py:331
  64.9 4.5 %collective-permute-done.7 = bf16[192,384]{1,0:T(8,128)(2,1)S(1)} collective-permute-done((bf16[192,384]{1,0:T(8,128)(2,1)S(1)}, bf16[192,384]{1,0:T(8,128)(2,1)S(1)}, u32[]{:S(2)}, u32[]{:S(2)}) %collective-permute-start.7) | collective-permute-done | bytes 147488 | tf_op jit(solution)/shard_map/ppermute | solution.py:331
  70.7 2.8 %collective-permute-start.17 = (bf16[192,384]{1,0:T(8,128)(2,1)S(1)}, bf16[192,384]{1,0:T(8,128)(2,1)S(1)}, u32[]{:S(2)}, u32[]{:S(2)}) collective-permute-start(bf16[192,384]{1,0:T(8,128)(2,1)S(1)} %broadcast_select_fusion.2), channel_id=1, source_target_pairs={{0,96},{2,98},{4,100},{6,102},{8,104},{10,106},{12,108},{14,110},{... | collective-permute-start | bytes 442376 | tf_op jit(solution)/shard_map/ppermute | solution.py:331
  74.2 4.1 %collective-permute-start.8 = (bf16[192,384]{1,0:T(8,128)(2,1)S(1)}, bf16[192,384]{1,0:T(8,128)(2,1)S(1)}, u32[]{:S(2)}, u32[]{:S(2)}) collective-permute-start(bf16[192,384]{1,0:T(8,128)(2,1)S(1)} %get-tuple-element.41), channel_id=1, source_target_pairs={{0,224},{2,226},{4,228},{6,230},{8,232},{10,234},{12,236},{14,238}... | collective-permute-start | bytes 442376 | tf_op jit(solution)/shard_map/ppermute | solution.py:331
  79.8 3.1 %collective-permute-start.18 = (bf16[192,384]{1,0:T(8,128)(2,1)S(1)}, bf16[192,384]{1,0:T(8,128)(2,1)S(1)}, u32[]{:S(2)}, u32[]{:S(2)}) collective-permute-start(bf16[192,384]{1,0:T(8,128)(2,1)S(1)} %broadcast_select_fusion), channel_id=1, source_target_pairs={{0,224},{2,226},{4,228},{6,230},{8,232},{10,234},{12,236},{14,238}... | collective-permute-start | bytes 442376 | tf_op jit(solution)/shard_map/ppermute | solution.py:331
  83.9 4.3 %collective-permute-done.4 = bf16[3,256,384]{2,1,0:T(8,128)(2,1)S(1)} collective-permute-done((bf16[3,256,384]{2,1,0:T(8,128)(2,1)S(1)}, bf16[3,256,384]{2,1,0:T(8,128)(2,1)S(1)}, u32[]{:S(2)}, u32[]{:S(2)}) %collective-permute-start.4) | collective-permute-done | bytes 589856 | tf_op jit(solution)/shard_map/ppermute | solution.py:408
  91.8 3.0 %shard_map.108 = (bf16[16,384]{1,0:T(8,128)(2,1)}, bf16[8,4,16,384]{3,2,1,0:T(8,128)(2,1)}) custom-call(s32[1]{0:T(128)} %bitcast.1.refs_0_.core, bf16[16,5,16,384]{3,2,1,0:T(8,128)(2,1)} %copy-done.7, bf16[4,192,384]{2,1,0:T(8,128)(2,1)} %copy-done.4, bf16[4,192,384]{2,1,0:T(8,128)(2,1)} %copy-done.9), custom_call_target="tpu_custom_call" | custom-call | flops 1000000000 | bytes 2568192 | tf_op jit(solution)/shard_map/pallas_call | solution.py:61
  94.8 3.9 %all-to-all-start.1 = ((bf16[8,4,16,384]{3,2,1,0:T(8,128)(2,1)}), bf16[8,4,16,384]{3,2,1,0:T(8,128)(2,1)S(1)}, u32[]{:S(2)}, u32[]{:S(2)}) async-start(bf16[8,4,16,384]{3,2,1,0:T(8,128)(2,1)} %get-tuple-element.42), calls=%async_computation.1 | async-start | bytes 786432 | tf_op jit(solution)/shard_map/all_to_all | solution.py:339
  100.9 5.3 %collective-permute-done.11 = bf16[1,256,384]{2,1,0:T(8,128)(2,1)S(1)} collective-permute-done((bf16[1,256,384]{2,1,0:T(8,128)(2,1)S(1)}, bf16[1,256,384]{2,1,0:T(8,128)(2,1)S(1)}, u32[]{:S(2)}, u32[]{:S(2)}) %collective-permute-start.11) | collective-permute-done | bytes 196640 | tf_op jit(solution)/shard_map/ppermute | solution.py:408
  106.9 7.1 %all-to-all-done.1.refs_2_ = bf16[8,4,16,384]{3,2,1,0:T(8,128)(2,1)S(1)} async-done(((bf16[8,4,16,384]{3,2,1,0:T(8,128)(2,1)}), bf16[8,4,16,384]{3,2,1,0:T(8,128)(2,1)S(1)}, u32[]{:S(2)}, u32[]{:S(2)}) %all-to-all-start.1) | async-done | bytes 393248 | tf_op jit(solution)/shard_map/all_to_all | solution.py:339
  115.1 2.8 %shard_map.109 = bf16[16,5,16,384]{3,2,1,0:T(8,128)(2,1)} custom-call(s32[1]{0:T(128)} %bitcast.1.refs_0_.core, s32[1]{0:T(128)} %bitcast.3.refs_1_, bf16[8,4,16,384]{3,2,1,0:T(8,128)(2,1)} %copy-done.11, bf16[16,384]{1,0:T(8,128)(2,1)} %get-tuple-element.44.refs_3_, bf16[5,192,384]{2,1,0:T(8,128)(2,1)} %bitcast_dynamic-update-slice_fusion.refs_4_, ...), custom_call_target="tpu_custom_call" | custom-call | flops 1000000000 | bytes 2863104 | tf_op jit(solution)/shard_map/pallas_call | solution.py:61
  117.9 6.6 %all-to-all-start.2 = ((bf16[16,5,16,384]{3,2,1,0:T(8,128)(2,1)}), bf16[16,5,16,384]{3,2,1,0:T(8,128)(2,1)S(1)}, u32[]{:S(2)}, u32[]{:S(2)}) async-start(bf16[16,5,16,384]{3,2,1,0:T(8,128)(2,1)} %shard_map.109), calls=%async_computation.2 | async-start | bytes 1966080 | tf_op jit(solution)/shard_map/all_to_all | solution.py:339
  124.7 6.1 %shard_map.110 = (f32[16,128,256]{2,1,0:T(8,128)}, bf16[16,2,128,128]{3,2,1,0:T(8,128)(2,1)}, bf16[8,2,128,384]{3,2,1,0:T(8,128)(2,1)}) custom-call(s32[16,2]{1,0:T(8,128)} %copy.16.cols.refs_0_, s32[8,2]{1,0:T(8,128)} %copy.17.sep_cols.refs_1_, bf16[16,128,256]{2,1,0:T(8,128)(2,1)} %get-tuple-element.56.refs_2_, bf16[16,128,128]{2,1,0:T(8,128)(2,1)} %refs_3_.1, ...), custom_call_target="tpu_custom_call" | custom-call | flops 1000000000 | bytes 8912896 | tf_op jit(solution)/shard_map/pallas_call | solution.py:61
  130.7 9.6 %all-to-all-done.2.refs_0_ = bf16[16,5,16,384]{3,2,1,0:T(8,128)(2,1)S(1)} async-done(((bf16[16,5,16,384]{3,2,1,0:T(8,128)(2,1)}), bf16[16,5,16,384]{3,2,1,0:T(8,128)(2,1)S(1)}, u32[]{:S(2)}, u32[]{:S(2)}) %all-to-all-start.2) | async-done | bytes 983072 | tf_op jit(solution)/shard_map/all_to_all | solution.py:339
  141.3 9.6 %shard_map.111 = (bf16[16,128,256]{2,1,0:T(8,128)(2,1)}, bf16[384,256]{1,0:T(8,128)(2,1)}) custom-call(s32[16,2]{1,0:T(8,128)} %copy.16.cols.refs_0_, s32[8,2]{1,0:T(8,128)} %copy.17.sep_cols.refs_1_, s32[1]{0:T(128)} %bitcast.1.refs_0_.core, s32[1]{0:T(128)} %bitcast.2.own_level, bf16[16,5,16,384]{3,2,1,0:T(8,128)(2,1)} %copy-done.2, ...), custom_call_target="tpu_custom_call" | custom-call | flops 1000000000 | bytes 11075584 | tf_op jit(solution)/shard_map/pallas_call | solution.py:61
  (96 shorter events, 33.1 us)
Async XLA Ops:
  3.0 8.6 %collective-permute-start = (bf16[192,384]{1,0:T(8,128)(2,1)}, bf16[192,384]{1,0:T(8,128)(2,1)S(1)}, u32[]{:S(2)}, u32[]{:S(2)}) collective-permute-start(bf16[192,384]{1,0:T(8,128)(2,1)} %get-tuple-element.32), channel_id=1, source_target_pairs={{0,2},{2,0},{4,6},{6,4},{8,10},{10,8},{12,14},{14,12},{16,18},{18,... | collective-permute-start | bytes 442376 | tf_op jit(solution)/shard_map/ppermute | solution.py:331
  11.7 5.2 %collective-permute-start.12 = (bf16[192,384]{1,0:T(8,128)(2,1)S(1)}, bf16[192,384]{1,0:T(8,128)(2,1)S(1)}, u32[]{:S(2)}, u32[]{:S(2)}) collective-permute-start(bf16[192,384]{1,0:T(8,128)(2,1)S(1)} %copy-done.12), channel_id=1, source_target_pairs={{0,2},{2,0},{4,6},{6,4},{8,10},{10,8},{12,14},{14,12},{16,18},{18,... | collective-permute-start | bytes 442376 | tf_op jit(solution)/shard_map/ppermute | solution.py:331
  12.4 5.2 %collective-permute-start.1 = (bf16[192,384]{1,0:T(8,128)(2,1)S(1)}, bf16[192,384]{1,0:T(8,128)(2,1)S(1)}, u32[]{:S(2)}, u32[]{:S(2)}) collective-permute-start(bf16[192,384]{1,0:T(8,128)(2,1)S(1)} %get-tuple-element.35), channel_id=1, source_target_pairs={{0,6},{2,4},{4,2},{6,0},{8,14},{10,12},{12,10},{14,8},{16,22},{18,... | collective-permute-start | bytes 442376 | tf_op jit(solution)/shard_map/ppermute | solution.py:331
  17.7 5.2 %collective-permute-start.13 = (bf16[192,384]{1,0:T(8,128)(2,1)S(1)}, bf16[192,384]{1,0:T(8,128)(2,1)S(1)}, u32[]{:S(2)}, u32[]{:S(2)}) collective-permute-start(bf16[192,384]{1,0:T(8,128)(2,1)S(1)} %get-tuple-element.48), channel_id=1, source_target_pairs={{0,6},{2,4},{4,2},{6,0},{8,14},{10,12},{12,10},{14,8},{16,22},{18,... | collective-permute-start | bytes 442376 | tf_op jit(solution)/shard_map/ppermute | solution.py:331
  19.9 5.2 %collective-permute-start.2 = (bf16[192,384]{1,0:T(8,128)(2,1)S(1)}, bf16[192,384]{1,0:T(8,128)(2,1)S(1)}, u32[]{:S(2)}, u32[]{:S(2)}) collective-permute-start(bf16[192,384]{1,0:T(8,128)(2,1)S(1)} %get-tuple-element.79), channel_id=1, source_target_pairs={{0,8},{2,10},{4,12},{6,14},{8,0},{10,2},{12,4},{14,6},{16,24},{18,... | collective-permute-start | bytes 442376 | tf_op jit(solution)/shard_map/ppermute | solution.py:331
  25.1 5.2 %collective-permute-start.14 = (bf16[192,384]{1,0:T(8,128)(2,1)S(1)}, bf16[192,384]{1,0:T(8,128)(2,1)S(1)}, u32[]{:S(2)}, u32[]{:S(2)}) collective-permute-start(bf16[192,384]{1,0:T(8,128)(2,1)S(1)} %get-tuple-element.49), channel_id=1, source_target_pairs={{0,8},{2,10},{4,12},{6,14},{8,0},{10,2},{12,4},{14,6},{16,24},{18,... | collective-permute-start | bytes 442376 | tf_op jit(solution)/shard_map/ppermute | solution.py:331
  27.4 6.4 %collective-permute-start.5 = (bf16[192,384]{1,0:T(8,128)(2,1)S(1)}, bf16[192,384]{1,0:T(8,128)(2,1)S(1)}, u32[]{:S(2)}, u32[]{:S(2)}) collective-permute-start(bf16[192,384]{1,0:T(8,128)(2,1)S(1)} %get-tuple-element.74), channel_id=1, source_target_pairs={{0,24},{2,26},{4,28},{6,30},{8,16},{10,18},{12,20},{14,22},{16,8},... | collective-permute-start | bytes 442376 | tf_op jit(solution)/shard_map/ppermute | solution.py:331
  29.6 17.7 %collective-permute-start.3 = (bf16[3,192,384]{2,1,0:T(8,128)(2,1)S(1)}, bf16[3,192,384]{2,1,0:T(8,128)(2,1)S(1)}, u32[]{:S(2)}, u32[]{:S(2)}) collective-permute-start(bf16[3,192,384]{2,1,0:T(8,128)(2,1)S(1)} %pad_maximum_fusion.1.refs_2_.refs_3_), channel_id=1, source_target_pairs={{0,1},{1,0},{2,3},{3,2},{4,5},{5,4},{6,7},{7,6},{8,9},{9,8},{10,11... | collective-permute-start | bytes 1327112 | tf_op jit(solution)/shard_map/ppermute | solution.py:275
  33.8 13.4 %collective-permute-start.15 = (bf16[192,384]{1,0:T(8,128)(2,1)S(1)}, bf16[192,384]{1,0:T(8,128)(2,1)S(1)}, u32[]{:S(2)}, u32[]{:S(2)}) collective-permute-start(bf16[192,384]{1,0:T(8,128)(2,1)S(1)} %get-tuple-element.50), channel_id=1, source_target_pairs={{0,24},{2,26},{4,28},{6,30},{8,16},{10,18},{12,20},{14,22},{16,8},... | collective-permute-start | bytes 442376 | tf_op jit(solution)/shard_map/ppermute | solution.py:331
  45.3 14.1 %collective-permute-start.6 = (bf16[192,384]{1,0:T(8,128)(2,1)S(1)}, bf16[192,384]{1,0:T(8,128)(2,1)S(1)}, u32[]{:S(2)}, u32[]{:S(2)}) collective-permute-start(bf16[192,384]{1,0:T(8,128)(2,1)S(1)} %get-tuple-element.69), channel_id=1, source_target_pairs={{0,32},{2,34},{4,36},{6,38},{8,40},{10,42},{12,44},{14,46},{16,48}... | collective-permute-start | bytes 442376 | tf_op jit(solution)/shard_map/ppermute | solution.py:331
  52.2 18.5 %all-to-all-start = ((bf16[16,5,16,384]{3,2,1,0:T(8,128)(2,1)}), bf16[16,5,16,384]{3,2,1,0:T(8,128)(2,1)S(1)}, u32[]{:S(2)}, u32[]{:S(2)}) async-start(bf16[16,5,16,384]{3,2,1,0:T(8,128)(2,1)} %get-tuple-element.36), calls=%async_computation | async-start | bytes 1966080 | tf_op jit(solution)/shard_map/all_to_all | solution.py:339
  59.4 5.5 %collective-permute-start.16 = (bf16[192,384]{1,0:T(8,128)(2,1)S(1)}, bf16[192,384]{1,0:T(8,128)(2,1)S(1)}, u32[]{:S(2)}, u32[]{:S(2)}) collective-permute-start(bf16[192,384]{1,0:T(8,128)(2,1)S(1)} %broadcast_select_fusion.4), channel_id=1, source_target_pairs={{0,32},{2,34},{4,36},{6,38},{8,40},{10,42},{12,44},{14,46},{16,48}... | collective-permute-start | bytes 442376 | tf_op jit(solution)/shard_map/ppermute | solution.py:331
  60.8 8.7 %collective-permute-start.7 = (bf16[192,384]{1,0:T(8,128)(2,1)S(1)}, bf16[192,384]{1,0:T(8,128)(2,1)S(1)}, u32[]{:S(2)}, u32[]{:S(2)}) collective-permute-start(bf16[192,384]{1,0:T(8,128)(2,1)S(1)} %get-tuple-element.40), channel_id=1, source_target_pairs={{0,96},{2,98},{4,100},{6,102},{8,104},{10,106},{12,108},{14,110},{... | collective-permute-start | bytes 442376 | tf_op jit(solution)/shard_map/ppermute | solution.py:331
  70.7 9.1 %collective-permute-start.17 = (bf16[192,384]{1,0:T(8,128)(2,1)S(1)}, bf16[192,384]{1,0:T(8,128)(2,1)S(1)}, u32[]{:S(2)}, u32[]{:S(2)}) collective-permute-start(bf16[192,384]{1,0:T(8,128)(2,1)S(1)} %broadcast_select_fusion.2), channel_id=1, source_target_pairs={{0,96},{2,98},{4,100},{6,102},{8,104},{10,106},{12,108},{14,110},{... | collective-permute-start | bytes 442376 | tf_op jit(solution)/shard_map/ppermute | solution.py:331
  74.2 8.7 %collective-permute-start.8 = (bf16[192,384]{1,0:T(8,128)(2,1)S(1)}, bf16[192,384]{1,0:T(8,128)(2,1)S(1)}, u32[]{:S(2)}, u32[]{:S(2)}) collective-permute-start(bf16[192,384]{1,0:T(8,128)(2,1)S(1)} %get-tuple-element.41), channel_id=1, source_target_pairs={{0,224},{2,226},{4,228},{6,230},{8,232},{10,234},{12,236},{14,238}... | collective-permute-start | bytes 442376 | tf_op jit(solution)/shard_map/ppermute | solution.py:331
  78.3 9.9 %collective-permute-start.4 = (bf16[3,256,384]{2,1,0:T(8,128)(2,1)S(1)}, bf16[3,256,384]{2,1,0:T(8,128)(2,1)S(1)}, u32[]{:S(2)}, u32[]{:S(2)}) collective-permute-start(bf16[3,256,384]{2,1,0:T(8,128)(2,1)S(1)} %copy-done.8), channel_id=1, source_target_pairs={{0,2},{2,0},{4,6},{6,4},{8,10},{10,8},{12,14},{14,12},{16,18},{18,... | collective-permute-start | bytes 1769480 | tf_op jit(solution)/shard_map/ppermute | solution.py:408
  79.8 9.7 %collective-permute-start.18 = (bf16[192,384]{1,0:T(8,128)(2,1)S(1)}, bf16[192,384]{1,0:T(8,128)(2,1)S(1)}, u32[]{:S(2)}, u32[]{:S(2)}) collective-permute-start(bf16[192,384]{1,0:T(8,128)(2,1)S(1)} %broadcast_select_fusion), channel_id=1, source_target_pairs={{0,224},{2,226},{4,228},{6,230},{8,232},{10,234},{12,236},{14,238}... | collective-permute-start | bytes 442376 | tf_op jit(solution)/shard_map/ppermute | solution.py:331
  83.0 7.9 %collective-permute-start.9 = (bf16[4,192,384]{2,1,0:T(8,128)(2,1)S(1)}, bf16[4,192,384]{2,1,0:T(8,128)(2,1)S(1)}, u32[]{:S(2)}, u32[]{:S(2)}) collective-permute-start(bf16[4,192,384]{2,1,0:T(8,128)(2,1)S(1)} %pad_maximum_fusion.refs_2_.refs_1_), channel_id=1, source_target_pairs={{0,1},{1,0},{2,3},{3,2},{4,5},{5,4},{6,7},{7,6},{8,9},{9,8},{10,11... | collective-permute-start | bytes 1769480 | tf_op jit(solution)/shard_map/ppermute | solution.py:275
  89.2 9.5 %collective-permute-start.10 = (bf16[2,256,384]{2,1,0:T(8,128)(2,1)}, bf16[2,256,384]{2,1,0:T(8,128)(2,1)S(1)}, u32[]{:S(2)}, u32[]{:S(2)}) collective-permute-start(bf16[2,256,384]{2,1,0:T(8,128)(2,1)} %slice.73), channel_id=1, source_target_pairs={{0,6},{2,4},{4,2},{6,0},{8,14},{10,12},{12,10},{14,8},{16,22},{18,... | collective-permute-start | bytes 1179656 | tf_op jit(solution)/shard_map/ppermute | solution.py:408
  90.9 23.1 %collective-permute-start.19 = (bf16[5,192,384]{2,1,0:T(8,128)(2,1)}, bf16[5,192,384]{2,1,0:T(8,128)(2,1)S(1)}, u32[]{:S(2)}, u32[]{:S(2)}) collective-permute-start(bf16[5,192,384]{2,1,0:T(8,128)(2,1)} %bitcast_dynamic-update-slice_fusion.refs_4_), channel_id=1, source_target_pairs={{0,1},{1,0},{2,3},{3,2},{4,5},{5,4},{6,7},{7,6},{8,9},{9,8},{10,11... | collective-permute-start | bytes 2211848 | tf_op jit(solution)/shard_map/ppermute | solution.py:275
  94.8 19.2 %all-to-all-start.1 = ((bf16[8,4,16,384]{3,2,1,0:T(8,128)(2,1)}), bf16[8,4,16,384]{3,2,1,0:T(8,128)(2,1)S(1)}, u32[]{:S(2)}, u32[]{:S(2)}) async-start(bf16[8,4,16,384]{3,2,1,0:T(8,128)(2,1)} %get-tuple-element.42), calls=%async_computation.1 | async-start | bytes 786432 | tf_op jit(solution)/shard_map/all_to_all | solution.py:339
  98.9 7.3 %collective-permute-start.11 = (bf16[1,256,384]{2,1,0:T(8,128)(2,1)S(1)}, bf16[1,256,384]{2,1,0:T(8,128)(2,1)S(1)}, u32[]{:S(2)}, u32[]{:S(2)}) collective-permute-start(bf16[1,256,384]{2,1,0:T(8,128)(2,1)S(1)} %slice.74), channel_id=1, source_target_pairs={{0,8},{2,10},{4,12},{6,14},{8,0},{10,2},{12,4},{14,6},{16,24},{18,... | collective-permute-start | bytes 589832 | tf_op jit(solution)/shard_map/ppermute | solution.py:408
  117.9 22.4 %all-to-all-start.2 = ((bf16[16,5,16,384]{3,2,1,0:T(8,128)(2,1)}), bf16[16,5,16,384]{3,2,1,0:T(8,128)(2,1)S(1)}, u32[]{:S(2)}, u32[]{:S(2)}) async-start(bf16[16,5,16,384]{3,2,1,0:T(8,128)(2,1)} %shard_map.109), calls=%async_computation.2 | async-start | bytes 1966080 | tf_op jit(solution)/shard_map/all_to_all | solution.py:339
  124.5 6.2 %collective-permute-start.20 = (bf16[3,192,384]{2,1,0:T(8,128)(2,1)S(1)}, bf16[3,192,384]{2,1,0:T(8,128)(2,1)S(1)}, u32[]{:S(2)}, u32[]{:S(2)}) collective-permute-start(bf16[3,192,384]{2,1,0:T(8,128)(2,1)S(1)} %pad_maximum_fusion.2.refs_5_), channel_id=1, source_target_pairs={{0,1},{1,0},{2,3},{3,2},{4,5},{5,4},{6,7},{7,6},{8,9},{9,8},{10,11... | collective-permute-start | bytes 1327112 | tf_op jit(solution)/shard_map/ppermute | solution.py:275
  (17 other events, 141.6 us)

commit v6 on v5

--- a/solution.py
+++ b/solution.py
@@ -387,7 +387,7 @@
     climb_gain(0)
     both(1, solved_first)
     for bit in range(2, LOW):
-        both(bit)
+        both(bit, solved)
     gains_low = with_other_core(flags[:LOW], gain_list)
     both(LOW)
     both(LOW + 1)

time: 152 us -> 153 us (level)
    unnamed x35 -> x33, local copies, waits for them, and re-layouts: 4.36 us -> 4.13 us
  transfers between devices with their start and end apart: 24 -> 24, of which waited for: 12 -> 11; matrix products, arithmetic and copies ran while one was open for 5% -> 5% of each run, Pallas kernels for 16% -> 16%
where the time goes in v6:
time: 153 us; the launch traced here: 152 us
  starting transfers between devices  53 us (35%)
  waiting for transfers between devices  44.4 us (29%)
  Pallas kernels  38.6 us (25%)
  local copies, waits for them, and re-layouts  5.55 us (4%)
  between operations  5.5 us (4%)
  other arithmetic  5.13 us (3%)
    pallas_call x8, Pallas kernels, placed(): pl.pallas_call(kernel, out_shape=tuple(outs), in_specs=[smem] * len(scala...  38.6 us
    ppermute x14, starting transfers between devices, climb(): arrived = lax.ppermute(top, 'blk', [(i, i ^ mask) for i in range(size)])  30.9 us
    all_to_all x3, starting transfers between devices, within(): lax.all_to_all(value, 'blk', 0, 0, axis_index_groups=members, tiled=True)  18.6 us
    all_to_all x3, waiting for transfers between devices, within(): lax.all_to_all(value, 'blk', 0, 0, axis_index_groups=members, tiled=True)  18.3 us
    ppermute x14, waiting for transfers between devices, climb(): arrived = lax.ppermute(top, 'blk', [(i, i ^ mask) for i in range(size)])  15.9 us
    ppermute x3, waiting for transfers between devices, swapped(): lax.ppermute(value, 'blk', [(i, i ^ mask) for i in range(size)])  10.2 us
    unnamed x33, local copies, waits for them, and re-layouts  4.13 us
    ppermute x3, starting transfers between devices, swapped(): lax.ppermute(value, 'blk', [(i, i ^ mask) for i in range(size)])  3.16 us
  transfers between devices with their start and end apart: 24, of which 11 were waited for; matrix products, arithmetic and copies ran while one was open for 5% of the time, Pallas kernels for 16%

profile of v6, /device:TPU:8, one launch (start us, length us, event | category | flops | bytes accessed | tf_op | source)
XLA Modules:
  0.0 152.2 jit_solution(8415749850329386188)
XLA Ops:
  0.6 2.3 %shard_map.104 = (bf16[192,384]{1,0:T(8,128)(2,1)}, bf16[192,384]{1,0:T(8,128)(2,1)}) custom-call(s32[1]{0:T(128)} %bitcast.1.refs_0_.core, bf16[384,384]{1,0:T(8,128)(2,1)} %bitcast.50, bf16[384,384]{1,0:T(8,128)(2,1)} %bitcast.51), custom_call_target="tpu_custom_call" | custom-call | flops 1000000000 | bytes 884736 | tf_op jit(solution)/shard_map/pallas_call | solution.py:61
  3.0 2.3 %collective-permute-start = (bf16[192,384]{1,0:T(8,128)(2,1)}, bf16[192,384]{1,0:T(8,128)(2,1)S(1)}, u32[]{:S(2)}, u32[]{:S(2)}) collective-permute-start(bf16[192,384]{1,0:T(8,128)(2,1)} %get-tuple-element.34), channel_id=1, source_target_pairs={{0,2},{2,0},{4,6},{6,4},{8,10},{10,8},{12,14},{14,12},{16,18},{18,... | collective-permute-start | bytes 442376 | tf_op jit(solution)/shard_map/ppermute | solution.py:331
  7.3 4.4 %shard_map.105.refs_5_ = bf16[8,128,256]{2,1,0:T(8,128)(2,1)} custom-call(s32[16,2]{1,0:T(8,128)} %copy.16.cols.refs_0_, bf16[16,128,128]{2,1,0:T(8,128)(2,1)} %refs_3_.1, bf16[16,2,128,128]{3,2,1,0:T(8,128)(2,1)} %refs_4_.1, bf16[16,128,256]{2,1,0:T(8,128)(2,1)} %refs_2_.2), custom_call_target="tpu_custom_call" | custom-call | flops 1000000000 | bytes 3145728 | tf_op jit(solution)/shard_map/pallas_call | solution.py:61
  13.1 6.4 %shard_map.106 = (bf16[16,128,256]{2,1,0:T(8,128)(2,1)}, f32[8,384,256]{2,1,0:T(8,128)}) custom-call(s32[16,2]{1,0:T(8,128)} %copy.16.cols.refs_0_, s32[8,2]{1,0:T(8,128)} %copy.17.sep_cols.refs_1_, s32[1]{0:T(128)} %bitcast.2.own_level, bf16[16,128,128]{2,1,0:T(8,128)(2,1)} %refs_3_.1, bf16[16,2,128,128]{3,2,1,0:T(8,128)(2,1)} %refs_4_.1, ...), custom_call_target="tpu_custom_call" | custom-call | flops 1000000000 | bytes 9109504 | tf_op jit(solution)/shard_map/pallas_call | solution.py:61
  21.0 3.7 %collective-permute-done.1 = bf16[192,384]{1,0:T(8,128)(2,1)S(1)} collective-permute-done((bf16[192,384]{1,0:T(8,128)(2,1)S(1)}, bf16[192,384]{1,0:T(8,128)(2,1)S(1)}, u32[]{:S(2)}, u32[]{:S(2)}) %collective-permute-start.1) | collective-permute-done | bytes 147488 | tf_op jit(solution)/shard_map/ppermute | solution.py:331
  37.6 3.4 %collective-permute-done.5 = bf16[192,384]{1,0:T(8,128)(2,1)S(1)} collective-permute-done((bf16[192,384]{1,0:T(8,128)(2,1)S(1)}, bf16[192,384]{1,0:T(8,128)(2,1)S(1)}, u32[]{:S(2)}, u32[]{:S(2)}) %collective-permute-start.5) | collective-permute-done | bytes 147488 | tf_op jit(solution)/shard_map/ppermute | solution.py:331
  41.0 2.7 %collective-permute-start.15 = (bf16[192,384]{1,0:T(8,128)(2,1)S(1)}, bf16[192,384]{1,0:T(8,128)(2,1)S(1)}, u32[]{:S(2)}, u32[]{:S(2)}) collective-permute-start(bf16[192,384]{1,0:T(8,128)(2,1)S(1)} %get-tuple-element.55), channel_id=1, source_target_pairs={{0,24},{2,26},{4,28},{6,30},{8,16},{10,18},{12,20},{14,22},{16,8},... | collective-permute-start | bytes 442376 | tf_op jit(solution)/shard_map/ppermute | solution.py:331
  48.5 4.1 %shard_map.107 = (bf16[3,256,384]{2,1,0:T(8,128)(2,1)}, bf16[16,5,16,384]{3,2,1,0:T(8,128)(2,1)}) custom-call(s32[1]{0:T(128)} %bitcast.1.refs_0_.core, f32[8,384,256]{2,1,0:T(8,128)} %get-tuple-element.36.refs_1_, bf16[3,192,384]{2,1,0:T(8,128)(2,1)} %copy-done.1, bf16[3,192,384]{2,1,0:T(8,128)(2,1)} %copy-done.5), custom_call_target="tpu_custom_call" | custom-call | flops 1000000000 | bytes 5603328 | tf_op jit(solution)/shard_map/pallas_call | solution.py:61
  52.6 7.0 %all-to-all-start = ((bf16[16,5,16,384]{3,2,1,0:T(8,128)(2,1)}), bf16[16,5,16,384]{3,2,1,0:T(8,128)(2,1)S(1)}, u32[]{:S(2)}, u32[]{:S(2)}) async-start(bf16[16,5,16,384]{3,2,1,0:T(8,128)(2,1)} %get-tuple-element.40), calls=%async_computation | async-start | bytes 1966080 | tf_op jit(solution)/shard_map/all_to_all | solution.py:339
  62.2 2.8 %collective-permute-start.7 = (bf16[192,384]{1,0:T(8,128)(2,1)S(1)}, bf16[192,384]{1,0:T(8,128)(2,1)S(1)}, u32[]{:S(2)}, u32[]{:S(2)}) collective-permute-start(bf16[192,384]{1,0:T(8,128)(2,1)S(1)} %get-tuple-element.44), channel_id=1, source_target_pairs={{0,96},{2,98},{4,100},{6,102},{8,104},{10,106},{12,108},{14,110},{... | collective-permute-start | bytes 442376 | tf_op jit(solution)/shard_map/ppermute | solution.py:331
  65.0 4.2 %collective-permute-done.7 = bf16[192,384]{1,0:T(8,128)(2,1)S(1)} collective-permute-done((bf16[192,384]{1,0:T(8,128)(2,1)S(1)}, bf16[192,384]{1,0:T(8,128)(2,1)S(1)}, u32[]{:S(2)}, u32[]{:S(2)}) %collective-permute-start.7) | collective-permute-done | bytes 147488 | tf_op jit(solution)/shard_map/ppermute | solution.py:331
  70.7 4.5 %collective-permute-start.17 = (bf16[192,384]{1,0:T(8,128)(2,1)S(1)}, bf16[192,384]{1,0:T(8,128)(2,1)S(1)}, u32[]{:S(2)}, u32[]{:S(2)}) collective-permute-start(bf16[192,384]{1,0:T(8,128)(2,1)S(1)} %broadcast_select_fusion.2), channel_id=1, source_target_pairs={{0,96},{2,98},{4,100},{6,102},{8,104},{10,106},{12,108},{14,110},{... | collective-permute-start | bytes 442376 | tf_op jit(solution)/shard_map/ppermute | solution.py:331
  76.0 3.2 %collective-permute-start.8 = (bf16[192,384]{1,0:T(8,128)(2,1)S(1)}, bf16[192,384]{1,0:T(8,128)(2,1)S(1)}, u32[]{:S(2)}, u32[]{:S(2)}) collective-permute-start(bf16[192,384]{1,0:T(8,128)(2,1)S(1)} %get-tuple-element.45), channel_id=1, source_target_pairs={{0,224},{2,226},{4,228},{6,230},{8,232},{10,234},{12,236},{14,238}... | collective-permute-start | bytes 442376 | tf_op jit(solution)/shard_map/ppermute | solution.py:331
  80.7 3.1 %collective-permute-start.18 = (bf16[192,384]{1,0:T(8,128)(2,1)S(1)}, bf16[192,384]{1,0:T(8,128)(2,1)S(1)}, u32[]{:S(2)}, u32[]{:S(2)}) collective-permute-start(bf16[192,384]{1,0:T(8,128)(2,1)S(1)} %broadcast_select_fusion), channel_id=1, source_target_pairs={{0,224},{2,226},{4,228},{6,230},{8,232},{10,234},{12,236},{14,238}... | collective-permute-start | bytes 442376 | tf_op jit(solution)/shard_map/ppermute | solution.py:331
  84.8 4.3 %collective-permute-done.4 = bf16[3,256,384]{2,1,0:T(8,128)(2,1)S(1)} collective-permute-done((bf16[3,256,384]{2,1,0:T(8,128)(2,1)S(1)}, bf16[3,256,384]{2,1,0:T(8,128)(2,1)S(1)}, u32[]{:S(2)}, u32[]{:S(2)}) %collective-permute-start.4) | collective-permute-done | bytes 589856 | tf_op jit(solution)/shard_map/ppermute | solution.py:408
  92.0 3.0 %shard_map.108 = (bf16[16,384]{1,0:T(8,128)(2,1)}, bf16[8,4,16,384]{3,2,1,0:T(8,128)(2,1)}) custom-call(s32[1]{0:T(128)} %bitcast.1.refs_0_.core, bf16[16,5,16,384]{3,2,1,0:T(8,128)(2,1)} %copy-done.7, bf16[4,192,384]{2,1,0:T(8,128)(2,1)} %copy-done.4, bf16[4,192,384]{2,1,0:T(8,128)(2,1)} %copy-done.9), custom_call_target="tpu_custom_call" | custom-call | flops 1000000000 | bytes 2568192 | tf_op jit(solution)/shard_map/pallas_call | solution.py:61
  95.0 4.6 %all-to-all-start.1 = ((bf16[8,4,16,384]{3,2,1,0:T(8,128)(2,1)}), bf16[8,4,16,384]{3,2,1,0:T(8,128)(2,1)S(1)}, u32[]{:S(2)}, u32[]{:S(2)}) async-start(bf16[8,4,16,384]{3,2,1,0:T(8,128)(2,1)} %get-tuple-element.46), calls=%async_computation.1 | async-start | bytes 786432 | tf_op jit(solution)/shard_map/all_to_all | solution.py:339
  101.1 5.8 %collective-permute-done.11 = bf16[1,256,384]{2,1,0:T(8,128)(2,1)S(1)} collective-permute-done((bf16[1,256,384]{2,1,0:T(8,128)(2,1)S(1)}, bf16[1,256,384]{2,1,0:T(8,128)(2,1)S(1)}, u32[]{:S(2)}, u32[]{:S(2)}) %collective-permute-start.11) | collective-permute-done | bytes 196640 | tf_op jit(solution)/shard_map/ppermute | solution.py:408
  107.7 7.3 %all-to-all-done.1.refs_2_ = bf16[8,4,16,384]{3,2,1,0:T(8,128)(2,1)S(1)} async-done(((bf16[8,4,16,384]{3,2,1,0:T(8,128)(2,1)}), bf16[8,4,16,384]{3,2,1,0:T(8,128)(2,1)S(1)}, u32[]{:S(2)}, u32[]{:S(2)}) %all-to-all-start.1) | async-done | bytes 393248 | tf_op jit(solution)/shard_map/all_to_all | solution.py:339
  115.8 2.8 %shard_map.109 = bf16[16,5,16,384]{3,2,1,0:T(8,128)(2,1)} custom-call(s32[1]{0:T(128)} %bitcast.1.refs_0_.core, s32[1]{0:T(128)} %bitcast.3.refs_1_, bf16[8,4,16,384]{3,2,1,0:T(8,128)(2,1)} %copy-done.11, bf16[16,384]{1,0:T(8,128)(2,1)} %get-tuple-element.48.refs_3_, bf16[5,192,384]{2,1,0:T(8,128)(2,1)} %bitcast_dynamic-update-slice_fusion.refs_4_, ...), custom_call_target="tpu_custom_call" | custom-call | flops 1000000000 | bytes 2863104 | tf_op jit(solution)/shard_map/pallas_call | solution.py:61
  118.6 7.1 %all-to-all-start.2 = ((bf16[16,5,16,384]{3,2,1,0:T(8,128)(2,1)}), bf16[16,5,16,384]{3,2,1,0:T(8,128)(2,1)S(1)}, u32[]{:S(2)}, u32[]{:S(2)}) async-start(bf16[16,5,16,384]{3,2,1,0:T(8,128)(2,1)} %shard_map.109), calls=%async_computation.2 | async-start | bytes 1966080 | tf_op jit(solution)/shard_map/all_to_all | solution.py:339
  125.9 6.1 %shard_map.110 = (f32[16,128,256]{2,1,0:T(8,128)}, bf16[16,2,128,128]{3,2,1,0:T(8,128)(2,1)}, bf16[8,2,128,384]{3,2,1,0:T(8,128)(2,1)}) custom-call(s32[16,2]{1,0:T(8,128)} %copy.16.cols.refs_0_, s32[8,2]{1,0:T(8,128)} %copy.17.sep_cols.refs_1_, bf16[16,128,256]{2,1,0:T(8,128)(2,1)} %get-tuple-element.60.refs_2_, bf16[16,128,128]{2,1,0:T(8,128)(2,1)} %refs_3_.1, ...), custom_call_target="tpu_custom_call" | custom-call | flops 1000000000 | bytes 8912896 | tf_op jit(solution)/shard_map/pallas_call | solution.py:61
  132.0 9.6 %all-to-all-done.2.refs_0_ = bf16[16,5,16,384]{3,2,1,0:T(8,128)(2,1)S(1)} async-done(((bf16[16,5,16,384]{3,2,1,0:T(8,128)(2,1)}), bf16[16,5,16,384]{3,2,1,0:T(8,128)(2,1)S(1)}, u32[]{:S(2)}, u32[]{:S(2)}) %all-to-all-start.2) | async-done | bytes 983072 | tf_op jit(solution)/shard_map/all_to_all | solution.py:339
  142.5 9.6 %shard_map.111 = (bf16[16,128,256]{2,1,0:T(8,128)(2,1)}, bf16[384,256]{1,0:T(8,128)(2,1)}) custom-call(s32[16,2]{1,0:T(8,128)} %copy.16.cols.refs_0_, s32[8,2]{1,0:T(8,128)} %copy.17.sep_cols.refs_1_, s32[1]{0:T(128)} %bitcast.1.refs_0_.core, s32[1]{0:T(128)} %bitcast.2.own_level, bf16[16,5,16,384]{3,2,1,0:T(8,128)(2,1)} %copy-done.2, ...), custom_call_target="tpu_custom_call" | custom-call | flops 1000000000 | bytes 11075584 | tf_op jit(solution)/shard_map/pallas_call | solution.py:61
  (94 shorter events, 32.4 us)
Async XLA Ops:
  3.0 8.7 %collective-permute-start = (bf16[192,384]{1,0:T(8,128)(2,1)}, bf16[192,384]{1,0:T(8,128)(2,1)S(1)}, u32[]{:S(2)}, u32[]{:S(2)}) collective-permute-start(bf16[192,384]{1,0:T(8,128)(2,1)} %get-tuple-element.34), channel_id=1, source_target_pairs={{0,2},{2,0},{4,6},{6,4},{8,10},{10,8},{12,14},{14,12},{16,18},{18,... | collective-permute-start | bytes 442376 | tf_op jit(solution)/shard_map/ppermute | solution.py:331
  11.8 9.2 %collective-permute-start.12 = (bf16[192,384]{1,0:T(8,128)(2,1)S(1)}, bf16[192,384]{1,0:T(8,128)(2,1)S(1)}, u32[]{:S(2)}, u32[]{:S(2)}) collective-permute-start(bf16[192,384]{1,0:T(8,128)(2,1)S(1)} %copy-done.12), channel_id=1, source_target_pairs={{0,2},{2,0},{4,6},{6,4},{8,10},{10,8},{12,14},{14,12},{16,18},{18,... | collective-permute-start | bytes 442376 | tf_op jit(solution)/shard_map/ppermute | solution.py:331
  19.5 5.2 %collective-permute-start.1 = (bf16[192,384]{1,0:T(8,128)(2,1)S(1)}, bf16[192,384]{1,0:T(8,128)(2,1)S(1)}, u32[]{:S(2)}, u32[]{:S(2)}) collective-permute-start(bf16[192,384]{1,0:T(8,128)(2,1)S(1)} %get-tuple-element.37), channel_id=1, source_target_pairs={{0,6},{2,4},{4,2},{6,0},{8,14},{10,12},{12,10},{14,8},{16,22},{18,... | collective-permute-start | bytes 442376 | tf_op jit(solution)/shard_map/ppermute | solution.py:331
  24.8 5.2 %collective-permute-start.13 = (bf16[192,384]{1,0:T(8,128)(2,1)S(1)}, bf16[192,384]{1,0:T(8,128)(2,1)S(1)}, u32[]{:S(2)}, u32[]{:S(2)}) collective-permute-start(bf16[192,384]{1,0:T(8,128)(2,1)S(1)} %get-tuple-element.53), channel_id=1, source_target_pairs={{0,6},{2,4},{4,2},{6,0},{8,14},{10,12},{12,10},{14,8},{16,22},{18,... | collective-permute-start | bytes 442376 | tf_op jit(solution)/shard_map/ppermute | solution.py:331
  26.8 5.5 %collective-permute-start.2 = (bf16[192,384]{1,0:T(8,128)(2,1)S(1)}, bf16[192,384]{1,0:T(8,128)(2,1)S(1)}, u32[]{:S(2)}, u32[]{:S(2)}) collective-permute-start(bf16[192,384]{1,0:T(8,128)(2,1)S(1)} %get-tuple-element.39), channel_id=1, source_target_pairs={{0,8},{2,10},{4,12},{6,14},{8,0},{10,2},{12,4},{14,6},{16,24},{18,... | collective-permute-start | bytes 442376 | tf_op jit(solution)/shard_map/ppermute | solution.py:331
  32.3 5.2 %collective-permute-start.14 = (bf16[192,384]{1,0:T(8,128)(2,1)S(1)}, bf16[192,384]{1,0:T(8,128)(2,1)S(1)}, u32[]{:S(2)}, u32[]{:S(2)}) collective-permute-start(bf16[192,384]{1,0:T(8,128)(2,1)S(1)} %get-tuple-element.54), channel_id=1, source_target_pairs={{0,8},{2,10},{4,12},{6,14},{8,0},{10,2},{12,4},{14,6},{16,24},{18,... | collective-permute-start | bytes 442376 | tf_op jit(solution)/shard_map/ppermute | solution.py:331
  34.6 6.4 %collective-permute-start.5 = (bf16[192,384]{1,0:T(8,128)(2,1)S(1)}, bf16[192,384]{1,0:T(8,128)(2,1)S(1)}, u32[]{:S(2)}, u32[]{:S(2)}) collective-permute-start(bf16[192,384]{1,0:T(8,128)(2,1)S(1)} %get-tuple-element.78), channel_id=1, source_target_pairs={{0,24},{2,26},{4,28},{6,30},{8,16},{10,18},{12,20},{14,22},{16,8},... | collective-permute-start | bytes 442376 | tf_op jit(solution)/shard_map/ppermute | solution.py:331
  36.8 10.9 %collective-permute-start.3 = (bf16[3,192,384]{2,1,0:T(8,128)(2,1)S(1)}, bf16[3,192,384]{2,1,0:T(8,128)(2,1)S(1)}, u32[]{:S(2)}, u32[]{:S(2)}) collective-permute-start(bf16[3,192,384]{2,1,0:T(8,128)(2,1)S(1)} %pad_maximum_fusion.1.refs_2_.refs_3_), channel_id=1, source_target_pairs={{0,1},{1,0},{2,3},{3,2},{4,5},{5,4},{6,7},{7,6},{8,9},{9,8},{10,11... | collective-permute-start | bytes 1327112 | tf_op jit(solution)/shard_map/ppermute | solution.py:275
  41.0 6.6 %collective-permute-start.15 = (bf16[192,384]{1,0:T(8,128)(2,1)S(1)}, bf16[192,384]{1,0:T(8,128)(2,1)S(1)}, u32[]{:S(2)}, u32[]{:S(2)}) collective-permute-start(bf16[192,384]{1,0:T(8,128)(2,1)S(1)} %get-tuple-element.55), channel_id=1, source_target_pairs={{0,24},{2,26},{4,28},{6,30},{8,16},{10,18},{12,20},{14,22},{16,8},... | collective-permute-start | bytes 442376 | tf_op jit(solution)/shard_map/ppermute | solution.py:331
  45.6 13.9 %collective-permute-start.6 = (bf16[192,384]{1,0:T(8,128)(2,1)S(1)}, bf16[192,384]{1,0:T(8,128)(2,1)S(1)}, u32[]{:S(2)}, u32[]{:S(2)}) collective-permute-start(bf16[192,384]{1,0:T(8,128)(2,1)S(1)} %get-tuple-element.73), channel_id=1, source_target_pairs={{0,32},{2,34},{4,36},{6,38},{8,40},{10,42},{12,44},{14,46},{16,48}... | collective-permute-start | bytes 442376 | tf_op jit(solution)/shard_map/ppermute | solution.py:331
  52.6 18.1 %all-to-all-start = ((bf16[16,5,16,384]{3,2,1,0:T(8,128)(2,1)}), bf16[16,5,16,384]{3,2,1,0:T(8,128)(2,1)S(1)}, u32[]{:S(2)}, u32[]{:S(2)}) async-start(bf16[16,5,16,384]{3,2,1,0:T(8,128)(2,1)} %get-tuple-element.40), calls=%async_computation | async-start | bytes 1966080 | tf_op jit(solution)/shard_map/all_to_all | solution.py:339
  59.6 5.4 %collective-permute-start.16 = (bf16[192,384]{1,0:T(8,128)(2,1)S(1)}, bf16[192,384]{1,0:T(8,128)(2,1)S(1)}, u32[]{:S(2)}, u32[]{:S(2)}) collective-permute-start(bf16[192,384]{1,0:T(8,128)(2,1)S(1)} %broadcast_select_fusion.4), channel_id=1, source_target_pairs={{0,32},{2,34},{4,36},{6,38},{8,40},{10,42},{12,44},{14,46},{16,48}... | collective-permute-start | bytes 442376 | tf_op jit(solution)/shard_map/ppermute | solution.py:331
  62.2 7.1 %collective-permute-start.7 = (bf16[192,384]{1,0:T(8,128)(2,1)S(1)}, bf16[192,384]{1,0:T(8,128)(2,1)S(1)}, u32[]{:S(2)}, u32[]{:S(2)}) collective-permute-start(bf16[192,384]{1,0:T(8,128)(2,1)S(1)} %get-tuple-element.44), channel_id=1, source_target_pairs={{0,96},{2,98},{4,100},{6,102},{8,104},{10,106},{12,108},{14,110},{... | collective-permute-start | bytes 442376 | tf_op jit(solution)/shard_map/ppermute | solution.py:331
  70.7 9.9 %collective-permute-start.17 = (bf16[192,384]{1,0:T(8,128)(2,1)S(1)}, bf16[192,384]{1,0:T(8,128)(2,1)S(1)}, u32[]{:S(2)}, u32[]{:S(2)}) collective-permute-start(bf16[192,384]{1,0:T(8,128)(2,1)S(1)} %broadcast_select_fusion.2), channel_id=1, source_target_pairs={{0,96},{2,98},{4,100},{6,102},{8,104},{10,106},{12,108},{14,110},{... | collective-permute-start | bytes 442376 | tf_op jit(solution)/shard_map/ppermute | solution.py:331
  76.0 7.8 %collective-permute-start.8 = (bf16[192,384]{1,0:T(8,128)(2,1)S(1)}, bf16[192,384]{1,0:T(8,128)(2,1)S(1)}, u32[]{:S(2)}, u32[]{:S(2)}) collective-permute-start(bf16[192,384]{1,0:T(8,128)(2,1)S(1)} %get-tuple-element.45), channel_id=1, source_target_pairs={{0,224},{2,226},{4,228},{6,230},{8,232},{10,234},{12,236},{14,238}... | collective-permute-start | bytes 442376 | tf_op jit(solution)/shard_map/ppermute | solution.py:331
  79.2 9.9 %collective-permute-start.4 = (bf16[3,256,384]{2,1,0:T(8,128)(2,1)S(1)}, bf16[3,256,384]{2,1,0:T(8,128)(2,1)S(1)}, u32[]{:S(2)}, u32[]{:S(2)}) collective-permute-start(bf16[3,256,384]{2,1,0:T(8,128)(2,1)S(1)} %copy-done.8), channel_id=1, source_target_pairs={{0,2},{2,0},{4,6},{6,4},{8,10},{10,8},{12,14},{14,12},{16,18},{18,... | collective-permute-start | bytes 1769480 | tf_op jit(solution)/shard_map/ppermute | solution.py:408
  80.7 9.0 %collective-permute-start.18 = (bf16[192,384]{1,0:T(8,128)(2,1)S(1)}, bf16[192,384]{1,0:T(8,128)(2,1)S(1)}, u32[]{:S(2)}, u32[]{:S(2)}) collective-permute-start(bf16[192,384]{1,0:T(8,128)(2,1)S(1)} %broadcast_select_fusion), channel_id=1, source_target_pairs={{0,224},{2,226},{4,228},{6,230},{8,232},{10,234},{12,236},{14,238}... | collective-permute-start | bytes 442376 | tf_op jit(solution)/shard_map/ppermute | solution.py:331
  83.9 7.2 %collective-permute-start.9 = (bf16[4,192,384]{2,1,0:T(8,128)(2,1)S(1)}, bf16[4,192,384]{2,1,0:T(8,128)(2,1)S(1)}, u32[]{:S(2)}, u32[]{:S(2)}) collective-permute-start(bf16[4,192,384]{2,1,0:T(8,128)(2,1)S(1)} %pad_maximum_fusion.refs_2_.refs_1_), channel_id=1, source_target_pairs={{0,1},{1,0},{2,3},{3,2},{4,5},{5,4},{6,7},{7,6},{8,9},{9,8},{10,11... | collective-permute-start | bytes 1769480 | tf_op jit(solution)/shard_map/ppermute | solution.py:275
  89.3 10.3 %collective-permute-start.10 = (bf16[2,256,384]{2,1,0:T(8,128)(2,1)S(1)}, bf16[2,256,384]{2,1,0:T(8,128)(2,1)S(1)}, u32[]{:S(2)}, u32[]{:S(2)}) collective-permute-start(bf16[2,256,384]{2,1,0:T(8,128)(2,1)S(1)} %slice.73), channel_id=1, source_target_pairs={{0,6},{2,4},{4,2},{6,0},{8,14},{10,12},{12,10},{14,8},{16,22},{18,... | collective-permute-start | bytes 1179656 | tf_op jit(solution)/shard_map/ppermute | solution.py:408
  91.1 23.9 %collective-permute-start.19 = (bf16[5,192,384]{2,1,0:T(8,128)(2,1)}, bf16[5,192,384]{2,1,0:T(8,128)(2,1)}, u32[]{:S(2)}, u32[]{:S(2)}) collective-permute-start(bf16[5,192,384]{2,1,0:T(8,128)(2,1)} %bitcast_dynamic-update-slice_fusion.refs_4_), channel_id=1, source_target_pairs={{0,1},{1,0},{2,3},{3,2},{4,5},{5,4},{6,7},{7,6},{8,9},{9,8},{10,11... | collective-permute-start | bytes 2211848 | tf_op jit(solution)/shard_map/ppermute | solution.py:275
  95.0 20.0 %all-to-all-start.1 = ((bf16[8,4,16,384]{3,2,1,0:T(8,128)(2,1)}), bf16[8,4,16,384]{3,2,1,0:T(8,128)(2,1)S(1)}, u32[]{:S(2)}, u32[]{:S(2)}) async-start(bf16[8,4,16,384]{3,2,1,0:T(8,128)(2,1)} %get-tuple-element.46), calls=%async_computation.1 | async-start | bytes 786432 | tf_op jit(solution)/shard_map/all_to_all | solution.py:339
  99.8 7.1 %collective-permute-start.11 = (bf16[1,256,384]{2,1,0:T(8,128)(2,1)S(1)}, bf16[1,256,384]{2,1,0:T(8,128)(2,1)S(1)}, u32[]{:S(2)}, u32[]{:S(2)}) collective-permute-start(bf16[1,256,384]{2,1,0:T(8,128)(2,1)S(1)} %slice.74), channel_id=1, source_target_pairs={{0,8},{2,10},{4,12},{6,14},{8,0},{10,2},{12,4},{14,6},{16,24},{18,... | collective-permute-start | bytes 589832 | tf_op jit(solution)/shard_map/ppermute | solution.py:408
  118.6 22.9 %all-to-all-start.2 = ((bf16[16,5,16,384]{3,2,1,0:T(8,128)(2,1)}), bf16[16,5,16,384]{3,2,1,0:T(8,128)(2,1)S(1)}, u32[]{:S(2)}, u32[]{:S(2)}) async-start(bf16[16,5,16,384]{3,2,1,0:T(8,128)(2,1)} %shard_map.109), calls=%async_computation.2 | async-start | bytes 1966080 | tf_op jit(solution)/shard_map/all_to_all | solution.py:339
  125.8 6.2 %collective-permute-start.20 = (bf16[3,192,384]{2,1,0:T(8,128)(2,1)S(1)}, bf16[3,192,384]{2,1,0:T(8,128)(2,1)S(1)}, u32[]{:S(2)}, u32[]{:S(2)}) collective-permute-start(bf16[3,192,384]{2,1,0:T(8,128)(2,1)S(1)} %pad_maximum_fusion.2.refs_5_), channel_id=1, source_target_pairs={{0,1},{1,0},{2,3},{3,2},{4,5},{5,4},{6,7},{7,6},{8,9},{9,8},{10,11... | collective-permute-start | bytes 1327112 | tf_op jit(solution)/shard_map/ppermute | solution.py:275
  (16 other events, 123.4 us)

commit v7 on v5

--- a/solution.py
+++ b/solution.py
@@ -389,7 +389,7 @@
     for bit in range(2, LOW):
         both(bit)
     gains_low = with_other_core(flags[:LOW], gain_list)
-    both(LOW)
+    both(LOW, solved)
     both(LOW + 1)
     low, shares = in_vmem(
         path_kernel,
@@ -408,7 +408,8 @@
         return added(value, lax.ppermute(value, "blk", [(i, i ^ mask) for i in range(size)]))
 
     low1 = swapped(after(low, arrived), 0)
-    both(LOW + 3, arrived)
+    finish_low = with_other_core(flags[:LOW], finish_list[:LOW])
+    both(LOW + 3, (arrived, finish_low))
     gains_high = with_other_core(flags[LOW:bits], gain_list[LOW:])
     climb_finish(bits - 1)
     finish_list.append((finish, finish))
@@ -428,7 +429,6 @@
         [core, (device >> PLANE_BITS)[None]],
         [arrived, fourth, *finish_high],
     )
-    finish_low = with_other_core(flags[:LOW], finish_list[:LOW])
     start, chain, couple = in_vmem(
         prepare_kernel,
         [

time: 152 us -> 159 us (1.046)
  waiting for transfers between devices: 43.4 us -> 53.6 us
  starting transfers between devices: 51.5 us -> 49.8 us
    ppermute x14, waiting for transfers between devices: 15.9 us -> 24.3 us  [climb(): arrived = lax.ppermute(top, 'blk', [(i, i ^ mask) for i in range(size)])]
    all_to_all x3, waiting for transfers between devices: 17.8 us -> 21.6 us  [within(): lax.all_to_all(value, 'blk', 0, 0, axis_index_groups=members, tiled=True)]
    ppermute x3, waiting for transfers between devices: 9.57 us -> 7.68 us  [swapped(): lax.ppermute(value, 'blk', [(i, i ^ mask) for i in range(size)])]
  transfers between devices with their start and end apart: 24 -> 24, of which waited for: 12 -> 14; matrix products, arithmetic and copies ran while one was open for 5% -> 5% of each run, Pallas kernels for 16% -> 15%
where the time goes in v7:
time: 159 us
  waiting for transfers between devices  53.6 us (34%)
  starting transfers between devices  49.8 us (31%)
  Pallas kernels  38.6 us (24%)
  local copies, waits for them, and re-layouts  5.78 us (4%)
  between operations  5.72 us (4%)
  other arithmetic  5.17 us (3%)
    pallas_call x8, Pallas kernels, placed(): pl.pallas_call(kernel, out_shape=tuple(outs), in_specs=[smem] * len(scala...  38.6 us
    ppermute x14, starting transfers between devices, climb(): arrived = lax.ppermute(top, 'blk', [(i, i ^ mask) for i in range(size)])  29.4 us
    ppermute x14, waiting for transfers between devices, climb(): arrived = lax.ppermute(top, 'blk', [(i, i ^ mask) for i in range(size)])  24.3 us
    all_to_all x3, waiting for transfers between devices, within(): lax.all_to_all(value, 'blk', 0, 0, axis_index_groups=members, tiled=True)  21.6 us
    all_to_all x3, starting transfers between devices, within(): lax.all_to_all(value, 'blk', 0, 0, axis_index_groups=members, tiled=True)  17.1 us
    ppermute x3, waiting for transfers between devices, swapped(): lax.ppermute(value, 'blk', [(i, i ^ mask) for i in range(size)])  7.68 us
    unnamed x35, local copies, waits for them, and re-layouts  4.37 us
  transfers between devices with their start and end apart: 24, of which 14 were waited for; matrix products, arithmetic and copies ran while one was open for 5% of the time, Pallas kernels for 15%

profile of v7, /device:TPU:8, one launch (start us, length us, event | category | flops | bytes accessed | tf_op | source)
XLA Modules:
  0.0 158.7 jit_solution(4359229801808576572)
XLA Ops:
  0.6 2.3 %shard_map.104 = (bf16[192,384]{1,0:T(8,128)(2,1)}, bf16[192,384]{1,0:T(8,128)(2,1)}) custom-call(s32[1]{0:T(128)} %bitcast.1.refs_0_.core, bf16[384,384]{1,0:T(8,128)(2,1)} %bitcast.50, bf16[384,384]{1,0:T(8,128)(2,1)} %bitcast.51), custom_call_target="tpu_custom_call" | custom-call | flops 1000000000 | bytes 884736 | tf_op jit(solution)/shard_map/pallas_call | solution.py:61
  7.3 4.4 %shard_map.105.refs_5_ = bf16[8,128,256]{2,1,0:T(8,128)(2,1)} custom-call(s32[16,2]{1,0:T(8,128)} %copy.16.cols.refs_0_, bf16[16,128,128]{2,1,0:T(8,128)(2,1)} %refs_3_.1, bf16[16,2,128,128]{3,2,1,0:T(8,128)(2,1)} %refs_4_.1, bf16[16,128,256]{2,1,0:T(8,128)(2,1)} %refs_2_.2), custom_call_target="tpu_custom_call" | custom-call | flops 1000000000 | bytes 3145728 | tf_op jit(solution)/shard_map/pallas_call | solution.py:61
  14.1 3.0 %collective-permute-done.8 = bf16[192,384]{1,0:T(8,128)(2,1)S(1)} collective-permute-done((bf16[192,384]{1,0:T(8,128)(2,1)S(1)}, bf16[192,384]{1,0:T(8,128)(2,1)S(1)}, u32[]{:S(2)}, u32[]{:S(2)}) %collective-permute-start.8) | collective-permute-done | bytes 147488 | tf_op jit(solution)/shard_map/ppermute | solution.py:331
  20.6 6.4 %shard_map.106 = (bf16[16,128,256]{2,1,0:T(8,128)(2,1)}, f32[8,384,256]{2,1,0:T(8,128)}) custom-call(s32[16,2]{1,0:T(8,128)} %copy.16.cols.refs_0_, s32[8,2]{1,0:T(8,128)} %copy.17.sep_cols.refs_1_, s32[1]{0:T(128)} %bitcast.2.own_level, bf16[16,128,128]{2,1,0:T(8,128)(2,1)} %refs_3_.1, bf16[16,2,128,128]{3,2,1,0:T(8,128)(2,1)} %refs_4_.1, ...), custom_call_target="tpu_custom_call" | custom-call | flops 1000000000 | bytes 9109504 | tf_op jit(solution)/shard_map/pallas_call | solution.py:61
  28.7 3.9 %collective-permute-done.2 = bf16[192,384]{1,0:T(8,128)(2,1)S(1)} collective-permute-done((bf16[192,384]{1,0:T(8,128)(2,1)S(1)}, bf16[192,384]{1,0:T(8,128)(2,1)S(1)}, u32[]{:S(2)}, u32[]{:S(2)}) %collective-permute-start.2) | collective-permute-done | bytes 147488 | tf_op jit(solution)/shard_map/ppermute | solution.py:331
  37.8 4.7 %collective-permute-done.5 = bf16[192,384]{1,0:T(8,128)(2,1)S(1)} collective-permute-done((bf16[192,384]{1,0:T(8,128)(2,1)S(1)}, bf16[192,384]{1,0:T(8,128)(2,1)S(1)}, u32[]{:S(2)}, u32[]{:S(2)}) %collective-permute-start.5) | collective-permute-done | bytes 147488 | tf_op jit(solution)/shard_map/ppermute | solution.py:331
  50.1 4.0 %shard_map.107 = (bf16[3,256,384]{2,1,0:T(8,128)(2,1)}, bf16[16,5,16,384]{3,2,1,0:T(8,128)(2,1)}) custom-call(s32[1]{0:T(128)} %bitcast.1.refs_0_.core, f32[8,384,256]{2,1,0:T(8,128)} %get-tuple-element.36.refs_1_, bf16[3,192,384]{2,1,0:T(8,128)(2,1)} %copy-done.1, bf16[3,192,384]{2,1,0:T(8,128)(2,1)} %copy-done.5), custom_call_target="tpu_custom_call" | custom-call | flops 1000000000 | bytes 5603328 | tf_op jit(solution)/shard_map/pallas_call | solution.py:61
  54.1 6.9 %all-to-all-start = ((bf16[16,5,16,384]{3,2,1,0:T(8,128)(2,1)}), bf16[16,5,16,384]{3,2,1,0:T(8,128)(2,1)S(1)}, u32[]{:S(2)}, u32[]{:S(2)}) async-start(bf16[16,5,16,384]{3,2,1,0:T(8,128)(2,1)} %get-tuple-element.38), calls=%async_computation | async-start | bytes 1966080 | tf_op jit(solution)/shard_map/all_to_all | solution.py:339
  63.8 2.8 %collective-permute-start.7 = (bf16[192,384]{1,0:T(8,128)(2,1)S(1)}, bf16[192,384]{1,0:T(8,128)(2,1)S(1)}, u32[]{:S(2)}, u32[]{:S(2)}) collective-permute-start(bf16[192,384]{1,0:T(8,128)(2,1)S(1)} %get-tuple-element.44), channel_id=1, source_target_pairs={{0,96},{2,98},{4,100},{6,102},{8,104},{10,106},{12,108},{14,110},{... | collective-permute-start | bytes 442376 | tf_op jit(solution)/shard_map/ppermute | solution.py:331
  66.7 5.9 %collective-permute-done.7 = bf16[192,384]{1,0:T(8,128)(2,1)S(1)} collective-permute-done((bf16[192,384]{1,0:T(8,128)(2,1)S(1)}, bf16[192,384]{1,0:T(8,128)(2,1)S(1)}, u32[]{:S(2)}, u32[]{:S(2)}) %collective-permute-start.7) | collective-permute-done | bytes 147488 | tf_op jit(solution)/shard_map/ppermute | solution.py:331
  72.7 4.5 %all-to-all-done.refs_1_ = bf16[16,5,16,384]{3,2,1,0:T(8,128)(2,1)S(1)} async-done(((bf16[16,5,16,384]{3,2,1,0:T(8,128)(2,1)}), bf16[16,5,16,384]{3,2,1,0:T(8,128)(2,1)S(1)}, u32[]{:S(2)}, u32[]{:S(2)}) %all-to-all-start) | async-done | bytes 983072 | tf_op jit(solution)/shard_map/all_to_all | solution.py:339
  77.2 2.7 %collective-permute-start.18 = (bf16[192,384]{1,0:T(8,128)(2,1)S(1)}, bf16[192,384]{1,0:T(8,128)(2,1)S(1)}, u32[]{:S(2)}, u32[]{:S(2)}) collective-permute-start(bf16[192,384]{1,0:T(8,128)(2,1)S(1)} %broadcast_select_fusion.2), channel_id=1, source_target_pairs={{0,96},{2,98},{4,100},{6,102},{8,104},{10,106},{12,108},{14,110},{... | collective-permute-start | bytes 442376 | tf_op jit(solution)/shard_map/ppermute | solution.py:331
  80.6 3.7 %collective-permute-start.12 = (bf16[192,384]{1,0:T(8,128)(2,1)S(1)}, bf16[192,384]{1,0:T(8,128)(2,1)S(1)}, u32[]{:S(2)}, u32[]{:S(2)}) collective-permute-start(bf16[192,384]{1,0:T(8,128)(2,1)S(1)} %get-tuple-element.51), channel_id=1, source_target_pairs={{0,224},{2,226},{4,228},{6,230},{8,232},{10,234},{12,236},{14,238}... | collective-permute-start | bytes 442376 | tf_op jit(solution)/shard_map/ppermute | solution.py:331
  85.9 3.2 %collective-permute-start.19 = (bf16[192,384]{1,0:T(8,128)(2,1)S(1)}, bf16[192,384]{1,0:T(8,128)(2,1)S(1)}, u32[]{:S(2)}, u32[]{:S(2)}) collective-permute-start(bf16[192,384]{1,0:T(8,128)(2,1)S(1)} %broadcast_select_fusion), channel_id=1, source_target_pairs={{0,224},{2,226},{4,228},{6,230},{8,232},{10,234},{12,236},{14,238}... | collective-permute-start | bytes 442376 | tf_op jit(solution)/shard_map/ppermute | solution.py:331
  89.1 5.0 %collective-permute-done.12 = bf16[192,384]{1,0:T(8,128)(2,1)S(1)} collective-permute-done((bf16[192,384]{1,0:T(8,128)(2,1)S(1)}, bf16[192,384]{1,0:T(8,128)(2,1)S(1)}, u32[]{:S(2)}, u32[]{:S(2)}) %collective-permute-start.12) | collective-permute-done | bytes 147488 | tf_op jit(solution)/shard_map/ppermute | solution.py:331
  99.8 3.0 %shard_map.108 = (bf16[16,384]{1,0:T(8,128)(2,1)}, bf16[8,4,16,384]{3,2,1,0:T(8,128)(2,1)}) custom-call(s32[1]{0:T(128)} %bitcast.1.refs_0_.core, bf16[16,5,16,384]{3,2,1,0:T(8,128)(2,1)} %copy-done.7, bf16[4,192,384]{2,1,0:T(8,128)(2,1)} %copy-done.4, bf16[4,192,384]{2,1,0:T(8,128)(2,1)} %copy-done.9), custom_call_target="tpu_custom_call" | custom-call | flops 1000000000 | bytes 2568192 | tf_op jit(solution)/shard_map/pallas_call | solution.py:61
  102.9 4.0 %all-to-all-start.1 = ((bf16[8,4,16,384]{3,2,1,0:T(8,128)(2,1)}), bf16[8,4,16,384]{3,2,1,0:T(8,128)(2,1)S(1)}, u32[]{:S(2)}, u32[]{:S(2)}) async-start(bf16[8,4,16,384]{3,2,1,0:T(8,128)(2,1)} %get-tuple-element.52), calls=%async_computation.1 | async-start | bytes 786432 | tf_op jit(solution)/shard_map/all_to_all | solution.py:339
  107.8 6.2 %collective-permute-done.15 = bf16[1,256,384]{2,1,0:T(8,128)(2,1)S(1)} collective-permute-done((bf16[1,256,384]{2,1,0:T(8,128)(2,1)S(1)}, bf16[1,256,384]{2,1,0:T(8,128)(2,1)S(1)}, u32[]{:S(2)}, u32[]{:S(2)}) %collective-permute-start.15) | collective-permute-done | bytes 196640 | tf_op jit(solution)/shard_map/ppermute | solution.py:408
  114.8 7.3 %all-to-all-done.1.refs_2_ = bf16[8,4,16,384]{3,2,1,0:T(8,128)(2,1)S(1)} async-done(((bf16[8,4,16,384]{3,2,1,0:T(8,128)(2,1)}), bf16[8,4,16,384]{3,2,1,0:T(8,128)(2,1)S(1)}, u32[]{:S(2)}, u32[]{:S(2)}) %all-to-all-start.1) | async-done | bytes 393248 | tf_op jit(solution)/shard_map/all_to_all | solution.py:339
  123.1 2.8 %shard_map.109 = bf16[16,5,16,384]{3,2,1,0:T(8,128)(2,1)} custom-call(s32[1]{0:T(128)} %bitcast.1.refs_0_.core, s32[1]{0:T(128)} %bitcast.3.refs_1_, bf16[8,4,16,384]{3,2,1,0:T(8,128)(2,1)} %copy-done.11, bf16[16,384]{1,0:T(8,128)(2,1)} %get-tuple-element.54.refs_3_, bf16[5,192,384]{2,1,0:T(8,128)(2,1)} %bitcast_dynamic-update-slice_fusion.refs_4_, ...), custom_call_target="tpu_custom_call" | custom-call | flops 1000000000 | bytes 2863104 | tf_op jit(solution)/shard_map/pallas_call | solution.py:61
  126.0 6.2 %all-to-all-start.2 = ((bf16[16,5,16,384]{3,2,1,0:T(8,128)(2,1)}), bf16[16,5,16,384]{3,2,1,0:T(8,128)(2,1)S(1)}, u32[]{:S(2)}, u32[]{:S(2)}) async-start(bf16[16,5,16,384]{3,2,1,0:T(8,128)(2,1)} %shard_map.109), calls=%async_computation.2 | async-start | bytes 1966080 | tf_op jit(solution)/shard_map/all_to_all | solution.py:339
  132.2 6.1 %shard_map.110 = (f32[16,128,256]{2,1,0:T(8,128)}, bf16[16,2,128,128]{3,2,1,0:T(8,128)(2,1)}, bf16[8,2,128,384]{3,2,1,0:T(8,128)(2,1)}) custom-call(s32[16,2]{1,0:T(8,128)} %copy.16.cols.refs_0_, s32[8,2]{1,0:T(8,128)} %copy.17.sep_cols.refs_1_, bf16[16,128,256]{2,1,0:T(8,128)(2,1)} %get-tuple-element.60.refs_2_, bf16[16,128,128]{2,1,0:T(8,128)(2,1)} %refs_3_.1, ...), custom_call_target="tpu_custom_call" | custom-call | flops 1000000000 | bytes 8912896 | tf_op jit(solution)/shard_map/pallas_call | solution.py:61
  138.3 9.8 %all-to-all-done.2.refs_0_ = bf16[16,5,16,384]{3,2,1,0:T(8,128)(2,1)S(1)} async-done(((bf16[16,5,16,384]{3,2,1,0:T(8,128)(2,1)}), bf16[16,5,16,384]{3,2,1,0:T(8,128)(2,1)S(1)}, u32[]{:S(2)}, u32[]{:S(2)}) %all-to-all-start.2) | async-done | bytes 983072 | tf_op jit(solution)/shard_map/all_to_all | solution.py:339
  149.0 9.6 %shard_map.111 = (bf16[16,128,256]{2,1,0:T(8,128)(2,1)}, bf16[384,256]{1,0:T(8,128)(2,1)}) custom-call(s32[16,2]{1,0:T(8,128)} %copy.16.cols.refs_0_, s32[8,2]{1,0:T(8,128)} %copy.17.sep_cols.refs_1_, s32[1]{0:T(128)} %bitcast.1.refs_0_.core, s32[1]{0:T(128)} %bitcast.2.own_level, bf16[16,5,16,384]{3,2,1,0:T(8,128)(2,1)} %copy-done.2, ...), custom_call_target="tpu_custom_call" | custom-call | flops 1000000000 | bytes 11075584 | tf_op jit(solution)/shard_map/pallas_call | solution.py:61
  (96 shorter events, 34.5 us)
Async XLA Ops:
  3.0 8.8 %collective-permute-start = (bf16[192,384]{1,0:T(8,128)(2,1)}, bf16[192,384]{1,0:T(8,128)(2,1)S(1)}, u32[]{:S(2)}, u32[]{:S(2)}) collective-permute-start(bf16[192,384]{1,0:T(8,128)(2,1)} %get-tuple-element.34), channel_id=1, source_target_pairs={{0,2},{2,0},{4,6},{6,4},{8,10},{10,8},{12,14},{14,12},{16,18},{18,... | collective-permute-start | bytes 442376 | tf_op jit(solution)/shard_map/ppermute | solution.py:331
  11.8 5.2 %collective-permute-start.8 = (bf16[192,384]{1,0:T(8,128)(2,1)S(1)}, bf16[192,384]{1,0:T(8,128)(2,1)S(1)}, u32[]{:S(2)}, u32[]{:S(2)}) collective-permute-start(bf16[192,384]{1,0:T(8,128)(2,1)S(1)} %copy-done.12), channel_id=1, source_target_pairs={{0,2},{2,0},{4,6},{6,4},{8,10},{10,8},{12,14},{14,12},{16,18},{18,... | collective-permute-start | bytes 442376 | tf_op jit(solution)/shard_map/ppermute | solution.py:331
  12.6 5.2 %collective-permute-start.1 = (bf16[192,384]{1,0:T(8,128)(2,1)S(1)}, bf16[192,384]{1,0:T(8,128)(2,1)S(1)}, u32[]{:S(2)}, u32[]{:S(2)}) collective-permute-start(bf16[192,384]{1,0:T(8,128)(2,1)S(1)} %get-tuple-element.37), channel_id=1, source_target_pairs={{0,6},{2,4},{4,2},{6,0},{8,14},{10,12},{12,10},{14,8},{16,22},{18,... | collective-permute-start | bytes 442376 | tf_op jit(solution)/shard_map/ppermute | solution.py:331
  17.8 10.8 %collective-permute-start.9 = (bf16[192,384]{1,0:T(8,128)(2,1)S(1)}, bf16[192,384]{1,0:T(8,128)(2,1)S(1)}, u32[]{:S(2)}, u32[]{:S(2)}) collective-permute-start(bf16[192,384]{1,0:T(8,128)(2,1)S(1)} %get-tuple-element.48), channel_id=1, source_target_pairs={{0,6},{2,4},{4,2},{6,0},{8,14},{10,12},{12,10},{14,8},{16,22},{18,... | collective-permute-start | bytes 442376 | tf_op jit(solution)/shard_map/ppermute | solution.py:331
  27.0 5.5 %collective-permute-start.2 = (bf16[192,384]{1,0:T(8,128)(2,1)S(1)}, bf16[192,384]{1,0:T(8,128)(2,1)S(1)}, u32[]{:S(2)}, u32[]{:S(2)}) collective-permute-start(bf16[192,384]{1,0:T(8,128)(2,1)S(1)} %get-tuple-element.83), channel_id=1, source_target_pairs={{0,8},{2,10},{4,12},{6,14},{8,0},{10,2},{12,4},{14,6},{16,24},{18,... | collective-permute-start | bytes 442376 | tf_op jit(solution)/shard_map/ppermute | solution.py:331
  32.5 5.2 %collective-permute-start.10 = (bf16[192,384]{1,0:T(8,128)(2,1)S(1)}, bf16[192,384]{1,0:T(8,128)(2,1)S(1)}, u32[]{:S(2)}, u32[]{:S(2)}) collective-permute-start(bf16[192,384]{1,0:T(8,128)(2,1)S(1)} %get-tuple-element.50), channel_id=1, source_target_pairs={{0,8},{2,10},{4,12},{6,14},{8,0},{10,2},{12,4},{14,6},{16,24},{18,... | collective-permute-start | bytes 442376 | tf_op jit(solution)/shard_map/ppermute | solution.py:331
  34.9 14.3 %collective-permute-start.3 = (bf16[3,192,384]{2,1,0:T(8,128)(2,1)S(1)}, bf16[3,192,384]{2,1,0:T(8,128)(2,1)S(1)}, u32[]{:S(2)}, u32[]{:S(2)}) collective-permute-start(bf16[3,192,384]{2,1,0:T(8,128)(2,1)S(1)} %pad_maximum_fusion.1.refs_2_.refs_3_), channel_id=1, source_target_pairs={{0,1},{1,0},{2,3},{3,2},{4,5},{5,4},{6,7},{7,6},{8,9},{9,8},{10,11... | collective-permute-start | bytes 1327112 | tf_op jit(solution)/shard_map/ppermute | solution.py:275
  35.0 7.5 %collective-permute-start.5 = (bf16[192,384]{1,0:T(8,128)(2,1)S(1)}, bf16[192,384]{1,0:T(8,128)(2,1)S(1)}, u32[]{:S(2)}, u32[]{:S(2)}) collective-permute-start(bf16[192,384]{1,0:T(8,128)(2,1)S(1)} %get-tuple-element.43), channel_id=1, source_target_pairs={{0,24},{2,26},{4,28},{6,30},{8,16},{10,18},{12,20},{14,22},{16,8},... | collective-permute-start | bytes 442376 | tf_op jit(solution)/shard_map/ppermute | solution.py:331
  42.5 6.7 %collective-permute-start.16 = (bf16[192,384]{1,0:T(8,128)(2,1)S(1)}, bf16[192,384]{1,0:T(8,128)(2,1)S(1)}, u32[]{:S(2)}, u32[]{:S(2)}) collective-permute-start(bf16[192,384]{1,0:T(8,128)(2,1)S(1)} %get-tuple-element.55), channel_id=1, source_target_pairs={{0,24},{2,26},{4,28},{6,30},{8,16},{10,18},{12,20},{14,22},{16,8},... | collective-permute-start | bytes 442376 | tf_op jit(solution)/shard_map/ppermute | solution.py:331
  46.6 14.4 %collective-permute-start.6 = (bf16[192,384]{1,0:T(8,128)(2,1)S(1)}, bf16[192,384]{1,0:T(8,128)(2,1)S(1)}, u32[]{:S(2)}, u32[]{:S(2)}) collective-permute-start(bf16[192,384]{1,0:T(8,128)(2,1)S(1)} %get-tuple-element.69), channel_id=1, source_target_pairs={{0,32},{2,34},{4,36},{6,38},{8,40},{10,42},{12,44},{14,46},{16,48}... | collective-permute-start | bytes 442376 | tf_op jit(solution)/shard_map/ppermute | solution.py:331
  48.7 24.0 %collective-permute-start.11 = (bf16[3,192,384]{2,1,0:T(8,128)(2,1)S(1)}, bf16[3,192,384]{2,1,0:T(8,128)(2,1)S(1)}, u32[]{:S(2)}, u32[]{:S(2)}) collective-permute-start(bf16[3,192,384]{2,1,0:T(8,128)(2,1)S(1)} %pad_maximum_fusion.2.refs_5_), channel_id=1, source_target_pairs={{0,1},{1,0},{2,3},{3,2},{4,5},{5,4},{6,7},{7,6},{8,9},{9,8},{10,11... | collective-permute-start | bytes 1327112 | tf_op jit(solution)/shard_map/ppermute | solution.py:275
  54.1 23.1 %all-to-all-start = ((bf16[16,5,16,384]{3,2,1,0:T(8,128)(2,1)}), bf16[16,5,16,384]{3,2,1,0:T(8,128)(2,1)S(1)}, u32[]{:S(2)}, u32[]{:S(2)}) async-start(bf16[16,5,16,384]{3,2,1,0:T(8,128)(2,1)} %get-tuple-element.38), calls=%async_computation | async-start | bytes 1966080 | tf_op jit(solution)/shard_map/all_to_all | solution.py:339
  61.1 5.6 %collective-permute-start.17 = (bf16[192,384]{1,0:T(8,128)(2,1)S(1)}, bf16[192,384]{1,0:T(8,128)(2,1)S(1)}, u32[]{:S(2)}, u32[]{:S(2)}) collective-permute-start(bf16[192,384]{1,0:T(8,128)(2,1)S(1)} %broadcast_select_fusion.4), channel_id=1, source_target_pairs={{0,32},{2,34},{4,36},{6,38},{8,40},{10,42},{12,44},{14,46},{16,48}... | collective-permute-start | bytes 442376 | tf_op jit(solution)/shard_map/ppermute | solution.py:331
  63.8 8.9 %collective-permute-start.7 = (bf16[192,384]{1,0:T(8,128)(2,1)S(1)}, bf16[192,384]{1,0:T(8,128)(2,1)S(1)}, u32[]{:S(2)}, u32[]{:S(2)}) collective-permute-start(bf16[192,384]{1,0:T(8,128)(2,1)S(1)} %get-tuple-element.44), channel_id=1, source_target_pairs={{0,96},{2,98},{4,100},{6,102},{8,104},{10,106},{12,108},{14,110},{... | collective-permute-start | bytes 442376 | tf_op jit(solution)/shard_map/ppermute | solution.py:331
  77.2 8.7 %collective-permute-start.18 = (bf16[192,384]{1,0:T(8,128)(2,1)S(1)}, bf16[192,384]{1,0:T(8,128)(2,1)S(1)}, u32[]{:S(2)}, u32[]{:S(2)}) collective-permute-start(bf16[192,384]{1,0:T(8,128)(2,1)S(1)} %broadcast_select_fusion.2), channel_id=1, source_target_pairs={{0,96},{2,98},{4,100},{6,102},{8,104},{10,106},{12,108},{14,110},{... | collective-permute-start | bytes 442376 | tf_op jit(solution)/shard_map/ppermute | solution.py:331
  80.6 13.5 %collective-permute-start.12 = (bf16[192,384]{1,0:T(8,128)(2,1)S(1)}, bf16[192,384]{1,0:T(8,128)(2,1)S(1)}, u32[]{:S(2)}, u32[]{:S(2)}) collective-permute-start(bf16[192,384]{1,0:T(8,128)(2,1)S(1)} %get-tuple-element.51), channel_id=1, source_target_pairs={{0,224},{2,226},{4,228},{6,230},{8,232},{10,234},{12,236},{14,238}... | collective-permute-start | bytes 442376 | tf_op jit(solution)/shard_map/ppermute | solution.py:331
  84.4 12.2 %collective-permute-start.4 = (bf16[3,256,384]{2,1,0:T(8,128)(2,1)S(1)}, bf16[3,256,384]{2,1,0:T(8,128)(2,1)S(1)}, u32[]{:S(2)}, u32[]{:S(2)}) collective-permute-start(bf16[3,256,384]{2,1,0:T(8,128)(2,1)S(1)} %copy-done.8), channel_id=1, source_target_pairs={{0,2},{2,0},{4,6},{6,4},{8,10},{10,8},{12,14},{14,12},{16,18},{18,... | collective-permute-start | bytes 1769480 | tf_op jit(solution)/shard_map/ppermute | solution.py:408
  85.9 11.7 %collective-permute-start.19 = (bf16[192,384]{1,0:T(8,128)(2,1)S(1)}, bf16[192,384]{1,0:T(8,128)(2,1)S(1)}, u32[]{:S(2)}, u32[]{:S(2)}) collective-permute-start(bf16[192,384]{1,0:T(8,128)(2,1)S(1)} %broadcast_select_fusion), channel_id=1, source_target_pairs={{0,224},{2,226},{4,228},{6,230},{8,232},{10,234},{12,236},{14,238}... | collective-permute-start | bytes 442376 | tf_op jit(solution)/shard_map/ppermute | solution.py:331
  94.3 4.7 %collective-permute-start.13 = (bf16[4,192,384]{2,1,0:T(8,128)(2,1)S(1)}, bf16[4,192,384]{2,1,0:T(8,128)(2,1)S(1)}, u32[]{:S(2)}, u32[]{:S(2)}) collective-permute-start(bf16[4,192,384]{2,1,0:T(8,128)(2,1)S(1)} %pad_maximum_fusion.refs_2_.refs_1_), channel_id=1, source_target_pairs={{0,1},{1,0},{2,3},{3,2},{4,5},{5,4},{6,7},{7,6},{8,9},{9,8},{10,11... | collective-permute-start | bytes 1769480 | tf_op jit(solution)/shard_map/ppermute | solution.py:275
  96.8 10.1 %collective-permute-start.14 = (bf16[2,256,384]{2,1,0:T(8,128)(2,1)S(1)}, bf16[2,256,384]{2,1,0:T(8,128)(2,1)S(1)}, u32[]{:S(2)}, u32[]{:S(2)}) collective-permute-start(bf16[2,256,384]{2,1,0:T(8,128)(2,1)S(1)} %slice.73), channel_id=1, source_target_pairs={{0,6},{2,4},{4,2},{6,0},{8,14},{10,12},{12,10},{14,8},{16,22},{18,... | collective-permute-start | bytes 1179656 | tf_op jit(solution)/shard_map/ppermute | solution.py:408
  99.0 23.2 %collective-permute-start.20 = (bf16[5,192,384]{2,1,0:T(8,128)(2,1)}, bf16[5,192,384]{2,1,0:T(8,128)(2,1)S(1)}, u32[]{:S(2)}, u32[]{:S(2)}) collective-permute-start(bf16[5,192,384]{2,1,0:T(8,128)(2,1)} %bitcast_dynamic-update-slice_fusion.refs_4_), channel_id=1, source_target_pairs={{0,1},{1,0},{2,3},{3,2},{4,5},{5,4},{6,7},{7,6},{8,9},{9,8},{10,11... | collective-permute-start | bytes 2211848 | tf_op jit(solution)/shard_map/ppermute | solution.py:275
  102.9 19.3 %all-to-all-start.1 = ((bf16[8,4,16,384]{3,2,1,0:T(8,128)(2,1)}), bf16[8,4,16,384]{3,2,1,0:T(8,128)(2,1)S(1)}, u32[]{:S(2)}, u32[]{:S(2)}) async-start(bf16[8,4,16,384]{3,2,1,0:T(8,128)(2,1)} %get-tuple-element.52), calls=%async_computation.1 | async-start | bytes 786432 | tf_op jit(solution)/shard_map/all_to_all | solution.py:339
  107.0 7.0 %collective-permute-start.15 = (bf16[1,256,384]{2,1,0:T(8,128)(2,1)S(1)}, bf16[1,256,384]{2,1,0:T(8,128)(2,1)S(1)}, u32[]{:S(2)}, u32[]{:S(2)}) collective-permute-start(bf16[1,256,384]{2,1,0:T(8,128)(2,1)S(1)} %slice.74), channel_id=1, source_target_pairs={{0,8},{2,10},{4,12},{6,14},{8,0},{10,2},{12,4},{14,6},{16,24},{18,... | collective-permute-start | bytes 589832 | tf_op jit(solution)/shard_map/ppermute | solution.py:408
  126.0 22.0 %all-to-all-start.2 = ((bf16[16,5,16,384]{3,2,1,0:T(8,128)(2,1)}), bf16[16,5,16,384]{3,2,1,0:T(8,128)(2,1)S(1)}, u32[]{:S(2)}, u32[]{:S(2)}) async-start(bf16[16,5,16,384]{3,2,1,0:T(8,128)(2,1)} %shard_map.109), calls=%async_computation.2 | async-start | bytes 1966080 | tf_op jit(solution)/shard_map/all_to_all | solution.py:339
  (17 other events, 135.9 us)

commit v8 on v4

--- a/solution.py
+++ b/solution.py
@@ -429,7 +429,7 @@
         mask = step_mask(bit)
         return added(value, lax.ppermute(value, "blk", [(i, i ^ mask) for i in range(size)]))
 
-    low1 = swapped(low, 0)
+    low1 = swapped(after(low, arrived), 0)
     low2 = swapped(low1[1:], 1)
     low3 = swapped(low2[1:], 2)
     gain_list[-1] = after(gain_list[-1], arrived)
@@ -441,9 +441,9 @@
         plane_kernel,
         [shaped(piece, BF16), shaped((size // plane, bits - LOW, *piece), BF16)],
         [core],
-        [after(arrived, (low3, finish)), *gains_high],
-    )
-    arrived = within(above, towers)
+        [arrived, *gains_high],
+    )
+    arrived = after(within(above, towers), low3)
     matrix = (sep_width, sep_width)
     (spread,) = placed(
         top_kernel,

time: 157 us -> 150 us (0.955)
  waiting for transfers between devices: 45.9 us -> 32.3 us
  starting transfers between devices: 57.5 us -> 60.5 us
  other arithmetic: 2.38 us -> 4.46 us
    all_to_all x3, waiting for transfers between devices: 16.5 us -> 8.9 us  [within(): lax.all_to_all(value, 'blk', 0, 0, axis_index_groups=members, tiled=True)]
    ppermute x3, waiting for transfers between devices: 9.63 us -> 2.55 us  [swapped(): lax.ppermute(value, 'blk', [(i, i ^ mask) for i in range(size)])]
    all_to_all x3, starting transfers between devices: 18.7 us -> 22.2 us  [within(): lax.all_to_all(value, 'blk', 0, 0, axis_index_groups=members, tiled=True)]
    convert_element_type x3, other arithmetic: 0.97 us -> 3.02 us  [added(): return (mine.astype(F32) + other.astype(F32)).astype(BF16)]
    unnamed x55 -> x53, local copies, waits for them, and re-layouts: 4.17 us -> 4.13 us
  transfers between devices with their start and end apart: 22 -> 22, of which waited for: 9 -> 8; matrix products, arithmetic and copies ran while one was open for 3% -> 5% of each run, Pallas kernels for 13% -> 16%
where the time goes in v8:
time: 150 us; the launch traced here: 149 us
  starting transfers between devices  60.5 us (40%)
  Pallas kernels  39.3 us (26%)
  waiting for transfers between devices  32.3 us (22%)
  local copies, waits for them, and re-layouts  6.95 us (5%)
  between operations  5.62 us (4%)
  other arithmetic  4.46 us (3%)
    pallas_call x8, Pallas kernels, placed(): pl.pallas_call(kernel, out_shape=tuple(outs), in_specs=[smem] * len(scala...  39.3 us
    ppermute x14, starting transfers between devices, climb(): arrived = lax.ppermute(top, 'blk', [(i, i ^ mask) for i in range(size)])  33.7 us
    all_to_all x3, starting transfers between devices, within(): lax.all_to_all(value, 'blk', 0, 0, axis_index_groups=members, tiled=True)  22.2 us
    ppermute x14, waiting for transfers between devices, climb(): arrived = lax.ppermute(top, 'blk', [(i, i ^ mask) for i in range(size)])  20.8 us
    all_to_all x3, waiting for transfers between devices, within(): lax.all_to_all(value, 'blk', 0, 0, axis_index_groups=members, tiled=True)  8.9 us
    ppermute x3, starting transfers between devices, swapped(): lax.ppermute(value, 'blk', [(i, i ^ mask) for i in range(size)])  4.35 us
    unnamed x53, local copies, waits for them, and re-layouts  4.13 us
    convert_element_type x3, other arithmetic, added(): return (mine.astype(F32) + other.astype(F32)).astype(BF16)  3.02 us
  transfers between devices with their start and end apart: 22, of which 8 were waited for; matrix products, arithmetic and copies ran while one was open for 5% of the time, Pallas kernels for 16%

profile of v8, /device:TPU:8, one launch (start us, length us, event | category | flops | bytes accessed | tf_op | source)
XLA Modules:
  0.0 149.2 jit_solution(4227564971519701235)
XLA Ops:
  0.6 2.3 %shard_map.104 = (bf16[192,384]{1,0:T(8,128)(2,1)}, bf16[384,384]{1,0:T(8,128)(2,1)}) custom-call(s32[1]{0:T(128)} %bitcast.1.refs_0_.core, bf16[384,384]{1,0:T(8,128)(2,1)} %bitcast.34, bf16[384,384]{1,0:T(8,128)(2,1)} %bitcast.35), custom_call_target="tpu_custom_call" | custom-call | flops 1000000000 | bytes 1032192 | tf_op jit(solution)/shard_map/pallas_call | solution.py:78
  3.0 2.3 %collective-permute-start = (bf16[192,384]{1,0:T(8,128)(2,1)}, bf16[192,384]{1,0:T(8,128)(2,1)S(1)}, u32[]{:S(2)}, u32[]{:S(2)}) collective-permute-start(bf16[192,384]{1,0:T(8,128)(2,1)} %get-tuple-element.29), channel_id=1, source_target_pairs={{0,2},{2,0},{4,6},{6,4},{8,10},{10,8},{12,14},{14,12},{16,18},{18,... | collective-permute-start | bytes 442376 | tf_op jit(solution)/shard_map/ppermute | solution.py:353
  7.3 4.4 %shard_map.105.refs_5_ = bf16[8,128,256]{2,1,0:T(8,128)(2,1)} custom-call(s32[16,2]{1,0:T(8,128)} %copy.16.cols.refs_0_, bf16[16,128,128]{2,1,0:T(8,128)(2,1)} %refs_3_.1, bf16[16,2,128,128]{3,2,1,0:T(8,128)(2,1)} %refs_4_.1, bf16[16,128,256]{2,1,0:T(8,128)(2,1)} %refs_2_.2), custom_call_target="tpu_custom_call" | custom-call | flops 1000000000 | bytes 3145728 | tf_op jit(solution)/shard_map/pallas_call | solution.py:78
  13.1 3.9 %collective-permute-done.1 = bf16[192,384]{1,0:T(8,128)(2,1)S(1)} collective-permute-done((bf16[192,384]{1,0:T(8,128)(2,1)S(1)}, bf16[192,384]{1,0:T(8,128)(2,1)S(1)}, u32[]{:S(2)}, u32[]{:S(2)}) %collective-permute-start.1) | collective-permute-done | bytes 147488 | tf_op jit(solution)/shard_map/ppermute | solution.py:353
  19.6 6.5 %shard_map.106 = (bf16[16,128,256]{2,1,0:T(8,128)(2,1)}, f32[8,384,256]{2,1,0:T(8,128)}) custom-call(s32[16,2]{1,0:T(8,128)} %copy.16.cols.refs_0_, s32[8,2]{1,0:T(8,128)} %copy.17.sep_cols.refs_1_, s32[1]{0:T(128)} %bitcast.2.own_level, bf16[16,128,128]{2,1,0:T(8,128)(2,1)} %refs_3_.1, bf16[16,2,128,128]{3,2,1,0:T(8,128)(2,1)} %refs_4_.1, ...), custom_call_target="tpu_custom_call" | custom-call | flops 1000000000 | bytes 9109504 | tf_op jit(solution)/shard_map/pallas_call | solution.py:78
  30.7 3.1 %collective-permute-done.12.refs_12_ = bf16[384,384]{1,0:T(8,128)(2,1)S(1)} collective-permute-done((bf16[384,384]{1,0:T(8,128)(2,1)S(1)}, bf16[384,384]{1,0:T(8,128)(2,1)S(1)}, u32[]{:S(2)}, u32[]{:S(2)}) %collective-permute-start.12) | collective-permute-done | bytes 294944 | tf_op jit(solution)/shard_map/ppermute | solution.py:353
  36.4 4.0 %shard_map.107 = (bf16[3,256,384]{2,1,0:T(8,128)(2,1)}, bf16[16,5,16,384]{3,2,1,0:T(8,128)(2,1)}) custom-call(s32[1]{0:T(128)} %bitcast.1.refs_0_.core, f32[8,384,256]{2,1,0:T(8,128)} %get-tuple-element.31.refs_1_, bf16[3,192,384]{2,1,0:T(8,128)(2,1)} %copy-done.1, bf16[3,192,384]{2,1,0:T(8,128)(2,1)} %copy-done.11), custom_call_target="tpu_custom_call" | custom-call | flops 1000000000 | bytes 5603328 | tf_op jit(solution)/shard_map/pallas_call | solution.py:78
  43.8 7.2 %all-to-all-start = ((bf16[16,5,16,384]{3,2,1,0:T(8,128)(2,1)}), bf16[16,5,16,384]{3,2,1,0:T(8,128)(2,1)}, u32[]{:S(2)}, u32[]{:S(2)}) async-start(bf16[16,5,16,384]{3,2,1,0:T(8,128)(2,1)} %get-tuple-element.33), calls=%async_computation | async-start | bytes 1966080 | tf_op jit(solution)/shard_map/all_to_all | solution.py:361
  51.0 4.6 %collective-permute-start.6 = (bf16[192,384]{1,0:T(8,128)(2,1)S(1)}, bf16[192,384]{1,0:T(8,128)(2,1)S(1)}, u32[]{:S(2)}, u32[]{:S(2)}) collective-permute-start(bf16[192,384]{1,0:T(8,128)(2,1)S(1)} %get-tuple-element.59), channel_id=1, source_target_pairs={{0,96},{2,98},{4,100},{6,102},{8,104},{10,106},{12,108},{14,110},{... | collective-permute-start | bytes 442376 | tf_op jit(solution)/shard_map/ppermute | solution.py:353
  55.7 2.8 %collective-permute-start.15 = (bf16[384,384]{1,0:T(8,128)(2,1)S(1)}, bf16[384,384]{1,0:T(8,128)(2,1)S(1)}, u32[]{:S(2)}, u32[]{:S(2)}) collective-permute-start(bf16[384,384]{1,0:T(8,128)(2,1)S(1)} %broadcast_select_fusion.6.refs_2_), channel_id=1, source_target_pairs={{0,24},{2,26},{4,28},{6,30},{8,16},{10,18},{12,20},{14,22},{16,8},... | collective-permute-start | bytes 884744 | tf_op jit(solution)/shard_map/ppermute | solution.py:353
  59.8 4.3 %collective-permute-start.7 = (bf16[192,384]{1,0:T(8,128)(2,1)S(1)}, bf16[192,384]{1,0:T(8,128)(2,1)S(1)}, u32[]{:S(2)}, u32[]{:S(2)}) collective-permute-start(bf16[192,384]{1,0:T(8,128)(2,1)S(1)} %get-tuple-element.36), channel_id=1, source_target_pairs={{0,224},{2,226},{4,228},{6,230},{8,232},{10,234},{12,236},{14,238}... | collective-permute-start | bytes 442376 | tf_op jit(solution)/shard_map/ppermute | solution.py:353
  64.1 3.6 %collective-permute-done.15.refs_3_ = bf16[384,384]{1,0:T(8,128)(2,1)S(1)} collective-permute-done((bf16[384,384]{1,0:T(8,128)(2,1)S(1)}, bf16[384,384]{1,0:T(8,128)(2,1)S(1)}, u32[]{:S(2)}, u32[]{:S(2)}) %collective-permute-start.15) | collective-permute-done | bytes 294944 | tf_op jit(solution)/shard_map/ppermute | solution.py:353
  69.8 5.3 %collective-permute-done.16.refs_5_ = bf16[384,384]{1,0:T(8,128)(2,1)S(1)} collective-permute-done((bf16[384,384]{1,0:T(8,128)(2,1)S(1)}, bf16[384,384]{1,0:T(8,128)(2,1)S(1)}, u32[]{:S(2)}, u32[]{:S(2)}) %collective-permute-start.16) | collective-permute-done | bytes 294944 | tf_op jit(solution)/shard_map/ppermute | solution.py:353
  75.2 3.4 %collective-permute-start.17 = (bf16[384,384]{1,0:T(8,128)(2,1)S(1)}, bf16[384,384]{1,0:T(8,128)(2,1)S(1)}, u32[]{:S(2)}, u32[]{:S(2)}) collective-permute-start(bf16[384,384]{1,0:T(8,128)(2,1)S(1)} %broadcast_select_fusion.2.refs_6_), channel_id=1, source_target_pairs={{0,96},{2,98},{4,100},{6,102},{8,104},{10,106},{12,108},{14,110},{... | collective-permute-start | bytes 884744 | tf_op jit(solution)/shard_map/ppermute | solution.py:353
  78.6 2.5 %collective-permute-done.9 = bf16[3,256,384]{2,1,0:T(8,128)(2,1)S(1)} collective-permute-done((bf16[3,256,384]{2,1,0:T(8,128)(2,1)}, bf16[3,256,384]{2,1,0:T(8,128)(2,1)S(1)}, u32[]{:S(2)}, u32[]{:S(2)}) %collective-permute-start.9) | collective-permute-done | bytes 589856 | tf_op jit(solution)/shard_map/ppermute | solution.py:430
  85.8 5.0 %collective-permute-start.18 = (bf16[384,384]{1,0:T(8,128)(2,1)S(1)}, bf16[384,384]{1,0:T(8,128)(2,1)S(1)}, u32[]{:S(2)}, u32[]{:S(2)}) collective-permute-start(bf16[384,384]{1,0:T(8,128)(2,1)S(1)} %broadcast_select_fusion.1.refs_8_), channel_id=1, source_target_pairs={{0,224},{2,226},{4,228},{6,230},{8,232},{10,234},{12,236},{14,238}... | collective-permute-start | bytes 884744 | tf_op jit(solution)/shard_map/ppermute | solution.py:353
  91.7 3.0 %shard_map.108 = (bf16[16,384]{1,0:T(8,128)(2,1)}, bf16[8,4,16,384]{3,2,1,0:T(8,128)(2,1)}) custom-call(s32[1]{0:T(128)} %bitcast.1.refs_0_.core, bf16[16,5,16,384]{3,2,1,0:T(8,128)(2,1)} %all-to-all-done.refs_1_, bf16[4,192,384]{2,1,0:T(8,128)(2,1)} %copy-done.10, bf16[4,192,384]{2,1,0:T(8,128)(2,1)} %copy-done.21), custom_call_target="tpu_custom_call" | custom-call | flops 1000000000 | bytes 2568192 | tf_op jit(solution)/shard_map/pallas_call | solution.py:78
  94.8 3.8 %all-to-all-start.1 = ((bf16[8,4,16,384]{3,2,1,0:T(8,128)(2,1)}), bf16[8,4,16,384]{3,2,1,0:T(8,128)(2,1)S(1)}, u32[]{:S(2)}, u32[]{:S(2)}) async-start(bf16[8,4,16,384]{3,2,1,0:T(8,128)(2,1)} %get-tuple-element.37), calls=%async_computation.1 | async-start | bytes 786432 | tf_op jit(solution)/shard_map/all_to_all | solution.py:361
  101.6 4.9 %collective-permute-done.18.refs_9_ = bf16[384,384]{1,0:T(8,128)(2,1)S(1)} collective-permute-done((bf16[384,384]{1,0:T(8,128)(2,1)S(1)}, bf16[384,384]{1,0:T(8,128)(2,1)S(1)}, u32[]{:S(2)}, u32[]{:S(2)}) %collective-permute-start.18) | collective-permute-done | bytes 294944 | tf_op jit(solution)/shard_map/ppermute | solution.py:353
  110.2 3.5 %shard_map.109 = bf16[16,5,16,384]{3,2,1,0:T(8,128)(2,1)} custom-call(s32[1]{0:T(128)} %bitcast.3.place, s32[5]{0:T(128)} %slice.53.flags, bf16[8,4,16,384]{3,2,1,0:T(8,128)(2,1)} %copy-done.12, bf16[16,384]{1,0:T(8,128)(2,1)} %get-tuple-element.41.refs_1_, bf16[384,384]{1,0:T(8,128)(2,1)} %copy-done.6, bf16[384,384]{1,0:T(8,128)(2,1)} %copy-done.17, ...), custom_call_target="tpu_custom_call" | custom-call | flops 1000000000 | bytes 4337664 | tf_op jit(solution)/shard_map/pallas_call | solution.py:78
  113.7 11.3 %all-to-all-start.2 = ((bf16[16,5,16,384]{3,2,1,0:T(8,128)(2,1)}), bf16[16,5,16,384]{3,2,1,0:T(8,128)(2,1)S(1)}, u32[]{:S(2)}, u32[]{:S(2)}) async-start(bf16[16,5,16,384]{3,2,1,0:T(8,128)(2,1)} %shard_map.109), calls=%async_computation.2 | async-start | bytes 1966080 | tf_op jit(solution)/shard_map/all_to_all | solution.py:361
  125.0 6.0 %shard_map.110 = (f32[16,128,256]{2,1,0:T(8,128)}, bf16[16,2,128,128]{3,2,1,0:T(8,128)(2,1)}, bf16[8,2,128,384]{3,2,1,0:T(8,128)(2,1)}) custom-call(s32[16,2]{1,0:T(8,128)} %copy.16.cols.refs_0_, s32[8,2]{1,0:T(8,128)} %copy.17.sep_cols.refs_1_, bf16[16,128,256]{2,1,0:T(8,128)(2,1)} %get-tuple-element.50.refs_2_, bf16[16,128,128]{2,1,0:T(8,128)(2,1)} %refs_3_.1, ...), custom_call_target="tpu_custom_call" | custom-call | flops 1000000000 | bytes 8912896 | tf_op jit(solution)/shard_map/pallas_call | solution.py:78
  131.1 7.4 %all-to-all-done.2.refs_0_ = bf16[16,5,16,384]{3,2,1,0:T(8,128)(2,1)S(1)} async-done(((bf16[16,5,16,384]{3,2,1,0:T(8,128)(2,1)}), bf16[16,5,16,384]{3,2,1,0:T(8,128)(2,1)S(1)}, u32[]{:S(2)}, u32[]{:S(2)}) %all-to-all-start.2) | async-done | bytes 983072 | tf_op jit(solution)/shard_map/all_to_all | solution.py:361
  139.4 9.6 %shard_map.111 = (bf16[16,128,256]{2,1,0:T(8,128)(2,1)}, bf16[384,256]{1,0:T(8,128)(2,1)}) custom-call(s32[16,2]{1,0:T(8,128)} %copy.16.cols.refs_0_, s32[8,2]{1,0:T(8,128)} %copy.17.sep_cols.refs_1_, s32[1]{0:T(128)} %bitcast.1.refs_0_.core, s32[1]{0:T(128)} %bitcast.2.own_level, s32[8]{0:T(128)} %copy-done.23, bf16[16,5,16,384]{3,2,1,0:T(8,128)(2,1)} %copy-done.2, ...), custom_call_target="tpu_custom_call" | custom-call | flops 1000000000 | bytes 11960320 | tf_op jit(solution)/shard_map/pallas_call | solution.py:78
  (106 shorter events, 28.8 us)
Async XLA Ops:
  3.0 8.8 %collective-permute-start = (bf16[192,384]{1,0:T(8,128)(2,1)}, bf16[192,384]{1,0:T(8,128)(2,1)S(1)}, u32[]{:S(2)}, u32[]{:S(2)}) collective-permute-start(bf16[192,384]{1,0:T(8,128)(2,1)} %get-tuple-element.29), channel_id=1, source_target_pairs={{0,2},{2,0},{4,6},{6,4},{8,10},{10,8},{12,14},{14,12},{16,18},{18,... | collective-permute-start | bytes 442376 | tf_op jit(solution)/shard_map/ppermute | solution.py:353
  5.2 80.0 %copy-start.23 = (s32[8]{0:T(128)}, s32[8]{0:T(128)S(1)}, u32[]{:S(2)}) copy-start(s32[8]{0:T(128)S(1)} %shift-right-arithmetic_and_fusion.flags) | copy-start | bytes 100
  11.8 5.2 %collective-permute-start.1 = (bf16[192,384]{1,0:T(8,128)(2,1)S(1)}, bf16[192,384]{1,0:T(8,128)(2,1)S(1)}, u32[]{:S(2)}, u32[]{:S(2)}) collective-permute-start(bf16[192,384]{1,0:T(8,128)(2,1)S(1)} %get-tuple-element.32), channel_id=1, source_target_pairs={{0,6},{2,4},{4,2},{6,0},{8,14},{10,12},{12,10},{14,8},{16,22},{18,... | collective-permute-start | bytes 442376 | tf_op jit(solution)/shard_map/ppermute | solution.py:353
  17.0 11.3 %collective-permute-start.2 = (bf16[192,384]{1,0:T(8,128)(2,1)S(1)}, bf16[192,384]{1,0:T(8,128)(2,1)S(1)}, u32[]{:S(2)}, u32[]{:S(2)}) collective-permute-start(bf16[192,384]{1,0:T(8,128)(2,1)S(1)} %get-tuple-element.67), channel_id=1, source_target_pairs={{0,8},{2,10},{4,12},{6,14},{8,0},{10,2},{12,4},{14,6},{16,24},{18,... | collective-permute-start | bytes 442376 | tf_op jit(solution)/shard_map/ppermute | solution.py:353
  26.1 7.7 %collective-permute-start.12 = (bf16[384,384]{1,0:T(8,128)(2,1)S(1)}, bf16[384,384]{1,0:T(8,128)(2,1)S(1)}, u32[]{:S(2)}, u32[]{:S(2)}) collective-permute-start(bf16[384,384]{1,0:T(8,128)(2,1)S(1)} %copy-done.13), channel_id=1, source_target_pairs={{0,2},{2,0},{4,6},{6,4},{8,10},{10,8},{12,14},{14,12},{16,18},{18,... | collective-permute-start | bytes 884744 | tf_op jit(solution)/shard_map/ppermute | solution.py:353
  28.4 7.2 %collective-permute-start.4 = (bf16[192,384]{1,0:T(8,128)(2,1)S(1)}, bf16[192,384]{1,0:T(8,128)(2,1)S(1)}, u32[]{:S(2)}, u32[]{:S(2)}) collective-permute-start(bf16[192,384]{1,0:T(8,128)(2,1)S(1)} %get-tuple-element.62), channel_id=1, source_target_pairs={{0,24},{2,26},{4,28},{6,30},{8,16},{10,18},{12,20},{14,22},{16,8},... | collective-permute-start | bytes 442376 | tf_op jit(solution)/shard_map/ppermute | solution.py:353
  30.6 5.0 %collective-permute-start.3 = (bf16[3,192,384]{2,1,0:T(8,128)(2,1)S(1)}, bf16[3,192,384]{2,1,0:T(8,128)(2,1)S(1)}, u32[]{:S(2)}, u32[]{:S(2)}) collective-permute-start(bf16[3,192,384]{2,1,0:T(8,128)(2,1)S(1)} %pad_maximum_fusion.1.refs_2_.refs_3_), channel_id=1, source_target_pairs={{0,1},{1,0},{2,3},{3,2},{4,5},{5,4},{6,7},{7,6},{8,9},{9,8},{10,11... | collective-permute-start | bytes 1327112 | tf_op jit(solution)/shard_map/ppermute | solution.py:298
  33.9 8.6 %collective-permute-start.13 = (bf16[384,384]{1,0:T(8,128)(2,1)S(1)}, bf16[384,384]{1,0:T(8,128)(2,1)S(1)}, u32[]{:S(2)}, u32[]{:S(2)}) collective-permute-start(bf16[384,384]{1,0:T(8,128)(2,1)S(1)} %broadcast_select_fusion.4.refs_13_), channel_id=1, source_target_pairs={{0,6},{2,4},{4,2},{6,0},{8,14},{10,12},{12,10},{14,8},{16,22},{18,... | collective-permute-start | bytes 884744 | tf_op jit(solution)/shard_map/ppermute | solution.py:353
  40.5 10.5 %collective-permute-start.5 = (bf16[192,384]{1,0:T(8,128)(2,1)S(1)}, bf16[192,384]{1,0:T(8,128)(2,1)S(1)}, u32[]{:S(2)}, u32[]{:S(2)}) collective-permute-start(bf16[192,384]{1,0:T(8,128)(2,1)S(1)} %get-tuple-element.34), channel_id=1, source_target_pairs={{0,32},{2,34},{4,36},{6,38},{8,40},{10,42},{12,44},{14,46},{16,48}... | collective-permute-start | bytes 442376 | tf_op jit(solution)/shard_map/ppermute | solution.py:353
  42.6 13.1 %collective-permute-start.14 = (bf16[384,384]{1,0:T(8,128)(2,1)S(1)}, bf16[384,384]{1,0:T(8,128)(2,1)S(1)}, u32[]{:S(2)}, u32[]{:S(2)}) collective-permute-start(bf16[384,384]{1,0:T(8,128)(2,1)S(1)} %broadcast_select_fusion.5.refs_15_), channel_id=1, source_target_pairs={{0,8},{2,10},{4,12},{6,14},{8,0},{10,2},{12,4},{14,6},{16,24},{18,... | collective-permute-start | bytes 884744 | tf_op jit(solution)/shard_map/ppermute | solution.py:353
  43.8 25.2 %all-to-all-start = ((bf16[16,5,16,384]{3,2,1,0:T(8,128)(2,1)}), bf16[16,5,16,384]{3,2,1,0:T(8,128)(2,1)}, u32[]{:S(2)}, u32[]{:S(2)}) async-start(bf16[16,5,16,384]{3,2,1,0:T(8,128)(2,1)} %get-tuple-element.33), calls=%async_computation | async-start | bytes 1966080 | tf_op jit(solution)/shard_map/all_to_all | solution.py:361
  51.0 8.8 %collective-permute-start.6 = (bf16[192,384]{1,0:T(8,128)(2,1)S(1)}, bf16[192,384]{1,0:T(8,128)(2,1)S(1)}, u32[]{:S(2)}, u32[]{:S(2)}) collective-permute-start(bf16[192,384]{1,0:T(8,128)(2,1)S(1)} %get-tuple-element.59), channel_id=1, source_target_pairs={{0,96},{2,98},{4,100},{6,102},{8,104},{10,106},{12,108},{14,110},{... | collective-permute-start | bytes 442376 | tf_op jit(solution)/shard_map/ppermute | solution.py:353
  55.7 12.0 %collective-permute-start.15 = (bf16[384,384]{1,0:T(8,128)(2,1)S(1)}, bf16[384,384]{1,0:T(8,128)(2,1)S(1)}, u32[]{:S(2)}, u32[]{:S(2)}) collective-permute-start(bf16[384,384]{1,0:T(8,128)(2,1)S(1)} %broadcast_select_fusion.6.refs_2_), channel_id=1, source_target_pairs={{0,24},{2,26},{4,28},{6,30},{8,16},{10,18},{12,20},{14,22},{16,8},... | collective-permute-start | bytes 884744 | tf_op jit(solution)/shard_map/ppermute | solution.py:353
  59.8 9.2 %collective-permute-start.7 = (bf16[192,384]{1,0:T(8,128)(2,1)S(1)}, bf16[192,384]{1,0:T(8,128)(2,1)S(1)}, u32[]{:S(2)}, u32[]{:S(2)}) collective-permute-start(bf16[192,384]{1,0:T(8,128)(2,1)S(1)} %get-tuple-element.36), channel_id=1, source_target_pairs={{0,224},{2,226},{4,228},{6,230},{8,232},{10,234},{12,236},{14,238}... | collective-permute-start | bytes 442376 | tf_op jit(solution)/shard_map/ppermute | solution.py:353
  67.8 7.3 %collective-permute-start.16 = (bf16[384,384]{1,0:T(8,128)(2,1)S(1)}, bf16[384,384]{1,0:T(8,128)(2,1)S(1)}, u32[]{:S(2)}, u32[]{:S(2)}) collective-permute-start(bf16[384,384]{1,0:T(8,128)(2,1)S(1)} %broadcast_select_fusion.3.refs_4_), channel_id=1, source_target_pairs={{0,32},{2,34},{4,36},{6,38},{8,40},{10,42},{12,44},{14,46},{16,48}... | collective-permute-start | bytes 884744 | tf_op jit(solution)/shard_map/ppermute | solution.py:353
  69.0 12.1 %collective-permute-start.9 = (bf16[3,256,384]{2,1,0:T(8,128)(2,1)}, bf16[3,256,384]{2,1,0:T(8,128)(2,1)S(1)}, u32[]{:S(2)}, u32[]{:S(2)}) collective-permute-start(bf16[3,256,384]{2,1,0:T(8,128)(2,1)} %get-tuple-element.39), channel_id=1, source_target_pairs={{0,2},{2,0},{4,6},{6,4},{8,10},{10,8},{12,14},{14,12},{16,18},{18,... | collective-permute-start | bytes 1769480 | tf_op jit(solution)/shard_map/ppermute | solution.py:430
  69.7 21.1 %collective-permute-start.8 = (bf16[4,192,384]{2,1,0:T(8,128)(2,1)S(1)}, bf16[4,192,384]{2,1,0:T(8,128)(2,1)S(1)}, u32[]{:S(2)}, u32[]{:S(2)}) collective-permute-start(bf16[4,192,384]{2,1,0:T(8,128)(2,1)S(1)} %pad_maximum_fusion.refs_2_.refs_1_), channel_id=1, source_target_pairs={{0,1},{1,0},{2,3},{3,2},{4,5},{5,4},{6,7},{7,6},{8,9},{9,8},{10,11... | collective-permute-start | bytes 1769480 | tf_op jit(solution)/shard_map/ppermute | solution.py:298
  75.2 10.6 %collective-permute-start.17 = (bf16[384,384]{1,0:T(8,128)(2,1)S(1)}, bf16[384,384]{1,0:T(8,128)(2,1)S(1)}, u32[]{:S(2)}, u32[]{:S(2)}) collective-permute-start(bf16[384,384]{1,0:T(8,128)(2,1)S(1)} %broadcast_select_fusion.2.refs_6_), channel_id=1, source_target_pairs={{0,96},{2,98},{4,100},{6,102},{8,104},{10,106},{12,108},{14,110},{... | collective-permute-start | bytes 884744 | tf_op jit(solution)/shard_map/ppermute | solution.py:353
  83.3 15.3 %collective-permute-start.10 = (bf16[2,256,384]{2,1,0:T(8,128)(2,1)}, bf16[2,256,384]{2,1,0:T(8,128)(2,1)}, u32[]{:S(2)}, u32[]{:S(2)}) collective-permute-start(bf16[2,256,384]{2,1,0:T(8,128)(2,1)} %slice.63), channel_id=1, source_target_pairs={{0,6},{2,4},{4,2},{6,0},{8,14},{10,12},{12,10},{14,8},{16,22},{18,... | collective-permute-start | bytes 1179656 | tf_op jit(solution)/shard_map/ppermute | solution.py:430
  85.8 20.6 %copy-start.9 = (bf16[384,384]{1,0:T(8,128)(2,1)}, bf16[384,384]{1,0:T(8,128)(2,1)S(1)}, u32[]{:S(2)}) copy-start(bf16[384,384]{1,0:T(8,128)(2,1)S(1)} %broadcast_select_fusion.1.refs_8_) | copy-start | bytes 884740
  85.8 20.6 %collective-permute-start.18 = (bf16[384,384]{1,0:T(8,128)(2,1)S(1)}, bf16[384,384]{1,0:T(8,128)(2,1)S(1)}, u32[]{:S(2)}, u32[]{:S(2)}) collective-permute-start(bf16[384,384]{1,0:T(8,128)(2,1)S(1)} %broadcast_select_fusion.1.refs_8_), channel_id=1, source_target_pairs={{0,224},{2,226},{4,228},{6,230},{8,232},{10,234},{12,236},{14,238}... | collective-permute-start | bytes 884744 | tf_op jit(solution)/shard_map/ppermute | solution.py:353
  94.8 14.7 %all-to-all-start.1 = ((bf16[8,4,16,384]{3,2,1,0:T(8,128)(2,1)}), bf16[8,4,16,384]{3,2,1,0:T(8,128)(2,1)S(1)}, u32[]{:S(2)}, u32[]{:S(2)}) async-start(bf16[8,4,16,384]{3,2,1,0:T(8,128)(2,1)} %get-tuple-element.37), calls=%async_computation.1 | async-start | bytes 786432 | tf_op jit(solution)/shard_map/all_to_all | solution.py:361
  99.7 7.6 %collective-permute-start.11 = (bf16[1,256,384]{2,1,0:T(8,128)(2,1)S(1)}, bf16[1,256,384]{2,1,0:T(8,128)(2,1)S(1)}, u32[]{:S(2)}, u32[]{:S(2)}) collective-permute-start(bf16[1,256,384]{2,1,0:T(8,128)(2,1)S(1)} %slice.64), channel_id=1, source_target_pairs={{0,8},{2,10},{4,12},{6,14},{8,0},{10,2},{12,4},{14,6},{16,24},{18,... | collective-permute-start | bytes 589832 | tf_op jit(solution)/shard_map/ppermute | solution.py:430
  113.7 24.8 %all-to-all-start.2 = ((bf16[16,5,16,384]{3,2,1,0:T(8,128)(2,1)}), bf16[16,5,16,384]{3,2,1,0:T(8,128)(2,1)S(1)}, u32[]{:S(2)}, u32[]{:S(2)}) async-start(bf16[16,5,16,384]{3,2,1,0:T(8,128)(2,1)} %shard_map.109), calls=%async_computation.2 | async-start | bytes 1966080 | tf_op jit(solution)/shard_map/all_to_all | solution.py:361
  (24 other events, 203.3 us)

commit v9 on v8

--- a/solution.py
+++ b/solution.py
@@ -430,8 +430,6 @@
         return added(value, lax.ppermute(value, "blk", [(i, i ^ mask) for i in range(size)]))
 
     low1 = swapped(after(low, arrived), 0)
-    low2 = swapped(low1[1:], 1)
-    low3 = swapped(low2[1:], 2)
     gain_list[-1] = after(gain_list[-1], arrived)
     gains_high = with_other_core(flags[LOW:bits], gain_list[LOW:])
     finish = after(finish, gain)
@@ -443,7 +441,8 @@
         [core],
         [arrived, *gains_high],
     )
-    arrived = after(within(above, towers), low3)
+    low2 = swapped(after(low1[1:], above), 1)
+    arrived = after(within(above, towers), low2)
     matrix = (sep_width, sep_width)
     (spread,) = placed(
         top_kernel,
@@ -457,6 +456,7 @@
             pltpu.SemaphoreType.DMA((2 + count - LOW,)),
         ],
     )
+    low3 = swapped(after(low2[1:], spread), 2)
     start, chain, couple = in_vmem(
         prepare_kernel,
         [

time: 150 us -> 152 us (1.013)
  starting transfers between devices: 60.5 us -> 65.4 us
  other arithmetic: 4.46 us -> 2.39 us
    ppermute x3, waiting for transfers between devices: 2.55 us -> 11 us  [swapped(): lax.ppermute(value, 'blk', [(i, i ^ mask) for i in range(size)])]
    all_to_all x3, waiting for transfers between devices: 8.9 us -> 1.38 us  [within(): lax.all_to_all(value, 'blk', 0, 0, axis_index_groups=members, tiled=True)]
    ppermute x3, starting transfers between devices: 4.35 us -> 7.29 us  [swapped(): lax.ppermute(value, 'blk', [(i, i ^ mask) for i in range(size)])]
    all_to_all x3, starting transfers between devices: 22.2 us -> 24.4 us  [within(): lax.all_to_all(value, 'blk', 0, 0, axis_index_groups=members, tiled=True)]
    convert_element_type x3, other arithmetic: 3.02 us -> 0.97 us  [added(): return (mine.astype(F32) + other.astype(F32)).astype(BF16)]
    unnamed x53 -> x55, local copies, waits for them, and re-layouts: 4.13 us -> 4.1 us
  transfers between devices with their start and end apart: 22 -> 22, of which waited for: 8 -> 9; matrix products, arithmetic and copies ran while one was open for 5% -> 3% of each run, Pallas kernels for 16% -> 16%
where the time goes in v9:
time: 152 us; the launch traced here: 151 us
  starting transfers between devices  65.4 us (43%)
  Pallas kernels  39.4 us (26%)
  waiting for transfers between devices  32.3 us (21%)
  local copies, waits for them, and re-layouts  6.04 us (4%)
  between operations  5.57 us (4%)
  other arithmetic  2.39 us (2%)
    pallas_call x8, Pallas kernels, placed(): pl.pallas_call(kernel, out_shape=tuple(outs), in_specs=[smem] * len(scala...  39.4 us
    ppermute x14, starting transfers between devices, climb(): arrived = lax.ppermute(top, 'blk', [(i, i ^ mask) for i in range(size)])  33.3 us
    all_to_all x3, starting transfers between devices, within(): lax.all_to_all(value, 'blk', 0, 0, axis_index_groups=members, tiled=True)  24.4 us
    ppermute x14, waiting for transfers between devices, climb(): arrived = lax.ppermute(top, 'blk', [(i, i ^ mask) for i in range(size)])  19.9 us
    ppermute x3, waiting for transfers between devices, swapped(): lax.ppermute(value, 'blk', [(i, i ^ mask) for i in range(size)])  11 us
    ppermute x3, starting transfers between devices, swapped(): lax.ppermute(value, 'blk', [(i, i ^ mask) for i in range(size)])  7.29 us
    unnamed x55, local copies, waits for them, and re-layouts  4.1 us
  transfers between devices with their start and end apart: 22, of which 9 were waited for; matrix products, arithmetic and copies ran while one was open for 3% of the time, Pallas kernels for 16%

profile of v9, /device:TPU:8, one launch (start us, length us, event | category | flops | bytes accessed | tf_op | source)
XLA Modules:
  0.0 151.1 jit_solution(9797830171053573357)
XLA Ops:
  0.6 2.3 %shard_map.104 = (bf16[192,384]{1,0:T(8,128)(2,1)}, bf16[384,384]{1,0:T(8,128)(2,1)}) custom-call(s32[1]{0:T(128)} %bitcast.1.refs_0_.core, bf16[384,384]{1,0:T(8,128)(2,1)} %bitcast.34, bf16[384,384]{1,0:T(8,128)(2,1)} %bitcast.35), custom_call_target="tpu_custom_call" | custom-call | flops 1000000000 | bytes 1032192 | tf_op jit(solution)/shard_map/pallas_call | solution.py:78
  3.0 2.3 %collective-permute-start = (bf16[192,384]{1,0:T(8,128)(2,1)}, bf16[192,384]{1,0:T(8,128)(2,1)S(1)}, u32[]{:S(2)}, u32[]{:S(2)}) collective-permute-start(bf16[192,384]{1,0:T(8,128)(2,1)} %get-tuple-element.31), channel_id=1, source_target_pairs={{0,2},{2,0},{4,6},{6,4},{8,10},{10,8},{12,14},{14,12},{16,18},{18,... | collective-permute-start | bytes 442376 | tf_op jit(solution)/shard_map/ppermute | solution.py:353
  7.2 4.4 %shard_map.105.refs_5_ = bf16[8,128,256]{2,1,0:T(8,128)(2,1)} custom-call(s32[16,2]{1,0:T(8,128)} %copy.16.cols.refs_0_, bf16[16,128,128]{2,1,0:T(8,128)(2,1)} %refs_3_.1, bf16[16,2,128,128]{3,2,1,0:T(8,128)(2,1)} %refs_4_.1, bf16[16,128,256]{2,1,0:T(8,128)(2,1)} %refs_2_.2), custom_call_target="tpu_custom_call" | custom-call | flops 1000000000 | bytes 3145728 | tf_op jit(solution)/shard_map/pallas_call | solution.py:78
  13.1 3.8 %collective-permute-done.1 = bf16[192,384]{1,0:T(8,128)(2,1)S(1)} collective-permute-done((bf16[192,384]{1,0:T(8,128)(2,1)S(1)}, bf16[192,384]{1,0:T(8,128)(2,1)S(1)}, u32[]{:S(2)}, u32[]{:S(2)}) %collective-permute-start.1) | collective-permute-done | bytes 147488 | tf_op jit(solution)/shard_map/ppermute | solution.py:353
  19.6 6.5 %shard_map.106 = (bf16[16,128,256]{2,1,0:T(8,128)(2,1)}, f32[8,384,256]{2,1,0:T(8,128)}) custom-call(s32[16,2]{1,0:T(8,128)} %copy.16.cols.refs_0_, s32[8,2]{1,0:T(8,128)} %copy.17.sep_cols.refs_1_, s32[1]{0:T(128)} %bitcast.2.own_level, bf16[16,128,128]{2,1,0:T(8,128)(2,1)} %refs_3_.1, bf16[16,2,128,128]{3,2,1,0:T(8,128)(2,1)} %refs_4_.1, ...), custom_call_target="tpu_custom_call" | custom-call | flops 1000000000 | bytes 9109504 | tf_op jit(solution)/shard_map/pallas_call | solution.py:78
  30.7 3.2 %collective-permute-done.11.refs_12_ = bf16[384,384]{1,0:T(8,128)(2,1)S(1)} collective-permute-done((bf16[384,384]{1,0:T(8,128)(2,1)S(1)}, bf16[384,384]{1,0:T(8,128)(2,1)S(1)}, u32[]{:S(2)}, u32[]{:S(2)}) %collective-permute-start.11) | collective-permute-done | bytes 294944 | tf_op jit(solution)/shard_map/ppermute | solution.py:353
  36.4 4.1 %shard_map.107 = (bf16[3,256,384]{2,1,0:T(8,128)(2,1)}, bf16[16,5,16,384]{3,2,1,0:T(8,128)(2,1)}) custom-call(s32[1]{0:T(128)} %bitcast.1.refs_0_.core, f32[8,384,256]{2,1,0:T(8,128)} %get-tuple-element.33.refs_1_, bf16[3,192,384]{2,1,0:T(8,128)(2,1)} %copy-done.1, bf16[3,192,384]{2,1,0:T(8,128)(2,1)} %copy-done.11), custom_call_target="tpu_custom_call" | custom-call | flops 1000000000 | bytes 5603328 | tf_op jit(solution)/shard_map/pallas_call | solution.py:78
  43.7 7.2 %all-to-all-start = ((bf16[16,5,16,384]{3,2,1,0:T(8,128)(2,1)}), bf16[16,5,16,384]{3,2,1,0:T(8,128)(2,1)}, u32[]{:S(2)}, u32[]{:S(2)}) async-start(bf16[16,5,16,384]{3,2,1,0:T(8,128)(2,1)} %get-tuple-element.35), calls=%async_computation | async-start | bytes 1966080 | tf_op jit(solution)/shard_map/all_to_all | solution.py:361
  51.0 4.6 %collective-permute-start.6 = (bf16[192,384]{1,0:T(8,128)(2,1)S(1)}, bf16[192,384]{1,0:T(8,128)(2,1)S(1)}, u32[]{:S(2)}, u32[]{:S(2)}) collective-permute-start(bf16[192,384]{1,0:T(8,128)(2,1)S(1)} %get-tuple-element.63), channel_id=1, source_target_pairs={{0,96},{2,98},{4,100},{6,102},{8,104},{10,106},{12,108},{14,110},{... | collective-permute-start | bytes 442376 | tf_op jit(solution)/shard_map/ppermute | solution.py:353
  55.6 2.8 %collective-permute-start.14 = (bf16[384,384]{1,0:T(8,128)(2,1)S(1)}, bf16[384,384]{1,0:T(8,128)(2,1)S(1)}, u32[]{:S(2)}, u32[]{:S(2)}) collective-permute-start(bf16[384,384]{1,0:T(8,128)(2,1)S(1)} %broadcast_select_fusion.6.refs_2_), channel_id=1, source_target_pairs={{0,24},{2,26},{4,28},{6,30},{8,16},{10,18},{12,20},{14,22},{16,8},... | collective-permute-start | bytes 884744 | tf_op jit(solution)/shard_map/ppermute | solution.py:353
  59.7 4.2 %collective-permute-start.7 = (bf16[192,384]{1,0:T(8,128)(2,1)S(1)}, bf16[192,384]{1,0:T(8,128)(2,1)S(1)}, u32[]{:S(2)}, u32[]{:S(2)}) collective-permute-start(bf16[192,384]{1,0:T(8,128)(2,1)S(1)} %get-tuple-element.38), channel_id=1, source_target_pairs={{0,224},{2,226},{4,228},{6,230},{8,232},{10,234},{12,236},{14,238}... | collective-permute-start | bytes 442376 | tf_op jit(solution)/shard_map/ppermute | solution.py:353
  64.0 3.6 %collective-permute-done.14.refs_3_ = bf16[384,384]{1,0:T(8,128)(2,1)S(1)} collective-permute-done((bf16[384,384]{1,0:T(8,128)(2,1)S(1)}, bf16[384,384]{1,0:T(8,128)(2,1)S(1)}, u32[]{:S(2)}, u32[]{:S(2)}) %collective-permute-start.14) | collective-permute-done | bytes 294944 | tf_op jit(solution)/shard_map/ppermute | solution.py:353
  69.3 5.7 %collective-permute-done.15.refs_5_ = bf16[384,384]{1,0:T(8,128)(2,1)S(1)} collective-permute-done((bf16[384,384]{1,0:T(8,128)(2,1)S(1)}, bf16[384,384]{1,0:T(8,128)(2,1)S(1)}, u32[]{:S(2)}, u32[]{:S(2)}) %collective-permute-start.15) | collective-permute-done | bytes 294944 | tf_op jit(solution)/shard_map/ppermute | solution.py:353
  75.1 3.4 %collective-permute-start.16 = (bf16[384,384]{1,0:T(8,128)(2,1)S(1)}, bf16[384,384]{1,0:T(8,128)(2,1)S(1)}, u32[]{:S(2)}, u32[]{:S(2)}) collective-permute-start(bf16[384,384]{1,0:T(8,128)(2,1)S(1)} %broadcast_select_fusion.2.refs_6_), channel_id=1, source_target_pairs={{0,96},{2,98},{4,100},{6,102},{8,104},{10,106},{12,108},{14,110},{... | collective-permute-start | bytes 884744 | tf_op jit(solution)/shard_map/ppermute | solution.py:353
  78.5 3.7 %collective-permute-start.9 = (bf16[3,256,384]{2,1,0:T(8,128)(2,1)S(1)}, bf16[3,256,384]{2,1,0:T(8,128)(2,1)S(1)}, u32[]{:S(2)}, u32[]{:S(2)}) collective-permute-start(bf16[3,256,384]{2,1,0:T(8,128)(2,1)S(1)} %copy-done.22), channel_id=1, source_target_pairs={{0,2},{2,0},{4,6},{6,4},{8,10},{10,8},{12,14},{14,12},{16,18},{18,... | collective-permute-start | bytes 1769480 | tf_op jit(solution)/shard_map/ppermute | solution.py:430
  83.8 4.7 %collective-permute-start.17 = (bf16[384,384]{1,0:T(8,128)(2,1)S(1)}, bf16[384,384]{1,0:T(8,128)(2,1)S(1)}, u32[]{:S(2)}, u32[]{:S(2)}) collective-permute-start(bf16[384,384]{1,0:T(8,128)(2,1)S(1)} %broadcast_select_fusion.1.refs_8_), channel_id=1, source_target_pairs={{0,224},{2,226},{4,228},{6,230},{8,232},{10,234},{12,236},{14,238}... | collective-permute-start | bytes 884744 | tf_op jit(solution)/shard_map/ppermute | solution.py:353
  89.3 3.0 %shard_map.108 = (bf16[16,384]{1,0:T(8,128)(2,1)}, bf16[8,4,16,384]{3,2,1,0:T(8,128)(2,1)}) custom-call(s32[1]{0:T(128)} %bitcast.1.refs_0_.core, bf16[16,5,16,384]{3,2,1,0:T(8,128)(2,1)} %all-to-all-done.refs_1_, bf16[4,192,384]{2,1,0:T(8,128)(2,1)} %copy-done.10, bf16[4,192,384]{2,1,0:T(8,128)(2,1)} %copy-done.21), custom_call_target="tpu_custom_call" | custom-call | flops 1000000000 | bytes 2568192 | tf_op jit(solution)/shard_map/pallas_call | solution.py:78
  92.4 6.1 %all-to-all-start.1 = ((bf16[8,4,16,384]{3,2,1,0:T(8,128)(2,1)}), bf16[8,4,16,384]{3,2,1,0:T(8,128)(2,1)S(1)}, u32[]{:S(2)}, u32[]{:S(2)}) async-start(bf16[8,4,16,384]{3,2,1,0:T(8,128)(2,1)} %get-tuple-element.39), calls=%async_computation.1 | async-start | bytes 786432 | tf_op jit(solution)/shard_map/all_to_all | solution.py:361
  104.1 3.8 %collective-permute-done.10 = bf16[2,256,384]{2,1,0:T(8,128)(2,1)S(1)} collective-permute-done((bf16[2,256,384]{2,1,0:T(8,128)(2,1)S(1)}, bf16[2,256,384]{2,1,0:T(8,128)(2,1)S(1)}, u32[]{:S(2)}, u32[]{:S(2)}) %collective-permute-start.10) | collective-permute-done | bytes 393248 | tf_op jit(solution)/shard_map/ppermute | solution.py:430
  110.2 3.5 %shard_map.109 = bf16[16,5,16,384]{3,2,1,0:T(8,128)(2,1)} custom-call(s32[1]{0:T(128)} %bitcast.3.place, s32[5]{0:T(128)} %slice.53.flags, bf16[8,4,16,384]{3,2,1,0:T(8,128)(2,1)} %copy-done.12, bf16[16,384]{1,0:T(8,128)(2,1)} %get-tuple-element.44.refs_1_, bf16[384,384]{1,0:T(8,128)(2,1)} %copy-done.5, bf16[384,384]{1,0:T(8,128)(2,1)} %copy-done.17, ...), custom_call_target="tpu_custom_call" | custom-call | flops 1000000000 | bytes 4337664 | tf_op jit(solution)/shard_map/pallas_call | solution.py:78
  113.7 11.1 %all-to-all-start.2 = ((bf16[16,5,16,384]{3,2,1,0:T(8,128)(2,1)}), bf16[16,5,16,384]{3,2,1,0:T(8,128)(2,1)S(1)}, u32[]{:S(2)}, u32[]{:S(2)}) async-start(bf16[16,5,16,384]{3,2,1,0:T(8,128)(2,1)} %shard_map.109), calls=%async_computation.2 | async-start | bytes 1966080 | tf_op jit(solution)/shard_map/all_to_all | solution.py:361
  126.4 6.0 %shard_map.110 = (f32[16,128,256]{2,1,0:T(8,128)}, bf16[16,2,128,128]{3,2,1,0:T(8,128)(2,1)}, bf16[8,2,128,384]{3,2,1,0:T(8,128)(2,1)}) custom-call(s32[16,2]{1,0:T(8,128)} %copy.16.cols.refs_0_, s32[8,2]{1,0:T(8,128)} %copy.17.sep_cols.refs_1_, bf16[16,128,256]{2,1,0:T(8,128)(2,1)} %get-tuple-element.54.refs_2_, bf16[16,128,128]{2,1,0:T(8,128)(2,1)} %refs_3_.1, ...), custom_call_target="tpu_custom_call" | custom-call | flops 1000000000 | bytes 8912896 | tf_op jit(solution)/shard_map/pallas_call | solution.py:78
  132.5 7.2 %collective-permute-done.18 = bf16[1,256,384]{2,1,0:T(8,128)(2,1)S(1)} collective-permute-done((bf16[1,256,384]{2,1,0:T(8,128)(2,1)S(1)}, bf16[1,256,384]{2,1,0:T(8,128)(2,1)S(1)}, u32[]{:S(2)}, u32[]{:S(2)}) %collective-permute-start.18) | collective-permute-done | bytes 196640 | tf_op jit(solution)/shard_map/ppermute | solution.py:430
  141.3 9.6 %shard_map.111 = (bf16[16,128,256]{2,1,0:T(8,128)(2,1)}, bf16[384,256]{1,0:T(8,128)(2,1)}) custom-call(s32[16,2]{1,0:T(8,128)} %copy.16.cols.refs_0_, s32[8,2]{1,0:T(8,128)} %copy.17.sep_cols.refs_1_, s32[1]{0:T(128)} %bitcast.1.refs_0_.core, s32[1]{0:T(128)} %bitcast.2.own_level, s32[8]{0:T(128)} %copy-done.24, bf16[16,5,16,384]{3,2,1,0:T(8,128)(2,1)} %copy-done.2, ...), custom_call_target="tpu_custom_call" | custom-call | flops 1000000000 | bytes 11960320 | tf_op jit(solution)/shard_map/pallas_call | solution.py:78
  (108 shorter events, 28.7 us)
Async XLA Ops:
  3.0 8.7 %collective-permute-start = (bf16[192,384]{1,0:T(8,128)(2,1)}, bf16[192,384]{1,0:T(8,128)(2,1)S(1)}, u32[]{:S(2)}, u32[]{:S(2)}) collective-permute-start(bf16[192,384]{1,0:T(8,128)(2,1)} %get-tuple-element.31), channel_id=1, source_target_pairs={{0,2},{2,0},{4,6},{6,4},{8,10},{10,8},{12,14},{14,12},{16,18},{18,... | collective-permute-start | bytes 442376 | tf_op jit(solution)/shard_map/ppermute | solution.py:353
  5.2 95.4 %copy-start.24 = (s32[8]{0:T(128)}, s32[8]{0:T(128)S(1)}, u32[]{:S(2)}) copy-start(s32[8]{0:T(128)S(1)} %shift-right-arithmetic_and_fusion.flags) | copy-start | bytes 100
  11.7 5.2 %collective-permute-start.1 = (bf16[192,384]{1,0:T(8,128)(2,1)S(1)}, bf16[192,384]{1,0:T(8,128)(2,1)S(1)}, u32[]{:S(2)}, u32[]{:S(2)}) collective-permute-start(bf16[192,384]{1,0:T(8,128)(2,1)S(1)} %get-tuple-element.34), channel_id=1, source_target_pairs={{0,6},{2,4},{4,2},{6,0},{8,14},{10,12},{12,10},{14,8},{16,22},{18,... | collective-permute-start | bytes 442376 | tf_op jit(solution)/shard_map/ppermute | solution.py:353
  17.0 11.3 %collective-permute-start.2 = (bf16[192,384]{1,0:T(8,128)(2,1)S(1)}, bf16[192,384]{1,0:T(8,128)(2,1)S(1)}, u32[]{:S(2)}, u32[]{:S(2)}) collective-permute-start(bf16[192,384]{1,0:T(8,128)(2,1)S(1)} %get-tuple-element.71), channel_id=1, source_target_pairs={{0,8},{2,10},{4,12},{6,14},{8,0},{10,2},{12,4},{14,6},{16,24},{18,... | collective-permute-start | bytes 442376 | tf_op jit(solution)/shard_map/ppermute | solution.py:353
  26.1 7.8 %collective-permute-start.11 = (bf16[384,384]{1,0:T(8,128)(2,1)S(1)}, bf16[384,384]{1,0:T(8,128)(2,1)S(1)}, u32[]{:S(2)}, u32[]{:S(2)}) collective-permute-start(bf16[384,384]{1,0:T(8,128)(2,1)S(1)} %copy-done.13), channel_id=1, source_target_pairs={{0,2},{2,0},{4,6},{6,4},{8,10},{10,8},{12,14},{14,12},{16,18},{18,... | collective-permute-start | bytes 884744 | tf_op jit(solution)/shard_map/ppermute | solution.py:353
  28.3 7.2 %collective-permute-start.4 = (bf16[192,384]{1,0:T(8,128)(2,1)S(1)}, bf16[192,384]{1,0:T(8,128)(2,1)S(1)}, u32[]{:S(2)}, u32[]{:S(2)}) collective-permute-start(bf16[192,384]{1,0:T(8,128)(2,1)S(1)} %get-tuple-element.66), channel_id=1, source_target_pairs={{0,24},{2,26},{4,28},{6,30},{8,16},{10,18},{12,20},{14,22},{16,8},... | collective-permute-start | bytes 442376 | tf_op jit(solution)/shard_map/ppermute | solution.py:353
  30.6 5.0 %collective-permute-start.3 = (bf16[3,192,384]{2,1,0:T(8,128)(2,1)S(1)}, bf16[3,192,384]{2,1,0:T(8,128)(2,1)S(1)}, u32[]{:S(2)}, u32[]{:S(2)}) collective-permute-start(bf16[3,192,384]{2,1,0:T(8,128)(2,1)S(1)} %pad_maximum_fusion.1.refs_2_.refs_3_), channel_id=1, source_target_pairs={{0,1},{1,0},{2,3},{3,2},{4,5},{5,4},{6,7},{7,6},{8,9},{9,8},{10,11... | collective-permute-start | bytes 1327112 | tf_op jit(solution)/shard_map/ppermute | solution.py:298
  33.9 8.6 %collective-permute-start.12 = (bf16[384,384]{1,0:T(8,128)(2,1)S(1)}, bf16[384,384]{1,0:T(8,128)(2,1)S(1)}, u32[]{:S(2)}, u32[]{:S(2)}) collective-permute-start(bf16[384,384]{1,0:T(8,128)(2,1)S(1)} %broadcast_select_fusion.4.refs_13_), channel_id=1, source_target_pairs={{0,6},{2,4},{4,2},{6,0},{8,14},{10,12},{12,10},{14,8},{16,22},{18,... | collective-permute-start | bytes 884744 | tf_op jit(solution)/shard_map/ppermute | solution.py:353
  40.5 10.4 %collective-permute-start.5 = (bf16[192,384]{1,0:T(8,128)(2,1)S(1)}, bf16[192,384]{1,0:T(8,128)(2,1)S(1)}, u32[]{:S(2)}, u32[]{:S(2)}) collective-permute-start(bf16[192,384]{1,0:T(8,128)(2,1)S(1)} %get-tuple-element.36), channel_id=1, source_target_pairs={{0,32},{2,34},{4,36},{6,38},{8,40},{10,42},{12,44},{14,46},{16,48}... | collective-permute-start | bytes 442376 | tf_op jit(solution)/shard_map/ppermute | solution.py:353
  42.6 13.0 %collective-permute-start.13 = (bf16[384,384]{1,0:T(8,128)(2,1)S(1)}, bf16[384,384]{1,0:T(8,128)(2,1)S(1)}, u32[]{:S(2)}, u32[]{:S(2)}) collective-permute-start(bf16[384,384]{1,0:T(8,128)(2,1)S(1)} %broadcast_select_fusion.5.refs_15_), channel_id=1, source_target_pairs={{0,8},{2,10},{4,12},{6,14},{8,0},{10,2},{12,4},{14,6},{16,24},{18,... | collective-permute-start | bytes 884744 | tf_op jit(solution)/shard_map/ppermute | solution.py:353
  43.7 25.2 %all-to-all-start = ((bf16[16,5,16,384]{3,2,1,0:T(8,128)(2,1)}), bf16[16,5,16,384]{3,2,1,0:T(8,128)(2,1)}, u32[]{:S(2)}, u32[]{:S(2)}) async-start(bf16[16,5,16,384]{3,2,1,0:T(8,128)(2,1)} %get-tuple-element.35), calls=%async_computation | async-start | bytes 1966080 | tf_op jit(solution)/shard_map/all_to_all | solution.py:361
  51.0 8.7 %collective-permute-start.6 = (bf16[192,384]{1,0:T(8,128)(2,1)S(1)}, bf16[192,384]{1,0:T(8,128)(2,1)S(1)}, u32[]{:S(2)}, u32[]{:S(2)}) collective-permute-start(bf16[192,384]{1,0:T(8,128)(2,1)S(1)} %get-tuple-element.63), channel_id=1, source_target_pairs={{0,96},{2,98},{4,100},{6,102},{8,104},{10,106},{12,108},{14,110},{... | collective-permute-start | bytes 442376 | tf_op jit(solution)/shard_map/ppermute | solution.py:353
  55.6 12.0 %collective-permute-start.14 = (bf16[384,384]{1,0:T(8,128)(2,1)S(1)}, bf16[384,384]{1,0:T(8,128)(2,1)S(1)}, u32[]{:S(2)}, u32[]{:S(2)}) collective-permute-start(bf16[384,384]{1,0:T(8,128)(2,1)S(1)} %broadcast_select_fusion.6.refs_2_), channel_id=1, source_target_pairs={{0,24},{2,26},{4,28},{6,30},{8,16},{10,18},{12,20},{14,22},{16,8},... | collective-permute-start | bytes 884744 | tf_op jit(solution)/shard_map/ppermute | solution.py:353
  59.7 9.2 %collective-permute-start.7 = (bf16[192,384]{1,0:T(8,128)(2,1)S(1)}, bf16[192,384]{1,0:T(8,128)(2,1)S(1)}, u32[]{:S(2)}, u32[]{:S(2)}) collective-permute-start(bf16[192,384]{1,0:T(8,128)(2,1)S(1)} %get-tuple-element.38), channel_id=1, source_target_pairs={{0,224},{2,226},{4,228},{6,230},{8,232},{10,234},{12,236},{14,238}... | collective-permute-start | bytes 442376 | tf_op jit(solution)/shard_map/ppermute | solution.py:353
  67.7 7.4 %collective-permute-start.15 = (bf16[384,384]{1,0:T(8,128)(2,1)S(1)}, bf16[384,384]{1,0:T(8,128)(2,1)S(1)}, u32[]{:S(2)}, u32[]{:S(2)}) collective-permute-start(bf16[384,384]{1,0:T(8,128)(2,1)S(1)} %broadcast_select_fusion.3.refs_4_), channel_id=1, source_target_pairs={{0,32},{2,34},{4,36},{6,38},{8,40},{10,42},{12,44},{14,46},{16,48}... | collective-permute-start | bytes 884744 | tf_op jit(solution)/shard_map/ppermute | solution.py:353
  69.0 19.4 %collective-permute-start.8 = (bf16[4,192,384]{2,1,0:T(8,128)(2,1)S(1)}, bf16[4,192,384]{2,1,0:T(8,128)(2,1)S(1)}, u32[]{:S(2)}, u32[]{:S(2)}) collective-permute-start(bf16[4,192,384]{2,1,0:T(8,128)(2,1)S(1)} %pad_maximum_fusion.refs_2_.refs_1_), channel_id=1, source_target_pairs={{0,1},{1,0},{2,3},{3,2},{4,5},{5,4},{6,7},{7,6},{8,9},{9,8},{10,11... | collective-permute-start | bytes 1769480 | tf_op jit(solution)/shard_map/ppermute | solution.py:298
  75.1 8.7 %collective-permute-start.16 = (bf16[384,384]{1,0:T(8,128)(2,1)S(1)}, bf16[384,384]{1,0:T(8,128)(2,1)S(1)}, u32[]{:S(2)}, u32[]{:S(2)}) collective-permute-start(bf16[384,384]{1,0:T(8,128)(2,1)S(1)} %broadcast_select_fusion.2.refs_6_), channel_id=1, source_target_pairs={{0,96},{2,98},{4,100},{6,102},{8,104},{10,106},{12,108},{14,110},{... | collective-permute-start | bytes 884744 | tf_op jit(solution)/shard_map/ppermute | solution.py:353
  78.5 20.0 %collective-permute-start.9 = (bf16[3,256,384]{2,1,0:T(8,128)(2,1)S(1)}, bf16[3,256,384]{2,1,0:T(8,128)(2,1)S(1)}, u32[]{:S(2)}, u32[]{:S(2)}) collective-permute-start(bf16[3,256,384]{2,1,0:T(8,128)(2,1)S(1)} %copy-done.22), channel_id=1, source_target_pairs={{0,2},{2,0},{4,6},{6,4},{8,10},{10,8},{12,14},{14,12},{16,18},{18,... | collective-permute-start | bytes 1769480 | tf_op jit(solution)/shard_map/ppermute | solution.py:430
  83.8 19.5 %copy-start.8 = (bf16[384,384]{1,0:T(8,128)(2,1)}, bf16[384,384]{1,0:T(8,128)(2,1)S(1)}, u32[]{:S(2)}) copy-start(bf16[384,384]{1,0:T(8,128)(2,1)S(1)} %broadcast_select_fusion.1.refs_8_) | copy-start | bytes 884740
  83.8 19.5 %collective-permute-start.17 = (bf16[384,384]{1,0:T(8,128)(2,1)S(1)}, bf16[384,384]{1,0:T(8,128)(2,1)S(1)}, u32[]{:S(2)}, u32[]{:S(2)}) collective-permute-start(bf16[384,384]{1,0:T(8,128)(2,1)S(1)} %broadcast_select_fusion.1.refs_8_), channel_id=1, source_target_pairs={{0,224},{2,226},{4,228},{6,230},{8,232},{10,234},{12,236},{14,238}... | collective-permute-start | bytes 884744 | tf_op jit(solution)/shard_map/ppermute | solution.py:353
  92.4 17.1 %all-to-all-start.1 = ((bf16[8,4,16,384]{3,2,1,0:T(8,128)(2,1)}), bf16[8,4,16,384]{3,2,1,0:T(8,128)(2,1)S(1)}, u32[]{:S(2)}, u32[]{:S(2)}) async-start(bf16[8,4,16,384]{3,2,1,0:T(8,128)(2,1)} %get-tuple-element.39), calls=%async_computation.1 | async-start | bytes 786432 | tf_op jit(solution)/shard_map/all_to_all | solution.py:361
  98.7 9.3 %collective-permute-start.10 = (bf16[2,256,384]{2,1,0:T(8,128)(2,1)S(1)}, bf16[2,256,384]{2,1,0:T(8,128)(2,1)S(1)}, u32[]{:S(2)}, u32[]{:S(2)}) collective-permute-start(bf16[2,256,384]{2,1,0:T(8,128)(2,1)S(1)} %slice.63), channel_id=1, source_target_pairs={{0,6},{2,4},{4,2},{6,0},{8,14},{10,12},{12,10},{14,8},{16,22},{18,... | collective-permute-start | bytes 1179656 | tf_op jit(solution)/shard_map/ppermute | solution.py:430
  113.7 26.7 %all-to-all-start.2 = ((bf16[16,5,16,384]{3,2,1,0:T(8,128)(2,1)}), bf16[16,5,16,384]{3,2,1,0:T(8,128)(2,1)S(1)}, u32[]{:S(2)}, u32[]{:S(2)}) async-start(bf16[16,5,16,384]{3,2,1,0:T(8,128)(2,1)} %shard_map.109), calls=%async_computation.2 | async-start | bytes 1966080 | tf_op jit(solution)/shard_map/all_to_all | solution.py:361
  124.8 14.8 %collective-permute-start.18 = (bf16[1,256,384]{2,1,0:T(8,128)(2,1)S(1)}, bf16[1,256,384]{2,1,0:T(8,128)(2,1)S(1)}, u32[]{:S(2)}, u32[]{:S(2)}) collective-permute-start(bf16[1,256,384]{2,1,0:T(8,128)(2,1)S(1)} %slice.64), channel_id=1, source_target_pairs={{0,8},{2,10},{4,12},{6,14},{8,0},{10,2},{12,4},{14,6},{16,24},{18,... | collective-permute-start | bytes 589832 | tf_op jit(solution)/shard_map/ppermute | solution.py:430
  (25 other events, 248.9 us)
